TPU v7x, 32 devices: a whole 2x2x4 slice. The times are simulated.
32 devices in a mesh: groups: 2 (over y), wide: 4 (over z), lev: 2 (over x), fld: 2 (over core).
Axes of the slice: x: 2, y: 2, z: 4, core: 2. Of those that a mesh axis runs over, the one named last changes fastest.
Arguments:
- grid_state: bfloat16 [4, 3, 8, 512, 1024], P(('groups', 'fld'), None, 'lev', 'wide'), parts along dimension 0, may hold values from -6 to 6
- wave_slots: int32 [512], replicated, may hold values from 0 to 511, each once
- lat_basis: bfloat16 [512, 512, 512], P(('wide', 'lev')), may hold values from -0.25 to 0.25
- vert_modes: float32 [8, 8], replicated, may hold values from -1 to 1, as said below
- vert_rates: float32 [3, 8], replicated, may hold values from 0.05 to 20
- band_sizes: int32 [16], replicated, may hold values from 1 to 64, 512 in all
- norm_gain: float32 [24], replicated, may hold values from 0.25 to 1.75
- w_in: bfloat16 [512, 24], replicated, may hold values from -1.25 to 1.25
- band_bias: float32 [512, 16], replicated, may hold values from -6 to 6
- w_mid: bfloat16 [512, 512], replicated, may hold values from -0.25 to 0.25
- w_out: bfloat16 [24, 512], replicated, may hold values from -0.25 to 0.25
Outputs:
- spectral: float32 [512, 4, 3, 8, 2, 512], P(('wide', 'lev'), ('groups', 'fld')), parts along dimension 1
- new_state: bfloat16 [4, 3, 8, 512, 1024], P(('groups', 'fld'), None, None, ('wide', 'lev')), parts along dimension 0
There are 2 independent parts, one for each index of `groups`. A program takes and returns all parts, laid end to end along the dimension named above; an argument that names none is the same for every part. Nothing has to cross between parts.
Inputs may be any that keep to these rules, and one draw needn't show every extreme that they name: `wave_slots`: each number of 0 to 511 stands in exactly one slot. `band_sizes`: the 16 sizes sum to 512. `vert_modes`: an orthonormal matrix.
All inputs are finite; a program needn't handle non-finite values.
Results may differ from a plain program's by a relative error of at most 0.011.
Values may be sent and summed in bfloat16 or wider, within the bound.
No kernel may reach another device: no remote copies, remote signals or barrier semaphores. Data moves between devices by JAX's collectives and lax.ppermute only.
A program may use at most 192 MiB of HBM per device.

v0:
```python
import math

import jax
import jax.numpy as jnp
from jax import lax
from jax.sharding import PartitionSpec as P

transport_speed = 0.5
norm_eps = 1e-06


def extended(array, sides, width):
    for axis, dim in sides:
        size, length = (lax.axis_size(axis), array.shape[dim])
        up = [(i, (i + 1) % size) for i in range(size - 1)]
        down = [(j, i) for i, j in up]
        last = lax.slice_in_dim(array, length - width, length, axis=dim)
        initial = lax.slice_in_dim(array, 0, width, axis=dim)
        before = lax.ppermute(last, axis, up)
        after = lax.ppermute(initial, axis, down)
        array = jnp.concatenate([before, array, after], axis=dim)
    return array


def fourier_tables(wave_slots, lon_count):
    wave_count = wave_slots.shape[0]
    longitude = jnp.arange(lon_count, dtype=jnp.int32)
    integer_phase = longitude[:, None] * wave_slots[None, :] % lon_count
    phase_angle = integer_phase.astype(jnp.float32) * (2.0 * math.pi / lon_count)
    table_scale = 1.0 / math.sqrt(lon_count)
    cosine = jnp.cos(phase_angle) * table_scale
    sine_part = jnp.sin(phase_angle) * table_scale
    forward = (
        jnp.stack([cosine, -sine_part], axis=1)
        .reshape(lon_count, 2 * wave_count)
        .astype(jnp.bfloat16)
    )
    weight = jnp.where(wave_slots == 0, 1.0, 2.0).astype(jnp.float32)
    inverse = jnp.stack(
        [cosine.T * weight[:, None], -sine_part.T * weight[:, None]], axis=0
    ).astype(jnp.bfloat16)
    return (forward, inverse)


def advection_term(padded, main_band_entries):
    above_main_entries = padded[:, :, :, 2:, :].astype(jnp.float32)
    below_main_entries = padded[:, :, :, :-2, :].astype(jnp.float32)
    oscillation_factor = jnp.roll(main_band_entries, -1, axis=1).astype(jnp.float32)
    return (
        main_band_entries.astype(jnp.float32)
        + transport_speed * oscillation_factor * (above_main_entries - below_main_entries)
    ).astype(jnp.bfloat16)


def couple(spectra, wave_part, vert_modes, vert_rates):
    wave_count = spectra.shape[-1]
    degree = wave_part[:, None] + jnp.arange(wave_count, dtype=jnp.int32)[None, :]
    spectra = jnp.where((degree < wave_count)[:, None, None, None, None, :], spectra, 0.0)
    curvature = (degree * (degree + 1)).astype(jnp.float32) / float(wave_count * wave_count)
    vorticity = spectra[:, :, 0] / (
        1.0 + curvature[:, None, None, None, :] * vert_rates[0][None, None, :, None, None]
    )
    coupled_part = spectra[:, :, 1:]
    modal = jnp.einsum(
        "sbflrk,li->sbfirk", coupled_part, vert_modes, precision=lax.Precision.HIGHEST
    )
    scaled = modal / (
        1.0 + curvature[:, None, None, None, None, :] * vert_rates[1:][None, None, :, :, None, None]
    )
    restored = jnp.einsum("sbfirk,li->sbflrk", scaled, vert_modes, precision=lax.Precision.HIGHEST)
    return jnp.concatenate([vorticity[:, :, None], restored], axis=2)


def column_net(grid_cols, lat_first, band_sizes, norm_gain, w_in, band_bias, w_mid, w_out):
    members, fields, levels, lat_rows, lon_cells = grid_cols.shape
    unit_count = w_in.shape[0]
    values = grid_cols.reshape(members, fields * levels, lat_rows * lon_cells).astype(jnp.float32)
    average_squared = jnp.mean(values * values, axis=1, keepdims=True)
    rescaled_values = (
        values * lax.rsqrt(average_squared + norm_eps) * norm_gain[None, :, None]
    ).astype(jnp.bfloat16)
    band_ends = jnp.cumsum(band_sizes)
    band_starts = band_ends - band_sizes
    latitude = lat_first + jnp.arange(lat_rows, dtype=jnp.int32)
    inside = (
        (latitude[None, :] >= band_starts[:, None]) & (latitude[None, :] < band_ends[:, None])
    ).astype(jnp.float32)
    lat_bias = jnp.dot(band_bias, inside, precision=lax.Precision.HIGHEST)
    cell_bias = jnp.broadcast_to(lat_bias[:, :, None], (unit_count, lat_rows, lon_cells)).reshape(
        unit_count, lat_rows * lon_cells
    )
    first_layer = jnp.einsum(
        "hf,bfc->bhc", w_in, rescaled_values, preferred_element_type=jnp.float32
    )
    first_layer = jax.nn.silu(first_layer + cell_bias[None]).astype(jnp.bfloat16)
    second = jnp.einsum("hg,bgc->bhc", w_mid, first_layer, preferred_element_type=jnp.float32)
    second = jax.nn.silu(second).astype(jnp.bfloat16)
    increment = jnp.einsum("fh,bhc->bfc", w_out, second, preferred_element_type=jnp.float32)
    return (values + increment).astype(jnp.bfloat16).reshape(grid_cols.shape)


def local(
    grid_state,
    wave_slots,
    lat_basis,
    vert_modes,
    vert_rates,
    band_sizes,
    norm_gain,
    w_in,
    band_bias,
    w_mid,
    w_out,
):
    members, fields, lev_dev, lat_dev, lon_count = grid_state.shape
    wide_count = lax.axis_size("wide")
    lev_count = lax.axis_size("lev")
    slot_dev, wave_count, lat_count = lat_basis.shape
    levels = lev_dev * lev_count
    padded = extended(grid_state, (("wide", 3),), 1)
    advected = advection_term(padded, grid_state)
    forward, inverse = fourier_tables(wave_slots, lon_count)
    coeffs = jnp.dot(
        advected.reshape(-1, lon_count), forward, preferred_element_type=jnp.float32
    ).astype(jnp.bfloat16)
    coeffs = coeffs.reshape(members, fields, lev_dev, lat_dev, 2, wide_count, lev_count, slot_dev)
    by_wave = lax.all_to_all(
        lax.all_to_all(coeffs, "wide", split_axis=5, concat_axis=3, tiled=True),
        "lev",
        split_axis=6,
        concat_axis=2,
        tiled=True,
    )
    by_wave = by_wave.reshape(members, fields, levels, lat_count, 2, slot_dev)
    block_index = lax.axis_index("wide") * lev_count + lax.axis_index("lev")
    first_slot = block_index * slot_dev
    wave_part = lax.dynamic_slice_in_dim(wave_slots, first_slot, slot_dev)
    raw_spectra = jnp.einsum(
        "skj,bfljrs->sbflrk", lat_basis, by_wave, preferred_element_type=jnp.float32
    )
    spectral = couple(raw_spectra, wave_part, vert_modes, vert_rates)
    rounded = spectral.astype(jnp.bfloat16)
    back_coeffs = jnp.einsum(
        "skj,sbflrk->sbflrj", lat_basis, rounded, preferred_element_type=jnp.float32
    ).astype(jnp.bfloat16)
    lat_quarter = lat_count // (wide_count * lev_count)
    parcel = back_coeffs.reshape(
        1, 1, slot_dev, members, fields, levels, 2, wide_count, lev_count, lat_quarter
    )
    arrived = lax.all_to_all(
        lax.all_to_all(parcel, "wide", split_axis=7, concat_axis=0, tiled=True),
        "lev",
        split_axis=8,
        concat_axis=1,
        tiled=True,
    )
    arrived = arrived.reshape(wave_count, members, fields, levels, 2, lat_quarter)
    grid_mid = jnp.einsum(
        "pbflrj,rpi->bflji", arrived, inverse, preferred_element_type=jnp.float32
    ).astype(jnp.bfloat16)
    new_state = column_net(
        grid_mid, block_index * lat_quarter, band_sizes, norm_gain, w_in, band_bias, w_mid, w_out
    )
    return (spectral, new_state)


def solution(mesh):
    placed = (
        P(("groups", "fld"), None, "lev", "wide", None),
        P(),
        P(("wide", "lev"), None, None),
        P(),
        P(),
        P(),
        P(),
        P(),
        P(),
        P(),
        P(),
    )
    return jax.shard_map(
        local,
        mesh=mesh,
        in_specs=placed,
        out_specs=(
            P(("wide", "lev"), ("groups", "fld"), None, None, None, None),
            P(("groups", "fld"), None, None, ("wide", "lev"), None),
        ),
        check_vma=False,
    )
```

profile of v0, /device:TPU:0, one launch (start us, length us, event | category | flops | bytes accessed | tf_op | source)
XLA Modules:
  0.0 631.0 jit_solution(15577777845793812023)
XLA Ops:
  0.6 1.2 fusion.61
  1.8 1.3 collective-permute-start
  3.1 5.6 collective-permute-start.1
  8.7 9.9 %multiply_convert_fusion.5 = (bf16[1024,1,512]{0,2,1:T(8,128)(2,1)S(1)}, bf16[1024,1,512]{0,2,1:T(8,128)(2,1)S(1)}) fusion(s32[512]{0:T(512)} %param.12), kind=kLoop, calls=%fused_computation.64 | loop fusion | flops 9961472 | bytes 2099200 | tf_op jit(solution)/shard_map/convert.8
  18.8 2.2 copy-done.5
  21.0 0.4 slice-done
  21.7 2.9 add_convert_fusion
  24.5 4.9 convolution_convert_fusion
  29.5 12.3 %reshape.543 = bf16[1,3,4,128,2,4,2,64]{7,6,5,4,3,2,1,0:T(2,128)(2,1)} reshape(bf16[1536,1024]{1,0:T(8,128)(2,1)} %convolution_convert_fusion) | data formatting | bytes 6291456 | tf_op jit(solution)/shard_map/reshape | solution.py:126
  41.8 16.2 %copy.72 = bf16[1,3,4,128,2,4,2,64]{3,2,1,7,6,4,0,5:T(4,128)(2,1)} copy(bf16[1,3,4,128,2,4,2,64]{7,6,5,4,3,2,1,0:T(2,128)(2,1)} %reshape.543) | data formatting | bytes 6291456 | tf_op jit(solution)/shard_map/reshape | solution.py:126
  58.0 74.5 %all_to_all.66 = bf16[1,3,4,128,2,4,2,64]{3,2,1,7,6,4,0,5:T(4,128)(2,1)S(1)} all-to-all(bf16[1,3,4,128,2,4,2,64]{3,2,1,7,6,4,0,5:T(4,128)(2,1)} %copy.72), channel_id=1, replica_groups=mesh['groups'=2,'wide'=4,'lev'=2,'fld'=2] {'wide'}, dimensions={5} | all-to-all | bytes 6291456 | tf_op jit(solution)/shard_map/all_to_all | solution.py:128
  132.5 4.1 copy.91
  136.6 5.7 reshape.544
  142.3 17.3 %all-to-all-start.1 = ((bf16[1,3,4,512,2,1,2,64]{3,7,4,2,1,5,0,6:T(8,128)(2,1)}), bf16[1,3,4,512,2,1,2,64]{3,7,4,2,1,5,0,6:T(8,128)(2,1)}, u32[]{:S(2)}, u32[]{:S(2)}) async-start(bf16[1,3,4,512,2,1,2,64]{3,7,4,2,1,5,0,6:T(8,128)(2,1)} %reshape.544), calls=%async_computation.1 | async-start | bytes 6291456 | tf_op jit(solution)/shard_map/all_to_all | solution.py:127
  160.1 1.7 multiply_add_fusion
  161.8 32.7 %all-to-all-done.1 = bf16[1,3,4,512,2,1,2,64]{3,7,4,2,1,5,0,6:T(8,128)(2,1)} async-done(((bf16[1,3,4,512,2,1,2,64]{3,7,4,2,1,5,0,6:T(8,128)(2,1)}), bf16[1,3,4,512,2,1,2,64]{3,7,4,2,1,5,0,6:T(8,128)(2,1)}, u32[]{:S(2)}, u32[]{:S(2)}) %all-to-all-start.1) | async-done | bytes 3145760 | tf_op jit(solution)/shard_map/all_to_all | solution.py:127
  194.5 6.0 copy.75
  200.5 5.5 reshape.526
  206.0 18.7 %select_bitcast_fusion = f32[64,1,3,8,2,512]{5,3,4,2,0,1:T(8,128)} fusion(pred[64,512]{1,0:T(8,128)(4,1)S(1)} %fusion.49, bf16[3,8,512,2,64]{2,1,3,0,4:T(8,128)(2,1)} %reshape.526, bf16[64,512,512]{2,1,0:T(8,128)(2,1)} %param.13), kind=kOutput, calls=%fused_computation.21 | convolution fusion | flops 1612185600 | bytes 43024384 | tf_op jit(solution)/shard_map/skj,bfljrs->sbflrk/dot_general | solution.py:138
  224.7 3.9 convert_bitcast_fusion.1
  228.6 4.2 fusion.12
  232.8 4.4 fusion.29
  237.6 1.7 copy-done.4
  239.3 18.3 %fusion.22 = bf16[64,3,8,2,512]{4,2,3,1,0:T(8,128)(2,1)} fusion(bf16[64,512,512]{2,1,0:T(8,128)(2,1)} %param.13, bf16[64,2,8,2,512]{4,2,3,1,0:T(8,128)(2,1)S(1)} %convert_bitcast_fusion, bf16[64,1,8,2,512]{4,2,3,1,0:T(8,128)(2,1)} %get-tuple-element.14), kind=kOutput, calls=%fused_computation.43 | convolution fusion | flops 1613758464 | bytes 39845888 | tf_op jit(solution)/shard_map/skj,sbflrk->sbflrj/dot_general | solution.py:143
  257.6 12.4 %reshape.529 = bf16[1,1,64,1,3,8,2,4,2,64]{9,8,7,5,6,4,2,3,1,0:T(2,128)(2,1)} reshape(bf16[64,3,8,2,512]{4,2,3,1,0:T(8,128)(2,1)} %fusion.22) | data formatting | bytes 6291456 | tf_op jit(solution)/shard_map/reshape | solution.py:147
  270.1 6.8 %copy.99 = bf16[1,1,64,1,3,8,2,4,2,64]{9,8,5,6,4,2,3,1,0,7:T(2,128)(2,1)} copy(bf16[1,1,64,1,3,8,2,4,2,64]{9,8,7,5,6,4,2,3,1,0:T(2,128)(2,1)} %reshape.529) | data formatting | bytes 6291456 | tf_op jit(solution)/shard_map/reshape | solution.py:147
  276.9 7.7 %reshape.546 = bf16[4,2,196608]{2,1,0:T(2,128)(2,1)} reshape(bf16[4,1,1,1,64,3,2,8,2,64]{9,8,7,6,5,4,3,2,1,0:T(2,128)(2,1)} %bitcast.187) | data formatting | bytes 6291456
  284.6 74.1 %all_to_all.67 = bf16[4,2,196608]{2,1,0:T(2,128)(2,1)} all-to-all(bf16[4,2,196608]{2,1,0:T(2,128)(2,1)} %reshape.546), channel_id=1, replica_groups=mesh['groups'=2,'wide'=4,'lev'=2,'fld'=2] {'wide'}, dimensions={0} | all-to-all | bytes 6291456 | tf_op jit(solution)/shard_map/all_to_all | solution.py:151
  358.8 7.5 %reshape.547 = bf16[4,1,1,1,64,3,2,8,2,64]{9,8,7,6,5,4,3,2,1,0:T(2,128)(2,1)} reshape(bf16[4,2,196608]{2,1,0:T(2,128)(2,1)} %all_to_all.67) | data formatting | bytes 6291456
  366.3 6.8 %bitcast_bitcast_fusion.1 = bf16[4,1,64,1,3,8,2,1,2,64]{9,8,5,6,4,2,0,7,3,1:T(2,128)(2,1)} fusion(bf16[4,1,1,1,64,3,2,8,2,64]{9,8,7,6,5,4,3,2,1,0:T(2,128)(2,1)} %reshape.547), kind=kLoop, calls=%fused_computation.95 | loop fusion | bytes 6291456 | tf_op jit(solution)/shard_map/all_to_all | solution.py:151
  373.1 10.4 %copy.98 = bf16[4,1,64,1,3,8,2,1,2,64]{9,0,5,6,4,2,7,3,1,8:T(4,128)(2,1)} copy(bf16[4,1,64,1,3,8,2,1,2,64]{9,8,5,6,4,2,0,7,3,1:T(2,128)(2,1)} %bitcast_bitcast_fusion.1) | data formatting | bytes 6291456 | tf_op jit(solution)/shard_map/all_to_all | solution.py:151
  383.4 7.9 %reshape.548 = bf16[2,2,393216]{2,1,0:T(2,128)(2,1)} reshape(bf16[2,1,1,1,64,3,2,8,4,64]{9,8,7,6,5,4,3,2,1,0:T(4,128)(2,1)} %bitcast.188) | data formatting | bytes 6291456
  391.4 5.3 all-to-all-start.3
  397.3 10.9 %multiply_convert_fusion.4 = (bf16[1,512,1024]{2,1,0:T(8,128)(2,1)}, bf16[1,512,1024]{2,1,0:T(8,128)(2,1)}) fusion(f32[512]{0:T(512)S(1)} %get-tuple-element.20, s32[512]{0:T(512)S(1)} %copy-done.12, f32[512]{0:T(512)S(1)} %get-tuple-element.21), kind=kLoop, calls=%fused_computation.57 | loop fusion | flops 10485760 | bytes 2103296 | tf_op jit(solution)/shard_map/convert.2
  408.2 6.1 pad_maximum_fusion
  414.3 11.7 %copy.82 = f32[64,1,3,8,2,512]{5,4,3,2,1,0:T(2,128)} copy(f32[64,1,3,8,2,512]{5,3,4,2,0,1:T(8,128)} %pad_maximum_fusion) | data formatting | bytes 12582912
  426.0 5.6 all-to-all-done.3
  431.7 7.9 %reshape.549 = bf16[2,1,1,1,64,3,2,8,4,64]{9,8,7,6,5,4,3,2,1,0:T(4,128)(2,1)} reshape(bf16[2,2,393216]{2,1,0:T(2,128)(2,1)} %all-to-all-done.3) | data formatting | bytes 6291456
  439.6 8.7 %bitcast_bitcast_fusion = bf16[4,2,1,64,1,3,8,2,1,1,64]{10,0,6,7,5,3,1,9,8,4,2:T(4,128)(2,1)} fusion(bf16[2,1,1,1,64,3,2,8,4,64]{9,8,7,6,5,4,3,2,1,0:T(4,128)(2,1)} %reshape.549), kind=kLoop, calls=%fused_computation.94 | loop fusion | bytes 6291456 | tf_op jit(solution)/shard_map/all_to_all | solution.py:150
  448.3 17.6 %copy.80 = bf16[4,2,1,64,1,3,8,2,1,1,64]{3,1,0,10,7,6,5,9,8,4,2:T(2,128)(2,1)} copy(bf16[4,2,1,64,1,3,8,2,1,1,64]{10,0,6,7,5,3,1,9,8,4,2:T(4,128)(2,1)} %bitcast_bitcast_fusion) | data formatting | bytes 6291456 | tf_op jit(solution)/shard_map/all_to_all | solution.py:150
  465.9 14.8 %reshape.530 = bf16[512,3,8,2,64]{0,4,3,2,1:T(8,128)(2,1)} reshape(bf16[4,2,1,64,1,3,8,2,1,1,64]{3,1,0,10,7,6,5,9,8,4,2:T(2,128)(2,1)} %copy.80) | data formatting | bytes 6291456 | tf_op jit(solution)/shard_map/reshape.29
  480.8 5.4 multiply_reduce_fusion
  486.1 2.6 copy-done.3
  488.8 6.3 copy.94
  495.1 6.9 %reshape.536 = f32[1,24,65536]{2,1,0:T(8,128)} reshape(f32[3,8,64,1024]{3,2,1,0:T(8,128)} %copy-done.3) | data formatting | bytes 12582912 | tf_op jit(solution)/shard_map/convert_element_type | solution.py:77
  502.1 43.5 %fusion.4 = bf16[512,65536]{0,1:T(8,128)(2,1)} fusion(bf16[512,24]{0,1:T(8,128)(2,1)S(1)} %copy-done.11, f32[512,64]{0,1:T(8,128)S(1)} %convolution_bitcast_fusion.1, f32[24,65536]{1,0:T(8,128)} %bitcast.186, f32[24]{0:T(128)S(1)} %copy-done.14, f32[65536]{0:T(1024)S(1)} %bitcast.193), kind=kOutput, calls=%fused_computation.8 | convolution fusion | flops 1816657920 | bytes 73818208 | tf_op jit(solution)/shard_map/hf,bfc->bhc/dot_general | solution.py:92
  545.6 79.9 %fusion.7 = bf16[1,24,65536]{2,1,0:T(8,128)(2,1)} fusion(f32[1,24,65536]{2,1,0:T(8,128)} %reshape.536, bf16[24,512]{1,0:T(8,128)(2,1)S(1)} %copy-done.17, bf16[512,65536]{0,1:T(8,128)(2,1)} %fusion.4, bf16[512,512]{1,0:T(8,128)(2,1)S(1)} %copy-done), kind=kOutput, calls=%fused_computation.12 | convolution fusion | flops 36141268992 | bytes 77094912 | tf_op jit(solution)/shard_map/fh,bhc->bfc/dot_general | solution.py:98
  625.4 5.3 copy.83
  (55 shorter events, 2.0 us)
Async XLA Ops:
  0.6 544.9 %copy-start = (bf16[512,512]{1,0:T(8,128)(2,1)S(1)}, bf16[512,512]{1,0:T(8,128)(2,1)}, u32[]{:S(2)}) copy-start(bf16[512,512]{1,0:T(8,128)(2,1)} %param.20) | copy-start | bytes 1572868
  1.8 17.0 %collective-permute-start = (bf16[1,3,4,1,1024]{4,3,2,1,0:T(2,128)(2,1)S(1)}, bf16[1,3,4,1,1024]{4,3,2,1,0:T(2,128)(2,1)S(1)}, u32[]{:S(2)}, u32[]{:S(2)}) collective-permute-start(bf16[1,3,4,1,1024]{4,3,2,1,0:T(2,128)(2,1)S(1)} %get-tuple-element.16), channel_id=1, source_target_pairs={{4,0},{8,4},{12,8},{5,1},{9,5},{13,9},{6,2},{10,6},{14,10},{7,3},{... | collective-permute-start | bytes 73736 | tf_op jit(solution)/shard_map/ppermute | solution.py:20
  3.1 15.7 %collective-permute-start.1 = (bf16[1,3,4,1,1024]{4,3,2,1,0:T(2,128)(2,1)S(1)}, bf16[1,3,4,1,1024]{4,3,2,1,0:T(2,128)(2,1)S(1)}, u32[]{:S(2)}, u32[]{:S(2)}) collective-permute-start(bf16[1,3,4,1,1024]{4,3,2,1,0:T(2,128)(2,1)S(1)} %get-tuple-element.17), channel_id=1, source_target_pairs={{0,4},{4,8},{8,12},{1,5},{5,9},{9,13},{2,6},{6,10},{10,14},{3,7},{... | collective-permute-start | bytes 73736 | tf_op jit(solution)/shard_map/ppermute | solution.py:19
  18.8 2.3 copy-start.5
  18.8 2.6 slice-start
  18.8 2.9 slice-start.1
  142.3 17.3 %copy-start.12 = (s32[512]{0:T(512)S(1)}, s32[512]{0:T(512)}, u32[]{:S(2)}) copy-start(s32[512]{0:T(512)} %param.12) | copy-start | bytes 6148
  142.3 17.4 %copy-start.16 = (f32[3,8]{1,0:T(4,128)S(1)}, f32[3,8]{1,0:T(4,128)}, u32[]{:S(2)}) copy-start(f32[3,8]{1,0:T(4,128)} %param.15) | copy-start | bytes 292
  142.3 52.2 %all-to-all-start.1 = ((bf16[1,3,4,512,2,1,2,64]{3,7,4,2,1,5,0,6:T(8,128)(2,1)}), bf16[1,3,4,512,2,1,2,64]{3,7,4,2,1,5,0,6:T(8,128)(2,1)}, u32[]{:S(2)}, u32[]{:S(2)}) async-start(bf16[1,3,4,512,2,1,2,64]{3,7,4,2,1,5,0,6:T(8,128)(2,1)} %reshape.544), calls=%async_computation.1 | async-start | bytes 6291456 | tf_op jit(solution)/shard_map/all_to_all | solution.py:127
  206.0 22.6 %copy-start.13 = (f32[8,8]{1,0:T(8,128)S(1)}, f32[8,8]{1,0:T(8,128)}, u32[]{:S(2)}) copy-start(f32[8,8]{1,0:T(8,128)} %param.14) | copy-start | bytes 772
  224.7 3.9 copy-start.2
  228.6 4.2 copy-start.7
  237.3 2.1 copy-start.4
  391.3 5.3 copy-start.15
  391.3 5.6 copy-start.10
  391.3 16.9 %copy-start.6 = (f32[64,1,1,8,2,512]{5,3,4,2,0,1:T(8,128)S(1)}, f32[64,1,1,8,2,512]{5,3,4,2,0,1:T(8,128)}, u32[]{:S(2)}) copy-start(f32[64,1,1,8,2,512]{5,3,4,2,0,1:T(8,128)} %get-tuple-element.15) | copy-start | bytes 6291460
  391.4 40.3 %all-to-all-start.3 = ((bf16[2,2,393216]{2,1,0:T(2,128)(2,1)}), bf16[2,2,393216]{2,1,0:T(2,128)(2,1)}, u32[]{:S(2)}, u32[]{:S(2)}) async-start(bf16[2,2,393216]{2,1,0:T(2,128)(2,1)} %reshape.548), calls=%async_computation.3 | async-start | bytes 6291456 | tf_op jit(solution)/shard_map/all_to_all | solution.py:150
  465.9 14.8 %copy-start.8 = (bf16[1,512,1024]{2,1,0:T(8,128)(2,1)S(1)}, bf16[1,512,1024]{2,1,0:T(8,128)(2,1)}, u32[]{:S(2)}) copy-start(bf16[1,512,1024]{2,1,0:T(8,128)(2,1)} %get-tuple-element.18) | copy-start | bytes 3145732
  465.9 14.8 %copy-start.9 = (bf16[1,512,1024]{2,1,0:T(8,128)(2,1)S(1)}, bf16[1,512,1024]{2,1,0:T(8,128)(2,1)}, u32[]{:S(2)}) copy-start(bf16[1,512,1024]{2,1,0:T(8,128)(2,1)} %get-tuple-element.19) | copy-start | bytes 3145732
  486.1 2.7 copy-start.3
  495.1 7.0 %copy-start.11 = (bf16[512,24]{0,1:T(8,128)(2,1)S(1)}, bf16[512,24]{0,1:T(8,128)(2,1)}, u32[]{:S(2)}) copy-start(bf16[512,24]{0,1:T(8,128)(2,1)} %param.18) | copy-start | bytes 73732
  495.1 7.0 %copy-start.14 = (f32[24]{0:T(128)S(1)}, f32[24]{0:T(128)}, u32[]{:S(2)}) copy-start(f32[24]{0:T(128)} %param.17) | copy-start | bytes 292
  502.1 43.5 %copy-start.17 = (bf16[24,512]{1,0:T(8,128)(2,1)S(1)}, bf16[24,512]{1,0:T(8,128)(2,1)}, u32[]{:S(2)}) copy-start(bf16[24,512]{1,0:T(8,128)(2,1)} %param.21) | copy-start | bytes 73732
  625.4 5.3 copy-start.1
where the time goes:
time: 635 us; the launch traced here: 631 us
  local copies, waits for them, and re-layouts  197 us (31%)
  matrix products  180 us (28%)
  blocking collectives  149 us (23%)
  waiting for transfers between devices  38.4 us (6%)
  other arithmetic  36.5 us (6%)
  starting transfers between devices  29.4 us (5%)
    dot_general x1, matrix products, column_net(): jnp.einsum('fh,bhc->bfc', w_out, second, preferred_element_type=jnp.float32)  79.9 us
    all_to_all x1, blocking collectives, local(): lax.all_to_all(coeffs, 'wide', split_axis=5, concat_axis=3, tiled=True)  74.5 us
    all_to_all x1, blocking collectives, local(): lax.all_to_all(parcel, 'wide', split_axis=7, concat_axis=0, tiled=True)  74.1 us
    unnamed x44, local copies, waits for them, and re-layouts  61.1 us
    dot_general x1, matrix products, column_net(): jnp.einsum('hf,bfc->bhc', w_in, rescaled_values, preferred_element_type=j...  43.5 us
    all_to_all x1, waiting for transfers between devices, local(): lax.all_to_all(lax.all_to_all(coeffs, 'wide', split_axis=5, concat_axis=3...  32.7 us
    reshape x2, local copies, waits for them, and re-layouts, local(): coeffs.reshape(members, fields, lev_dev, lat_dev, 2, wide_count, lev_coun...  28.5 us
    all_to_all x2, local copies, waits for them, and re-layouts, local(): lax.all_to_all(lax.all_to_all(parcel, 'wide', split_axis=7, concat_axis=0...  26.3 us
  transfers between devices with their start and end apart: 4, of which 2 were waited for; matrix products, arithmetic and copies ran while one was open for 7% of the time, Pallas kernels for 0%

commit v1 on v0

--- a/solution.py
+++ b/solution.py
@@ -1,8 +1,11 @@
+import functools
 import math
 
 import jax
 import jax.numpy as jnp
 from jax import lax
+from jax.experimental import pallas as pl
+from jax.experimental.pallas import tpu as pltpu
 from jax.sharding import PartitionSpec as P
 
 transport_speed = 0.5
@@ -99,7 +102,7 @@
     return (values + increment).astype(jnp.bfloat16).reshape(grid_cols.shape)
 
 
-def local(
+def local_plain(
     grid_state,
     wave_slots,
     lat_basis,
@@ -164,6 +167,444 @@
     return (spectral, new_state)
 
 
+LANES = 128
+PACK = 16
+VMEM_BYTES = 58 * 2**20
+
+
+def angle_parts(slot_waves, lon_count):
+    coarse = jnp.arange(lon_count // LANES, dtype=jnp.int32) * LANES
+    fine = jnp.arange(LANES, dtype=jnp.int32)
+
+    def angles(longitude):
+        phase = slot_waves[:, None] * longitude[None, :] % lon_count
+        return phase.astype(jnp.float32) * (2.0 * math.pi / lon_count)
+
+    a, b = angles(coarse), angles(fine)
+    scale = 1.0 / math.sqrt(lon_count)
+    return jnp.cos(a), jnp.sin(a), jnp.cos(b) * scale, jnp.sin(b) * scale
+
+
+def table_kernel(devices, ca_ref, sa_ref, cb_ref, sb_ref, out_ref):
+    slots, tiles = ca_ref.shape
+    per = slots // devices
+    cb, sb = cb_ref[...], sb_ref[...]
+    for t in range(tiles):
+        ca, sa = ca_ref[:, t : t + 1], sa_ref[:, t : t + 1]
+        cosine = (ca * cb - sa * sb).astype(jnp.bfloat16)
+        minus_sine = (-(sa * cb + ca * sb)).astype(jnp.bfloat16)
+        cols = slice(t * LANES, (t + 1) * LANES)
+        for d in range(devices):
+            rows = slice(d * per, (d + 1) * per)
+            out_ref[d, 0, :, cols] = cosine[rows]
+            out_ref[d, 1, :, cols] = minus_sine[rows]
+
+
+def fourier_kernel(x_ref, next_ref, before_ref, after_ref, table_ref, out_ref):
+    _, levels, rows, _ = x_ref.shape
+    parts = []
+    row = lax.broadcasted_iota(jnp.int32, (rows, 1), 0)
+    for l in range(levels):
+        x = x_ref[0, l].astype(jnp.float32)
+        up = jnp.where(row == rows - 1, after_ref[0, l].astype(jnp.float32), pltpu.roll(x, rows - 1, 0))
+        down = jnp.where(row == 0, before_ref[0, l].astype(jnp.float32), pltpu.roll(x, 1, 0))
+        mixed = x + transport_speed * next_ref[0, l].astype(jnp.float32) * (up - down)
+        parts.append(mixed.astype(jnp.bfloat16))
+    advected = jnp.concatenate(parts, axis=0)
+    out_ref[...] = lax.dot_general(
+        table_ref[...], advected, (((1,), (1,)), ((), ())), preferred_element_type=jnp.float32
+    ).astype(jnp.bfloat16)
+
+
+def fourier(grid_state, before, after, table):
+    _, fields, lev_dev, lat_dev, lon_count = grid_state.shape
+    x, before, after = grid_state[0], before[0], after[0]
+    pair = 2 if lev_dev % 2 == 0 else 1
+    rows = table.shape[0]
+    halves = lev_dev // pair
+    return pl.pallas_call(
+        fourier_kernel,
+        grid=(fields, halves),
+        in_specs=[
+            pl.BlockSpec((1, pair, lat_dev, lon_count), lambda f, h: (f, h, 0, 0)),
+            pl.BlockSpec((1, pair, lat_dev, lon_count), lambda f, h: (lax.rem(f + 1, fields), h, 0, 0)),
+            pl.BlockSpec((1, pair, 1, lon_count), lambda f, h: (f, h, 0, 0)),
+            pl.BlockSpec((1, pair, 1, lon_count), lambda f, h: (f, h, 0, 0)),
+            pl.BlockSpec((rows, lon_count), lambda f, h: (0, 0)),
+        ],
+        out_specs=pl.BlockSpec((rows, pair * lat_dev), lambda f, h: (0, f * halves + h)),
+        out_shape=jax.ShapeDtypeStruct((rows, fields * lev_dev * lat_dev), jnp.bfloat16),
+        compiler_params=pltpu.CompilerParams(vmem_limit_bytes=VMEM_BYTES),
+        cost_estimate=pl.CostEstimate(
+            flops=2 * rows * lon_count * fields * lev_dev * lat_dev,
+            bytes_accessed=4 * rows * fields * lev_dev * lat_dev,
+            transcendentals=0,
+        ),
+    )(x, x, before, after, table)
+
+
+def legendre_kernel(
+    dims, rates_ref, modes_ref, wave_ref, x_ref, basis_ref, spec_ref, *rest
+):
+    fields, levels, lev_dev, lev_count, subs, parts = dims
+    y_refs, (flat_ref, work_ref) = rest[: len(parts)], rest[len(parts) :]
+    group, wave_count, lat_count = basis_ref.shape
+    cols = fields * 2 * levels
+    tiles = lat_count // LANES
+    wave_tiles = wave_count // LANES
+    wide_count = x_ref.shape[0] // lev_count
+    per_tile = lat_count // wide_count // LANES
+    jw = LANES // levels
+
+    def place(f, r, l):
+        return (f * 2 + r) * levels + l
+
+    for w in range(wide_count):
+        for lx in range(lev_count):
+            for f in range(fields):
+                for l in range(lev_dev):
+                    for p in range(per_tile):
+                        lane = ((f * lev_dev + l) * per_tile + p) * LANES
+                        for r in range(2):
+                            block = x_ref[w * lev_count + lx, r, :, lane : lane + LANES].astype(jnp.float32)
+                            start = place(f, r, lx * lev_dev + l)
+                            for h in range(group // 8):
+                                flat_ref[w * per_tile + p, pl.ds(start + h * 8 * cols, 8, stride=cols), :] = block[
+                                    h * 8 : (h + 1) * 8
+                                ]
+
+    def forward(s, carry):
+        rows = pl.ds(pl.multiple_of(s * cols, 8), cols)
+        lhs = jnp.concatenate([flat_ref[t, rows, :].astype(jnp.bfloat16) for t in range(tiles)], axis=1)
+        raw = lax.dot_general(
+            lhs, basis_ref[s], (((1,), (1,)), ((), ())), preferred_element_type=jnp.float32
+        )
+        for t in range(wave_tiles):
+            work_ref[t, rows, :] = raw[:, t * LANES : (t + 1) * LANES]
+        return carry
+
+    lax.fori_loop(0, group, forward, 0, unroll=4)
+
+    def couple_tile(step, carry):
+        t, h = lax.div(step, group // 8), lax.rem(step, group // 8)
+        slot0 = pl.multiple_of(h * 8, 8)
+        wave = wave_ref[pl.ds(slot0, 8), :]
+        degree = wave + lax.broadcasted_iota(jnp.int32, (8, LANES), 1) + t * LANES
+        inside = degree < wave_count
+        curvature = (degree * (degree + 1)).astype(jnp.float32) * (1.0 / float(wave_count * wave_count))
+        for f in range(fields):
+            gains = [
+                jnp.where(inside, 1.0 / (1.0 + curvature * rates_ref[f, l]), 0.0) for l in range(levels)
+            ]
+            for r in range(2):
+                where = [pl.ds(slot0 * cols + place(f, r, l), 8, stride=cols) for l in range(levels)]
+                raw = [work_ref[t, where[l], :] for l in range(levels)]
+                if f == 0:
+                    spectral = [raw[l] * gains[l] for l in range(levels)]
+                else:
+                    scaled = []
+                    for i in range(levels):
+                        total = raw[0] * modes_ref[0, i]
+                        for l in range(1, levels):
+                            total = total + raw[l] * modes_ref[l, i]
+                        scaled.append(total * gains[i])
+                    spectral = []
+                    for l in range(levels):
+                        total = scaled[0] * modes_ref[l, 0]
+                        for i in range(1, levels):
+                            total = total + scaled[i] * modes_ref[l, i]
+                        spectral.append(total)
+                for l in range(levels):
+                    work_ref[t, where[l], :] = spectral[l]
+                    per_slot = fields * levels * wave_tiles * 2
+                    row = ((f * levels + l) * wave_tiles + t) * 2 + r
+                    spec_ref[pl.ds(slot0 * per_slot + row, 8, stride=per_slot), :] = spectral[l]
+        return carry
+
+    lax.fori_loop(0, wave_tiles * (group // 8), couple_tile, 0)
+
+    def backward(s, carry):
+        rows = pl.ds(pl.multiple_of(s * cols, 8), cols)
+        lhs = jnp.concatenate(
+            [work_ref[t, rows, :].astype(jnp.bfloat16) for t in range(wave_tiles)], axis=1
+        )
+        back = jnp.dot(lhs, basis_ref[s], preferred_element_type=jnp.float32)
+        for t in range(tiles):
+            flat_ref[t, rows, :] = back[:, t * LANES : (t + 1) * LANES]
+        return carry
+
+    lax.fori_loop(0, group, backward, 0, unroll=4)
+
+    lane = lax.broadcasted_iota(jnp.int32, (8, LANES), 1)
+    weights = [
+        jnp.where(wave_ref[h * 8 : (h + 1) * 8, :] == 0, 1.0, 2.0) for h in range(group // 8)
+    ]
+    part_of = {}
+    for index, members in enumerate(parts):
+        for place_in, sub in enumerate(members):
+            part_of[sub] = (index, place_in)
+    dest_per_tile = levels // subs if levels >= subs else 1
+
+    def scatter(t, carry):
+        for f in range(fields):
+            for r in range(2):
+                halves = []
+                for h in range(group // 8):
+                    start = h * 8 * cols
+                    pieces = [
+                        flat_ref[t, pl.ds(start + place(f, r, l), 8, stride=cols), :] * weights[h]
+                        for l in range(levels)
+                    ]
+                    bit = 1
+                    while bit < levels:
+                        shift = bit * jw
+                        odd = (lane // shift) % 2 == 1
+                        swapped = list(pieces)
+                        for l in range(levels):
+                            if l & bit == 0:
+                                low, high = pieces[l], pieces[l | bit]
+                                swapped[l] = jnp.where(odd, pltpu.roll(high, shift, 1), low)
+                                swapped[l | bit] = jnp.where(odd, high, pltpu.roll(low, LANES - shift, 1))
+                        pieces = swapped
+                        bit *= 2
+                    halves.append(pieces)
+                for g in range(levels):
+                    block = jnp.concatenate([half[g] for half in halves], axis=0).astype(jnp.bfloat16)
+                    index, place_in = part_of[g % subs]
+                    y_refs[index][t * dest_per_tile + g // subs, place_in, f, r] = block
+        return carry
+
+    lax.fori_loop(0, tiles, scatter, 0)
+
+
+def legendre(received, lat_basis, wave_part, vert_modes, vert_rates, dims):
+    fields, levels, lev_dev, lev_count, subs, parts = dims
+    devices = received.shape[0]
+    slots, wave_count, lat_count = lat_basis.shape
+    group = PACK
+    lanes_in = received.shape[-1]
+    cols = fields * 2 * levels
+    per_slot = fields * levels * (wave_count // LANES) * 2
+    outs = pl.pallas_call(
+        functools.partial(legendre_kernel, dims),
+        grid=(slots // group,),
+        in_specs=[
+            pl.BlockSpec(memory_space=pltpu.SMEM),
+            pl.BlockSpec(memory_space=pltpu.SMEM),
+            pl.BlockSpec((group, 1), lambda g: (g, 0)),
+            pl.BlockSpec((devices, 2, group, lanes_in), lambda g: (0, 0, g, 0)),
+            pl.BlockSpec((group, wave_count, lat_count), lambda g: (g, 0, 0)),
+        ],
+        out_specs=[pl.BlockSpec((group * per_slot, LANES), lambda g: (g, 0))]
+        + [
+            pl.BlockSpec((devices, len(p), fields, 2, group, LANES), lambda g: (0, 0, 0, 0, g, 0))
+            for p in parts
+        ],
+        out_shape=[jax.ShapeDtypeStruct((slots * per_slot, LANES), jnp.float32)]
+        + [
+            jax.ShapeDtypeStruct((devices, len(p), fields, 2, slots, LANES), jnp.bfloat16) for p in parts
+        ],
+        scratch_shapes=[
+            pltpu.VMEM((lat_count // LANES, group * cols, LANES), jnp.float32),
+            pltpu.VMEM((wave_count // LANES, group * cols, LANES), jnp.float32),
+        ],
+        compiler_params=pltpu.CompilerParams(vmem_limit_bytes=VMEM_BYTES),
+        cost_estimate=pl.CostEstimate(
+            flops=4 * slots * cols * wave_count * lat_count,
+            bytes_accessed=2 * slots * wave_count * lat_count,
+            transcendentals=0,
+        ),
+    )(vert_rates, vert_modes, wave_part[:, None], received.reshape(devices, 2, slots, lanes_in), lat_basis)
+    spec, parcels = outs[0], outs[1:]
+    spec = spec.reshape(slots, fields, levels, wave_count // LANES, 2, LANES)
+    spec = spec.transpose(0, 1, 2, 4, 3, 5).reshape(slots, 1, fields, levels, 2, wave_count)
+    return spec, parcels
+
+
+def column_kernel(
+    shape, band_ref, y_ref, table_ref, w_in_ref, w_mid_ref, w_out_ref, gain_ref, *rest
+):
+    fields, levels, jw, padded = shape
+    out_ref, grid_ref, done_ref = rest[-3:]
+    features = fields * levels
+    subs = y_ref.shape[1]
+    lon_count = table_ref.shape[1]
+    lon_tiles = lon_count // LANES
+    depth = table_ref.shape[0]
+    bands = (w_in_ref.shape[1] - padded) // 3
+    row = lax.broadcasted_iota(jnp.int32, (3 * bands, lon_count), 0)
+    for sub in range(subs):
+        lhs = jnp.concatenate(
+            [y_ref[:, sub, f].reshape(depth, LANES) for f in range(fields)], axis=1
+        )
+        grid_mid = lax.dot_general(
+            lhs, table_ref[...], (((0,), (0,)), ((), ())), preferred_element_type=jnp.float32
+        )
+        grid_mid = grid_mid.astype(jnp.bfloat16).astype(jnp.float32)
+        for t in range(lon_tiles):
+            grid_ref[t] = grid_mid[:, t * LANES : (t + 1) * LANES]
+
+        def one_row(j, carry):
+            where = pl.ds(j, features, stride=jw)
+            x = jnp.concatenate([grid_ref[t, where, :] for t in range(lon_tiles)], axis=1)
+            mean = jnp.sum(x * x, axis=0, keepdims=True) * (1.0 / features)
+            normed = x * lax.rsqrt(mean + norm_eps) * gain_ref[...]
+            if padded > features:
+                normed = jnp.concatenate(
+                    [normed, jnp.zeros((padded - features, lon_count), jnp.float32)], axis=0
+                )
+            chosen = lax.rem(row, bands) == band_ref[sub * jw + j]
+            entries = jnp.concatenate(
+                [normed.astype(jnp.bfloat16), jnp.where(chosen, 1.0, 0.0).astype(jnp.bfloat16)], axis=0
+            )
+            half = jnp.dot(w_in_ref[...], entries, preferred_element_type=jnp.float32)
+            hidden = (half * jnp.tanh(half) + half).astype(jnp.bfloat16)
+            half = jnp.dot(w_mid_ref[...], hidden, preferred_element_type=jnp.float32)
+            hidden = (half * jnp.tanh(half) + half).astype(jnp.bfloat16)
+            grown = jnp.dot(w_out_ref[...], hidden, preferred_element_type=jnp.float32)
+            result = x + grown[:features]
+            for t in range(lon_tiles):
+                done_ref[t, where, :] = result[:, t * LANES : (t + 1) * LANES]
+            return carry
+
+        lax.fori_loop(0, jw, one_row, 0)
+        for t in range(lon_tiles):
+            out_ref[:, sub * jw : (sub + 1) * jw, t * LANES : (t + 1) * LANES] = (
+                done_ref[t].reshape(features, jw, LANES).astype(jnp.bfloat16)
+            )
+
+
+def column_part(arrived, table, bands_here, weights, so_far, first, lat_quarter, dims):
+    fields, levels, jw = dims
+    w_in, w_mid, w_out, gain, padded = weights
+    subs = arrived.shape[1]
+    features = fields * levels
+    depth, lon_count = table.shape
+    rows = subs * jw
+    whole = pl.BlockSpec(memory_space=pltpu.VMEM)
+    args = [bands_here, arrived, table, w_in, w_mid, w_out, gain]
+    specs = [pl.BlockSpec(memory_space=pltpu.SMEM)] + [whole] * 6
+    aliases = {}
+    if so_far is not None:
+        args.append(so_far)
+        specs.append(pl.BlockSpec(memory_space=pl.ANY))
+        aliases = {len(args) - 1: 0}
+    block = first // rows
+    units = w_mid.shape[0]
+    return pl.pallas_call(
+        functools.partial(column_kernel, (fields, levels, jw, padded)),
+        grid=(1,),
+        in_specs=specs,
+        out_specs=pl.BlockSpec((features, rows, lon_count), lambda g: (0, block, 0)),
+        out_shape=jax.ShapeDtypeStruct((features, lat_quarter, lon_count), jnp.bfloat16),
+        input_output_aliases=aliases,
+        scratch_shapes=[
+            pltpu.VMEM((lon_count // LANES, features * jw, LANES), jnp.float32),
+            pltpu.VMEM((lon_count // LANES, features * jw, LANES), jnp.float32),
+        ],
+        compiler_params=pltpu.CompilerParams(vmem_limit_bytes=VMEM_BYTES),
+        cost_estimate=pl.CostEstimate(
+            flops=2 * rows * lon_count * units * (units + 2 * 256) + 2 * depth * lon_count * features * rows,
+            bytes_accessed=4 * features * rows * lon_count,
+            transcendentals=2 * rows * lon_count * units,
+        ),
+    )(*args)
+
+
+def local_tiled(
+    grid_state, wave_slots, lat_basis, vert_modes, vert_rates, band_sizes, norm_gain, w_in, band_bias, w_mid, w_out
+):
+    _, fields, lev_dev, lat_dev, lon_count = grid_state.shape
+    wide_count = lax.axis_size("wide")
+    lev_count = lax.axis_size("lev")
+    devices = wide_count * lev_count
+    slot_dev, wave_count, lat_count = lat_basis.shape
+    levels = lev_dev * lev_count
+    lat_quarter = lat_count // devices
+    jw = LANES // levels
+    subs = lat_quarter // jw
+    block_index = lax.axis_index("wide") * lev_count + lax.axis_index("lev")
+
+    up = [(i, i + 1) for i in range(wide_count - 1)]
+    down = [(j, i) for i, j in up]
+    before = lax.ppermute(grid_state[:, :, :, lat_dev - 1 :], "wide", up)
+    after = lax.ppermute(grid_state[:, :, :, :1], "wide", down)
+    angle_arrays = angle_parts(wave_slots, lon_count)
+    table = pl.pallas_call(
+        functools.partial(table_kernel, devices),
+        out_shape=jax.ShapeDtypeStruct((devices, 2, slot_dev, lon_count), jnp.bfloat16),
+        compiler_params=pltpu.CompilerParams(vmem_limit_bytes=VMEM_BYTES),
+    )(*angle_arrays).reshape(devices * 2 * slot_dev, lon_count)
+
+    coeffs = fourier(grid_state, before, after, table)
+    received = lax.all_to_all(
+        coeffs.reshape(devices, 2 * slot_dev, coeffs.shape[1]),
+        ("wide", "lev"),
+        split_axis=0,
+        concat_axis=0,
+        tiled=True,
+    )
+    wave_part = lax.dynamic_slice_in_dim(wave_slots, block_index * slot_dev, slot_dev)
+    count = 2 if subs % 2 == 0 else 1
+    parts = tuple(
+        tuple(range(i * subs // count, (i + 1) * subs // count)) for i in range(count)
+    )
+    dims = (fields, levels, lev_dev, lev_count, subs, parts)
+    spectral, parcels = legendre(received, lat_basis, wave_part, vert_modes, vert_rates, dims)
+
+    bands = band_sizes.shape[0]
+    latitude = block_index * lat_quarter + jnp.arange(lat_quarter, dtype=jnp.int32)
+    bands_here = jnp.sum(
+        (latitude[:, None] >= jnp.cumsum(band_sizes)[None, :]).astype(jnp.int32), axis=1
+    )
+    features = fields * levels
+    padded = -(-features // PACK) * PACK
+    pieces, rest = [], band_bias
+    for _ in range(3):
+        piece = lax.reduce_precision(rest, 8, 7)
+        pieces.append(piece.astype(jnp.bfloat16))
+        rest = rest - piece
+    half = jnp.bfloat16(0.5)
+    w_first = jnp.concatenate(
+        [jnp.pad(w_in, ((0, 0), (0, padded - features)))] + pieces, axis=1
+    ) * half
+    weights = (
+        w_first,
+        w_mid * half,
+        jnp.pad(w_out, ((0, padded - features), (0, 0))),
+        norm_gain[:, None],
+        padded,
+    )
+    new_state = None
+    for part, parcel in zip(parts, parcels):
+        arrived = lax.all_to_all(parcel, ("wide", "lev"), split_axis=0, concat_axis=0, tiled=True)
+        rows = slice(part[0] * jw, (part[-1] + 1) * jw)
+        new_state = column_part(
+            arrived, table, bands_here[rows], weights, new_state, part[0] * jw, lat_quarter, (fields, levels, jw)
+        )
+    return spectral, new_state.reshape(1, fields, levels, lat_quarter, lon_count)
+
+
+def local(grid_state, wave_slots, lat_basis, *rest):
+    members, _, lev_dev, lat_dev, lon_count = grid_state.shape
+    lev_count = lax.axis_size("lev")
+    slot_dev, wave_count, lat_count = lat_basis.shape
+    levels = lev_dev * lev_count
+    lat_quarter = lat_dev // lev_count
+    fits = (
+        members == 1
+        and levels == 8
+        and lat_dev % LANES == 0
+        and lon_count % LANES == 0
+        and wave_count % LANES == 0
+        and slot_dev % PACK == 0
+        and lat_quarter % (LANES // levels) == 0
+        and lat_quarter <= LANES
+    )
+    chosen = local_tiled if fits else local_plain
+    return chosen(grid_state, wave_slots, lat_basis, *rest)
+
+
 def solution(mesh):
     placed = (
         P(("groups", "fld"), None, "lev", "wide", None),

time: 635 us -> 285 us (0.45)
  local copies, waits for them, and re-layouts: 197 us -> 8.53 us
  matrix products: 180 us -> 0 us
  blocking collectives: 149 us -> 0 us
  Pallas kernels: 0 us -> 146 us
  waiting for transfers between devices: 38.4 us -> 101 us
  other arithmetic: 36.5 us -> 7.1 us
  starting transfers between devices: 29.4 us -> 19.6 us
    dot_general x9 -> x0, matrix products: 180 us -> none  [the longest x1 79.9 us: column_net(): jnp.einsum('fh,bhc->bfc', w_out, second, preferred_element_type=jnp.float32)]
    all_to_all x2 -> x0, blocking collectives: 149 us -> none  [the longest x1 74.5 us: local(): lax.all_to_all(coeffs, 'wide', split_axis=5, concat_axis=3, tiled=True)]
    pallas_call x0 -> x5, Pallas kernels: none -> 146 us  [the longest x2 89.1 us: column_part(): pl.pallas_call(functools.partial(column_kernel, (fields, levels, jw, padd...]
    all_to_all x2 -> x3, waiting for transfers between devices: 38.3 us -> 101 us  [the longest x1 68.7 us: local_tiled(): lax.all_to_all(coeffs.reshape(devices, 2 * slot_dev, coeffs.shape[1]), ('...]
    all_to_all x7 -> x0, local copies, waits for them, and re-layouts: 59.3 us -> none  [the longest x2 26.3 us: local(): lax.all_to_all(lax.all_to_all(parcel, 'wide', split_axis=7, concat_axis=0...]
    unnamed x44 -> x24, local copies, waits for them, and re-layouts: 61.1 us -> 3.72 us
    reshape x4 -> x0, local copies, waits for them, and re-layouts: 47.8 us -> none  [the longest x2 28.5 us: local(): coeffs.reshape(members, fields, lev_dev, lat_dev, 2, wide_count, lev_coun...]
    another operation x5 -> x2, other arithmetic: 21.1 us -> 0.16 us
  transfers between devices with their start and end apart: 4 -> 5, of which waited for: 2 -> 2; matrix products, arithmetic and copies ran while one was open for 7% -> 4% of each run, Pallas kernels for 0% -> 17%
where the time goes in v1:
time: 285 us; the launch traced here: 284 us
  Pallas kernels  146 us (51%)
  waiting for transfers between devices  101 us (35%)
  starting transfers between devices  19.6 us (7%)
  local copies, waits for them, and re-layouts  8.53 us (3%)
  other arithmetic  7.1 us (2%)
    pallas_call x2, Pallas kernels, column_part(): pl.pallas_call(functools.partial(column_kernel, (fields, levels, jw, padd...  89.1 us
    all_to_all x1, waiting for transfers between devices, local_tiled(): lax.all_to_all(coeffs.reshape(devices, 2 * slot_dev, coeffs.shape[1]), ('...  68.7 us
    pallas_call x1, Pallas kernels, legendre(): pl.pallas_call(functools.partial(legendre_kernel, dims), grid=(slots // g...  44 us
    all_to_all x2, waiting for transfers between devices, local_tiled(): lax.all_to_all(parcel, ('wide', 'lev'), split_axis=0, concat_axis=0, tile...  32.7 us
    pallas_call x1, Pallas kernels, fourier(): pl.pallas_call(fourier_kernel, grid=(fields, halves), in_specs=[pl.BlockS...  9.46 us
    all_to_all x2, starting transfers between devices, local_tiled(): lax.all_to_all(parcel, ('wide', 'lev'), split_axis=0, concat_axis=0, tile...  7.55 us
  transfers between devices with their start and end apart: 5, of which 2 were waited for; matrix products, arithmetic and copies ran while one was open for 4% of the time, Pallas kernels for 17%

profile of v1, /device:TPU:0, one launch (start us, length us, event | category | flops | bytes accessed | tf_op | source)
XLA Modules:
  0.0 283.9 jit_solution(8245208257698812487)
XLA Ops:
  0.6 1.1 fusion.15
  1.7 1.3 collective-permute-start.1
  3.0 5.6 %collective-permute-start = (bf16[1,3,4,1,1024]{4,3,2,1,0:T(2,128)(2,1)S(1)}, bf16[1,3,4,1,1024]{4,3,2,1,0:T(2,128)(2,1)S(1)}, u32[]{:S(2)}, u32[]{:S(2)}) collective-permute-start(bf16[1,3,4,1,1024]{4,3,2,1,0:T(2,128)(2,1)S(1)} %get-tuple-element.9), channel_id=1, source_target_pairs={{0,4},{4,8},{8,12},{1,5},{5,9},{9,13},{2,6},{6,10},{10,14},{3,7},{... | collective-permute-start | bytes 73736 | tf_op jit(solution)/shard_map/ppermute | solution.py:530
  8.6 0.8 fusion.13
  9.4 0.1 copy.44
  9.5 1.7 multiply_sine_fusion
  11.2 2.6 sine_multiply_fusion
  13.8 3.9 %shard_map.122 = bf16[8,2,64,1024]{3,2,1,0:T(8,128)(2,1)} custom-call(f32[512,8]{1,0:T(8,128)} %get-tuple-element.14.ca_ref, f32[512,8]{1,0:T(8,128)} %get-tuple-element.13.sa_ref, f32[512,128]{1,0:T(8,128)} %get-tuple-element.16.cb_ref, f32[512,128]{1,0:T(8,128)} %get-tuple-element.15.sb_ref), custom_call_target="tpu_custom_call" | custom-call | tf_op jit(solution)/shard_map/pallas_call | solution.py:533
  17.7 0.0 collective-permute-done.1
  17.7 0.0 collective-permute-done
  17.7 0.0 copy-start.10
  17.7 0.6 copy-done.9
  18.3 0.0 copy-done.10
  18.3 9.5 %shard_map.123 = bf16[1024,1536]{1,0:T(8,128)(2,1)} custom-call(bf16[3,4,128,1024]{3,2,1,0:T(8,128)(2,1)} %bitcast.21, bf16[3,4,128,1024]{3,2,1,0:T(8,128)(2,1)} %bitcast.22, bf16[3,4,1,1024]{3,2,1,0:T(2,128)(2,1)} %bitcast.27, bf16[3,4,1,1024]{3,2,1,0:T(2,128)(2,1)} %bitcast.26, bf16[1024,1024]{1,0:T(8,128)(2,1)} %bitcast.18), custom_call_target="tpu_custom_call" | custom-call | flops 3221225472 | bytes 6291456 | tf_op jit(solution)/shard_map/pallas_call | solution.py:225
  27.8 5.2 %all-to-all-start = ((bf16[8,128,1536]{2,1,0:T(8,128)(2,1)}), bf16[8,128,1536]{2,1,0:T(8,128)(2,1)S(1)}, u32[]{:S(2)}, u32[]{:S(2)}) async-start(bf16[8,128,1536]{2,1,0:T(8,128)(2,1)} %bitcast.17), calls=%async_computation | async-start | bytes 6291456 | tf_op jit(solution)/shard_map/all_to_all | solution.py:540
  33.0 0.8 dynamic-slice_bitcast_fusion
  33.8 0.7 copy.47.wave_ref
  34.5 68.7 %all-to-all-done = bf16[8,128,1536]{2,1,0:T(8,128)(2,1)S(1)} async-done(((bf16[8,128,1536]{2,1,0:T(8,128)(2,1)}), bf16[8,128,1536]{2,1,0:T(8,128)(2,1)S(1)}, u32[]{:S(2)}, u32[]{:S(2)}) %all-to-all-start) | async-done | bytes 3145760 | tf_op jit(solution)/shard_map/all_to_all | solution.py:540
  103.2 1.7 copy-done
  104.8 44.0 %shard_map.124 = (f32[12288,128]{1,0:T(8,128)}, bf16[8,2,3,2,64,128]{5,4,3,2,1,0:T(8,128)(2,1)}, bf16[8,2,3,2,64,128]{5,4,3,2,1,0:T(8,128)(2,1)}) custom-call(f32[3,8]{1,0:T(4,128)} %rates_ref.1, f32[8,8]{1,0:T(8,128)} %modes_ref.1, s32[64,1]{1,0:T(8,128)} %copy.47.wave_ref, bf16[8,2,64,1536]{3,2,1,0:T(8,128)(2,1)} %bitcast.16, bf16[64,512,512]{2,1,0:T(8,128)(2,1)} %basis_ref.1), custom_call_target="tpu_custom_call" | custom-call | flops 3221225472 | bytes 33554432 | tf_op jit(solution)/shard_map/pallas_call | solution.py:388
  148.8 0.0 copy-start.8
  148.8 0.0 copy-start.5
  148.8 0.0 copy-start.6
  148.9 0.0 copy-start.3
  148.9 3.8 %all-to-all-start.2 = ((bf16[8,2,3,2,64,128]{5,4,3,2,1,0:T(8,128)(2,1)}), bf16[8,2,3,2,64,128]{5,4,3,2,1,0:T(8,128)(2,1)S(1)}, u32[]{:S(2)}, u32[]{:S(2)}) async-start(bf16[8,2,3,2,64,128]{5,4,3,2,1,0:T(8,128)(2,1)} %get-tuple-element.7), calls=%async_computation.2 | async-start | bytes 3145728 | tf_op jit(solution)/shard_map/all_to_all | solution.py:580
  152.7 0.0 copy-done.4
  152.7 0.1 copy.52
  152.8 0.0 copy-done.7
  152.8 0.1 copy.49
  152.9 0.1 reduce
  153.1 0.0 copy-done.8
  153.1 0.7 copy.55.gain_ref
  153.7 0.0 copy-done.5
  153.7 0.1 copy.50
  153.9 0.1 copy.51
  154.0 0.0 copy-done.6
  154.0 0.6 pad.9.w_out_ref
  154.6 0.1 convert_reduce_fusion
  154.7 0.1 reduce-precision_convert_fusion
  154.8 0.8 fusion.12.w_in_ref
  155.6 0.6 fusion.16
  156.2 0.9 broadcast_multiply_fusion.w_mid_ref
  157.1 32.7 %all-to-all-done.2.y_ref = bf16[8,2,3,2,64,128]{5,4,3,2,1,0:T(8,128)(2,1)S(1)} async-done(((bf16[8,2,3,2,64,128]{5,4,3,2,1,0:T(8,128)(2,1)}), bf16[8,2,3,2,64,128]{5,4,3,2,1,0:T(8,128)(2,1)S(1)}, u32[]{:S(2)}, u32[]{:S(2)}) %all-to-all-start.2) | async-done | bytes 1572896 | tf_op jit(solution)/shard_map/all_to_all | solution.py:580
  189.8 3.8 %all-to-all-start.1 = ((bf16[8,2,3,2,64,128]{5,4,3,2,1,0:T(8,128)(2,1)}), bf16[8,2,3,2,64,128]{5,4,3,2,1,0:T(8,128)(2,1)S(1)}, u32[]{:S(2)}, u32[]{:S(2)}) async-start(bf16[8,2,3,2,64,128]{5,4,3,2,1,0:T(8,128)(2,1)} %get-tuple-element.6), calls=%async_computation.1 | async-start | bytes 3145728 | tf_op jit(solution)/shard_map/all_to_all | solution.py:580
  193.6 44.5 %shard_map.125.rest_0_ = bf16[24,64,1024]{2,1,0:T(8,128)(2,1)} custom-call(s32[32]{0:T(128)} %get-tuple-element.17.band_ref, bf16[8,2,3,2,64,128]{5,4,3,2,1,0:T(8,128)(2,1)} %copy-done.1, bf16[1024,1024]{1,0:T(8,128)(2,1)} %bitcast.19, bf16[512,80]{1,0:T(8,128)(2,1)} %fusion.12.w_in_ref, bf16[512,512]{1,0:T(8,128)(2,1)} %broadcast_multiply_fusion.w_mid_ref, ...), custom_call_target="tpu_custom_call" | custom-call | flops 35970351104 | bytes 3145728 | tf_op jit(solution)/shard_map/pallas_call | solution.py:494
  238.2 0.0 all-to-all-done.1.y_ref
  238.2 1.2 copy-done.2
  239.3 44.6 %shard_map.126 = bf16[24,64,1024]{2,1,0:T(8,128)(2,1)} custom-call(s32[32]{0:T(128)} %get-tuple-element.18.band_ref, bf16[8,2,3,2,64,128]{5,4,3,2,1,0:T(8,128)(2,1)} %copy-done.2, bf16[1024,1024]{1,0:T(8,128)(2,1)} %bitcast.20, bf16[512,80]{1,0:T(8,128)(2,1)} %fusion.12.w_in_ref, ...), custom_call_target="tpu_custom_call", output_to_operand_aliasing={{}: (7, {})} | custom-call | flops 35970351104 | bytes 3145728 | tf_op jit(solution)/shard_map/pallas_call | solution.py:494
  (12 shorter events, 0.1 us)
Async XLA Ops:
  1.7 15.9 %collective-permute-start.1 = (bf16[1,3,4,1,1024]{4,3,2,1,0:T(2,128)(2,1)S(1)}, bf16[1,3,4,1,1024]{4,3,2,1,0:T(2,128)(2,1)S(1)}, u32[]{:S(2)}, u32[]{:S(2)}) collective-permute-start(bf16[1,3,4,1,1024]{4,3,2,1,0:T(2,128)(2,1)S(1)} %get-tuple-element.8), channel_id=1, source_target_pairs={{4,0},{8,4},{12,8},{5,1},{9,5},{13,9},{6,2},{10,6},{14,10},{7,3},{... | collective-permute-start | bytes 73736 | tf_op jit(solution)/shard_map/ppermute | solution.py:531
  3.0 14.7 %collective-permute-start = (bf16[1,3,4,1,1024]{4,3,2,1,0:T(2,128)(2,1)S(1)}, bf16[1,3,4,1,1024]{4,3,2,1,0:T(2,128)(2,1)S(1)}, u32[]{:S(2)}, u32[]{:S(2)}) collective-permute-start(bf16[1,3,4,1,1024]{4,3,2,1,0:T(2,128)(2,1)S(1)} %get-tuple-element.9), channel_id=1, source_target_pairs={{0,4},{4,8},{8,12},{1,5},{5,9},{9,13},{2,6},{6,10},{10,14},{3,7},{... | collective-permute-start | bytes 73736 | tf_op jit(solution)/shard_map/ppermute | solution.py:530
  17.7 0.6 copy-start.9
  17.7 0.6 copy-start.10
  27.8 75.4 %all-to-all-start = ((bf16[8,128,1536]{2,1,0:T(8,128)(2,1)}), bf16[8,128,1536]{2,1,0:T(8,128)(2,1)S(1)}, u32[]{:S(2)}, u32[]{:S(2)}) async-start(bf16[8,128,1536]{2,1,0:T(8,128)(2,1)} %bitcast.17), calls=%async_computation | async-start | bytes 6291456 | tf_op jit(solution)/shard_map/all_to_all | solution.py:540
  103.2 1.7 copy-start
  148.8 3.8 %copy-start.4 = (f32[512,16]{0,1:T(8,128)S(1)}, f32[512,16]{0,1:T(8,128)}, u32[]{:S(2)}) copy-start(f32[512,16]{0,1:T(8,128)} %param.19) | copy-start | bytes 98308
  148.8 4.0 %copy-start.7 = (s32[16]{0:T(128)S(1)}, s32[16]{0:T(128)}, u32[]{:S(2)}) copy-start(s32[16]{0:T(128)} %param.16) | copy-start | bytes 196
  148.8 4.2 %copy-start.8 = (f32[24]{0:T(128)S(1)}, f32[24]{0:T(128)}, u32[]{:S(2)}) copy-start(f32[24]{0:T(128)} %param.17) | copy-start | bytes 292
  148.8 4.9 %copy-start.5 = (bf16[512,24]{0,1:T(8,128)(2,1)S(1)}, bf16[512,24]{0,1:T(8,128)(2,1)}, u32[]{:S(2)}) copy-start(bf16[512,24]{0,1:T(8,128)(2,1)} %param.18) | copy-start | bytes 73732
  148.8 5.2 %copy-start.6 = (bf16[24,512]{1,0:T(8,128)(2,1)S(1)}, bf16[24,512]{1,0:T(8,128)(2,1)}, u32[]{:S(2)}) copy-start(bf16[24,512]{1,0:T(8,128)(2,1)} %param.21) | copy-start | bytes 73732
  148.9 7.4 %copy-start.3 = (bf16[512,512]{1,0:T(8,128)(2,1)S(1)}, bf16[512,512]{1,0:T(8,128)(2,1)}, u32[]{:S(2)}) copy-start(bf16[512,512]{1,0:T(8,128)(2,1)} %param.20) | copy-start | bytes 1572868
  148.9 41.0 %all-to-all-start.2 = ((bf16[8,2,3,2,64,128]{5,4,3,2,1,0:T(8,128)(2,1)}), bf16[8,2,3,2,64,128]{5,4,3,2,1,0:T(8,128)(2,1)S(1)}, u32[]{:S(2)}, u32[]{:S(2)}) async-start(bf16[8,2,3,2,64,128]{5,4,3,2,1,0:T(8,128)(2,1)} %get-tuple-element.7), calls=%async_computation.2 | async-start | bytes 3145728 | tf_op jit(solution)/shard_map/all_to_all | solution.py:580
  189.8 3.8 %copy-start.1 = (bf16[8,2,3,2,64,128]{5,4,3,2,1,0:T(8,128)(2,1)}, bf16[8,2,3,2,64,128]{5,4,3,2,1,0:T(8,128)(2,1)S(1)}, u32[]{:S(2)}) copy-start(bf16[8,2,3,2,64,128]{5,4,3,2,1,0:T(8,128)(2,1)S(1)} %all-to-all-done.2.y_ref) | copy-start | bytes 4718596
  189.8 48.3 %all-to-all-start.1 = ((bf16[8,2,3,2,64,128]{5,4,3,2,1,0:T(8,128)(2,1)}), bf16[8,2,3,2,64,128]{5,4,3,2,1,0:T(8,128)(2,1)S(1)}, u32[]{:S(2)}, u32[]{:S(2)}) async-start(bf16[8,2,3,2,64,128]{5,4,3,2,1,0:T(8,128)(2,1)} %get-tuple-element.6), calls=%async_computation.1 | async-start | bytes 3145728 | tf_op jit(solution)/shard_map/all_to_all | solution.py:580
  238.2 1.2 copy-start.2

commit v2 on v1

--- a/solution.py
+++ b/solution.py
@@ -185,9 +185,9 @@
     return jnp.cos(a), jnp.sin(a), jnp.cos(b) * scale, jnp.sin(b) * scale
 
 
-def table_kernel(devices, ca_ref, sa_ref, cb_ref, sb_ref, out_ref):
-    slots, tiles = ca_ref.shape
-    per = slots // devices
+def table_kernel(ca_ref, sa_ref, cb_ref, sb_ref, out_ref):
+    tiles = ca_ref.shape[1]
+    chunks, devices, _, per, _ = out_ref.shape
     cb, sb = cb_ref[...], sb_ref[...]
     for t in range(tiles):
         ca, sa = ca_ref[:, t : t + 1], sa_ref[:, t : t + 1]
@@ -195,12 +195,13 @@
         minus_sine = (-(sa * cb + ca * sb)).astype(jnp.bfloat16)
         cols = slice(t * LANES, (t + 1) * LANES)
         for d in range(devices):
-            rows = slice(d * per, (d + 1) * per)
-            out_ref[d, 0, :, cols] = cosine[rows]
-            out_ref[d, 1, :, cols] = minus_sine[rows]
-
-
-def fourier_kernel(x_ref, next_ref, before_ref, after_ref, table_ref, out_ref):
+            for c in range(chunks):
+                first = (d * chunks + c) * per
+                out_ref[c, d, 0, :, cols] = cosine[first : first + per]
+                out_ref[c, d, 1, :, cols] = minus_sine[first : first + per]
+
+
+def fourier_kernel(x_ref, next_ref, before_ref, after_ref, table_ref, *out_refs):
     _, levels, rows, _ = x_ref.shape
     parts = []
     row = lax.broadcasted_iota(jnp.int32, (rows, 1), 0)
@@ -211,12 +212,15 @@
         mixed = x + transport_speed * next_ref[0, l].astype(jnp.float32) * (up - down)
         parts.append(mixed.astype(jnp.bfloat16))
     advected = jnp.concatenate(parts, axis=0)
-    out_ref[...] = lax.dot_general(
+    coeffs = lax.dot_general(
         table_ref[...], advected, (((1,), (1,)), ((), ())), preferred_element_type=jnp.float32
     ).astype(jnp.bfloat16)
-
-
-def fourier(grid_state, before, after, table):
+    rows = coeffs.shape[0] // len(out_refs)
+    for c, out_ref in enumerate(out_refs):
+        out_ref[...] = coeffs[c * rows : (c + 1) * rows]
+
+
+def fourier(grid_state, before, after, table, chunks):
     _, fields, lev_dev, lat_dev, lon_count = grid_state.shape
     x, before, after = grid_state[0], before[0], after[0]
     pair = 2 if lev_dev % 2 == 0 else 1
@@ -232,8 +236,8 @@
             pl.BlockSpec((1, pair, 1, lon_count), lambda f, h: (f, h, 0, 0)),
             pl.BlockSpec((rows, lon_count), lambda f, h: (0, 0)),
         ],
-        out_specs=pl.BlockSpec((rows, pair * lat_dev), lambda f, h: (0, f * halves + h)),
-        out_shape=jax.ShapeDtypeStruct((rows, fields * lev_dev * lat_dev), jnp.bfloat16),
+        out_specs=[pl.BlockSpec((rows // chunks, pair * lat_dev), lambda f, h: (0, f * halves + h))] * chunks,
+        out_shape=[jax.ShapeDtypeStruct((rows // chunks, fields * lev_dev * lat_dev), jnp.bfloat16)] * chunks,
         compiler_params=pltpu.CompilerParams(vmem_limit_bytes=VMEM_BYTES),
         cost_estimate=pl.CostEstimate(
             flops=2 * rows * lon_count * fields * lev_dev * lat_dev,
@@ -244,10 +248,11 @@
 
 
 def legendre_kernel(
-    dims, rates_ref, modes_ref, wave_ref, x_ref, basis_ref, spec_ref, *rest
+    dims, rates_ref, modes_ref, wave_ref, x_ref, basis_ref, *rest
 ):
     fields, levels, lev_dev, lev_count, subs, parts = dims
-    y_refs, (flat_ref, work_ref) = rest[: len(parts)], rest[len(parts) :]
+    rest = rest[-len(parts) - 3 :]
+    spec_ref, y_refs, (flat_ref, work_ref) = rest[0], rest[1:-2], rest[-2:]
     group, wave_count, lat_count = basis_ref.shape
     cols = fields * 2 * levels
     tiles = lat_count // LANES
@@ -283,7 +288,7 @@
             work_ref[t, rows, :] = raw[:, t * LANES : (t + 1) * LANES]
         return carry
 
-    lax.fori_loop(0, group, forward, 0, unroll=4)
+    lax.fori_loop(0, group, forward, 0, unroll=16)
 
     def couple_tile(step, carry):
         t, h = lax.div(step, group // 8), lax.rem(step, group // 8)
@@ -292,33 +297,41 @@
         degree = wave + lax.broadcasted_iota(jnp.int32, (8, LANES), 1) + t * LANES
         inside = degree < wave_count
         curvature = (degree * (degree + 1)).astype(jnp.float32) * (1.0 / float(wave_count * wave_count))
-        for f in range(fields):
-            gains = [
-                jnp.where(inside, 1.0 / (1.0 + curvature * rates_ref[f, l]), 0.0) for l in range(levels)
-            ]
+        per_slot = fields * levels * wave_tiles * 2
+
+        def gain(f, l):
+            return jnp.where(inside, 1.0 / (1.0 + curvature * rates_ref[f, l]), 0.0)
+
+        def where(f, r, l):
+            return pl.ds(slot0 * cols + place(f, r, l), 8, stride=cols)
+
+        def keep(f, r, l, value):
+            work_ref[t, where(f, r, l), :] = value
+            row = ((f * levels + l) * wave_tiles + t) * 2 + r
+            spec_ref[pl.ds(slot0 * per_slot + row, 8, stride=per_slot), :] = value
+
+        for l in range(levels):
+            scale = gain(0, l)
             for r in range(2):
-                where = [pl.ds(slot0 * cols + place(f, r, l), 8, stride=cols) for l in range(levels)]
-                raw = [work_ref[t, where[l], :] for l in range(levels)]
-                if f == 0:
-                    spectral = [raw[l] * gains[l] for l in range(levels)]
-                else:
-                    scaled = []
-                    for i in range(levels):
-                        total = raw[0] * modes_ref[0, i]
-                        for l in range(1, levels):
-                            total = total + raw[l] * modes_ref[l, i]
-                        scaled.append(total * gains[i])
-                    spectral = []
-                    for l in range(levels):
-                        total = scaled[0] * modes_ref[l, 0]
-                        for i in range(1, levels):
-                            total = total + scaled[i] * modes_ref[l, i]
-                        spectral.append(total)
-                for l in range(levels):
-                    work_ref[t, where[l], :] = spectral[l]
-                    per_slot = fields * levels * wave_tiles * 2
-                    row = ((f * levels + l) * wave_tiles + t) * 2 + r
-                    spec_ref[pl.ds(slot0 * per_slot + row, 8, stride=per_slot), :] = spectral[l]
+                keep(0, r, l, work_ref[t, where(0, r, l), :] * scale)
+        for f in range(1, fields):
+            raw = [[work_ref[t, where(f, r, l), :] for l in range(levels)] for r in range(2)]
+            scaled = [[], []]
+            for i in range(levels):
+                totals = [raw[r][0] * modes_ref[0, i] for r in range(2)]
+                for l in range(1, levels):
+                    mode = modes_ref[l, i]
+                    totals = [totals[r] + raw[r][l] * mode for r in range(2)]
+                scale = gain(f, i)
+                for r in range(2):
+                    scaled[r].append(totals[r] * scale)
+            for l in range(levels):
+                totals = [scaled[r][0] * modes_ref[l, 0] for r in range(2)]
+                for i in range(1, levels):
+                    mode = modes_ref[l, i]
+                    totals = [totals[r] + scaled[r][i] * mode for r in range(2)]
+                for r in range(2):
+                    keep(f, r, l, totals[r])
         return carry
 
     lax.fori_loop(0, wave_tiles * (group // 8), couple_tile, 0)
@@ -333,7 +346,7 @@
             flat_ref[t, rows, :] = back[:, t * LANES : (t + 1) * LANES]
         return carry
 
-    lax.fori_loop(0, group, backward, 0, unroll=4)
+    lax.fori_loop(0, group, backward, 0, unroll=16)
 
     lane = lax.broadcasted_iota(jnp.int32, (8, LANES), 1)
     weights = [
@@ -371,71 +384,95 @@
                 for g in range(levels):
                     block = jnp.concatenate([half[g] for half in halves], axis=0).astype(jnp.bfloat16)
                     index, place_in = part_of[g % subs]
-                    y_refs[index][t * dest_per_tile + g // subs, place_in, f, r] = block
+                    y_refs[index][t * dest_per_tile + g // subs, 0, place_in, f, r] = block
         return carry
 
     lax.fori_loop(0, tiles, scatter, 0)
 
 
-def legendre(received, lat_basis, wave_part, vert_modes, vert_rates, dims):
-    fields, levels, lev_dev, lev_count, subs, parts = dims
+def legendre(received, lat_basis, wave_part, vert_modes, vert_rates, chunk, so_far, dims):
+    fields, levels, lev_dev, lev_count, subs, parts, chunks = dims
     devices = received.shape[0]
     slots, wave_count, lat_count = lat_basis.shape
     group = PACK
     lanes_in = received.shape[-1]
+    here = slots // chunks
+    steps = here // group
     cols = fields * 2 * levels
     per_slot = fields * levels * (wave_count // LANES) * 2
-    outs = pl.pallas_call(
-        functools.partial(legendre_kernel, dims),
-        grid=(slots // group,),
+    args = [vert_rates, vert_modes, wave_part[:, None], received.reshape(devices, 2, here, lanes_in), lat_basis]
+    aliases = {}
+    if so_far is not None:
+        kept = [0] + list(range(2, 1 + len(parts)))
+        aliases = {len(args) + n: k for n, k in enumerate(kept)}
+        args = args + [so_far[k] for k in kept]
+    first = chunk * steps
+
+    def part_spec(index, part):
+        block = (devices, 1, len(part), fields, 2, group, LANES)
+        if index == 0:
+            return pl.BlockSpec(block, lambda g: (0, 0, 0, 0, 0, g, 0))
+        return pl.BlockSpec(block, lambda g: (0, chunk, 0, 0, 0, g, 0))
+
+    return pl.pallas_call(
+        functools.partial(legendre_kernel, (fields, levels, lev_dev, lev_count, subs, parts)),
+        grid=(steps,),
         in_specs=[
             pl.BlockSpec(memory_space=pltpu.SMEM),
             pl.BlockSpec(memory_space=pltpu.SMEM),
-            pl.BlockSpec((group, 1), lambda g: (g, 0)),
+            pl.BlockSpec((group, 1), lambda g: (first + g, 0)),
             pl.BlockSpec((devices, 2, group, lanes_in), lambda g: (0, 0, g, 0)),
-            pl.BlockSpec((group, wave_count, lat_count), lambda g: (g, 0, 0)),
-        ],
-        out_specs=[pl.BlockSpec((group * per_slot, LANES), lambda g: (g, 0))]
-        + [
-            pl.BlockSpec((devices, len(p), fields, 2, group, LANES), lambda g: (0, 0, 0, 0, g, 0))
-            for p in parts
-        ],
+            pl.BlockSpec((group, wave_count, lat_count), lambda g: (first + g, 0, 0)),
+        ]
+        + [pl.BlockSpec(memory_space=pl.ANY)] * len(aliases),
+        out_specs=[pl.BlockSpec((group * per_slot, LANES), lambda g: (first + g, 0))]
+        + [part_spec(i, p) for i, p in enumerate(parts)],
         out_shape=[jax.ShapeDtypeStruct((slots * per_slot, LANES), jnp.float32)]
         + [
-            jax.ShapeDtypeStruct((devices, len(p), fields, 2, slots, LANES), jnp.bfloat16) for p in parts
+            jax.ShapeDtypeStruct(
+                (devices, chunks if i else 1, len(p), fields, 2, here, LANES), jnp.bfloat16
+            )
+            for i, p in enumerate(parts)
         ],
+        input_output_aliases=aliases,
         scratch_shapes=[
             pltpu.VMEM((lat_count // LANES, group * cols, LANES), jnp.float32),
             pltpu.VMEM((wave_count // LANES, group * cols, LANES), jnp.float32),
         ],
         compiler_params=pltpu.CompilerParams(vmem_limit_bytes=VMEM_BYTES),
         cost_estimate=pl.CostEstimate(
-            flops=4 * slots * cols * wave_count * lat_count,
-            bytes_accessed=2 * slots * wave_count * lat_count,
+            flops=40 * here * cols * wave_count * lat_count,
+            bytes_accessed=2 * here * wave_count * lat_count,
             transcendentals=0,
         ),
-    )(vert_rates, vert_modes, wave_part[:, None], received.reshape(devices, 2, slots, lanes_in), lat_basis)
-    spec, parcels = outs[0], outs[1:]
-    spec = spec.reshape(slots, fields, levels, wave_count // LANES, 2, LANES)
-    spec = spec.transpose(0, 1, 2, 4, 3, 5).reshape(slots, 1, fields, levels, 2, wave_count)
-    return spec, parcels
+    )(*args)
 
 
 def column_kernel(
-    shape, band_ref, y_ref, table_ref, w_in_ref, w_mid_ref, w_out_ref, gain_ref, *rest
+    shape, band_ref, table_ref, w_in_ref, w_mid_ref, w_out_ref, gain_ref, *rest
 ):
-    fields, levels, jw, padded = shape
-    out_ref, grid_ref, done_ref = rest[-3:]
+    fields, levels, jw, padded, count = shape
+    y_refs, (out_ref, grid_ref, done_ref) = rest[:count], rest[-3:]
     features = fields * levels
-    subs = y_ref.shape[1]
+    subs = y_refs[0].shape[2]
     lon_count = table_ref.shape[1]
     lon_tiles = lon_count // LANES
-    depth = table_ref.shape[0]
     bands = (w_in_ref.shape[1] - padded) // 3
     row = lax.broadcasted_iota(jnp.int32, (3 * bands, lon_count), 0)
     for sub in range(subs):
         lhs = jnp.concatenate(
-            [y_ref[:, sub, f].reshape(depth, LANES) for f in range(fields)], axis=1
+            [
+                jnp.concatenate(
+                    [
+                        y_ref[:, c, sub, f].reshape(-1, LANES)
+                        for y_ref in y_refs
+                        for c in range(y_ref.shape[1])
+                    ],
+                    axis=0,
+                )
+                for f in range(fields)
+            ],
+            axis=1,
         )
         grid_mid = lax.dot_general(
             lhs, table_ref[...], (((0,), (0,)), ((), ())), preferred_element_type=jnp.float32
@@ -476,14 +513,15 @@
 
 def column_part(arrived, table, bands_here, weights, so_far, first, lat_quarter, dims):
     fields, levels, jw = dims
-    w_in, w_mid, w_out, gain, padded = weights
-    subs = arrived.shape[1]
+    w_in, w_mid, w_out, gain = weights
+    padded = w_out.shape[0]
+    subs = arrived[0].shape[2]
     features = fields * levels
     depth, lon_count = table.shape
     rows = subs * jw
     whole = pl.BlockSpec(memory_space=pltpu.VMEM)
-    args = [bands_here, arrived, table, w_in, w_mid, w_out, gain]
-    specs = [pl.BlockSpec(memory_space=pltpu.SMEM)] + [whole] * 6
+    args = [bands_here, table, w_in, w_mid, w_out, gain] + list(arrived)
+    specs = [pl.BlockSpec(memory_space=pltpu.SMEM)] + [whole] * (5 + len(arrived))
     aliases = {}
     if so_far is not None:
         args.append(so_far)
@@ -492,7 +530,7 @@
     block = first // rows
     units = w_mid.shape[0]
     return pl.pallas_call(
-        functools.partial(column_kernel, (fields, levels, jw, padded)),
+        functools.partial(column_kernel, (fields, levels, jw, padded, len(arrived))),
         grid=(1,),
         in_specs=specs,
         out_specs=pl.BlockSpec((features, rows, lon_count), lambda g: (0, block, 0)),
@@ -525,33 +563,33 @@
     subs = lat_quarter // jw
     block_index = lax.axis_index("wide") * lev_count + lax.axis_index("lev")
 
+    chunks = 2 if slot_dev % (2 * PACK) == 0 else 1
+    angle_arrays = angle_parts(wave_slots, lon_count)
+    edges = (grid_state[:, :, :, lat_dev - 1 :], grid_state[:, :, :, :1])
+    edges, angle_arrays = lax.optimization_barrier((edges, angle_arrays))
     up = [(i, i + 1) for i in range(wide_count - 1)]
     down = [(j, i) for i, j in up]
-    before = lax.ppermute(grid_state[:, :, :, lat_dev - 1 :], "wide", up)
-    after = lax.ppermute(grid_state[:, :, :, :1], "wide", down)
-    angle_arrays = angle_parts(wave_slots, lon_count)
+    before = lax.ppermute(edges[0], "wide", up)
+    after = lax.ppermute(edges[1], "wide", down)
     table = pl.pallas_call(
-        functools.partial(table_kernel, devices),
-        out_shape=jax.ShapeDtypeStruct((devices, 2, slot_dev, lon_count), jnp.bfloat16),
+        table_kernel,
+        out_shape=jax.ShapeDtypeStruct(
+            (chunks, devices, 2, slot_dev // chunks, lon_count), jnp.bfloat16
+        ),
         compiler_params=pltpu.CompilerParams(vmem_limit_bytes=VMEM_BYTES),
     )(*angle_arrays).reshape(devices * 2 * slot_dev, lon_count)
 
-    coeffs = fourier(grid_state, before, after, table)
-    received = lax.all_to_all(
-        coeffs.reshape(devices, 2 * slot_dev, coeffs.shape[1]),
-        ("wide", "lev"),
-        split_axis=0,
-        concat_axis=0,
-        tiled=True,
-    )
+    def exchange(parcel):
+        return lax.all_to_all(parcel, ("wide", "lev"), split_axis=0, concat_axis=0, tiled=True)
+
+    coeffs = fourier(grid_state, before, after, table, chunks)
+    received = [exchange(c.reshape(devices, -1, c.shape[1])) for c in coeffs]
     wave_part = lax.dynamic_slice_in_dim(wave_slots, block_index * slot_dev, slot_dev)
     count = 2 if subs % 2 == 0 else 1
     parts = tuple(
         tuple(range(i * subs // count, (i + 1) * subs // count)) for i in range(count)
     )
-    dims = (fields, levels, lev_dev, lev_count, subs, parts)
-    spectral, parcels = legendre(received, lat_basis, wave_part, vert_modes, vert_rates, dims)
-
+    dims = (fields, levels, lev_dev, lev_count, subs, parts, chunks)
     bands = band_sizes.shape[0]
     latitude = block_index * lat_quarter + jnp.arange(lat_quarter, dtype=jnp.int32)
     bands_here = jnp.sum(
@@ -573,11 +611,21 @@
         w_mid * half,
         jnp.pad(w_out, ((0, padded - features), (0, 0))),
         norm_gain[:, None],
-        padded,
-    )
+    )
+    received[0], weights, bands_here = lax.optimization_barrier((received[0], weights, bands_here))
+    so_far, arrived_first = None, []
+    for c in range(chunks):
+        so_far = legendre(received[c], lat_basis, wave_part, vert_modes, vert_rates, c, so_far, dims)
+        parcel = so_far[1]
+        if arrived_first:
+            arrived_first[-1], parcel = lax.optimization_barrier((arrived_first[-1], parcel))
+        arrived_first.append(exchange(parcel))
+    spectral = so_far[0].reshape(slot_dev, fields, levels, wave_count // LANES, 2, LANES)
+    spectral = spectral.transpose(0, 1, 2, 4, 3, 5).reshape(slot_dev, 1, fields, levels, 2, wave_count)
+
     new_state = None
-    for part, parcel in zip(parts, parcels):
-        arrived = lax.all_to_all(parcel, ("wide", "lev"), split_axis=0, concat_axis=0, tiled=True)
+    for index, part in enumerate(parts):
+        arrived = [exchange(so_far[1 + index])] if index else arrived_first
         rows = slice(part[0] * jw, (part[-1] + 1) * jw)
         new_state = column_part(
             arrived, table, bands_here[rows], weights, new_state, part[0] * jw, lat_quarter, (fields, levels, jw)

time: 285 us -> 257 us (0.902)
  waiting for transfers between devices: 101 us -> 28.8 us
  blocking collectives: 0 us -> 42.7 us
  starting transfers between devices: 19.6 us -> 23.3 us
    all_to_all x3 -> x4, waiting for transfers between devices: 101 us -> 28 us  [exchange(): lax.all_to_all(parcel, ('wide', 'lev'), split_axis=0, concat_axis=0, tile...]
    all_to_all x0 -> x1, blocking collectives: none -> 42.7 us  [exchange(): lax.all_to_all(parcel, ('wide', 'lev'), split_axis=0, concat_axis=0, tile...]
    all_to_all x3 -> x4, starting transfers between devices: 12.8 us -> 17.1 us  [exchange(): lax.all_to_all(parcel, ('wide', 'lev'), split_axis=0, concat_axis=0, tile...]
    pallas_call x2 -> x3, Pallas kernels: 47.9 us -> 48.6 us  [the longest x2 44.7 us: legendre(): pl.pallas_call(functools.partial(legendre_kernel, (fields, levels, lev_de...]
  transfers between devices with their start and end apart: 5 -> 6, of which waited for: 2 -> 3; matrix products, arithmetic and copies ran while one was open for 4% -> 2% of each run, Pallas kernels for 17% -> 36%
where the time goes in v2:
time: 257 us
  Pallas kernels  147 us (57%)
  blocking collectives  42.7 us (17%)
  waiting for transfers between devices  28.8 us (11%)
  starting transfers between devices  23.3 us (9%)
  other arithmetic  7.26 us (3%)
  local copies, waits for them, and re-layouts  6.73 us (3%)
    pallas_call x2, Pallas kernels, column_part(): pl.pallas_call(functools.partial(column_kernel, (fields, levels, jw, padd...  89.3 us
    pallas_call x2, Pallas kernels, legendre(): pl.pallas_call(functools.partial(legendre_kernel, (fields, levels, lev_de...  44.7 us
    all_to_all x1, blocking collectives, exchange(): lax.all_to_all(parcel, ('wide', 'lev'), split_axis=0, concat_axis=0, tile...  42.7 us
    all_to_all x4, waiting for transfers between devices, exchange(): lax.all_to_all(parcel, ('wide', 'lev'), split_axis=0, concat_axis=0, tile...  28 us
    all_to_all x4, starting transfers between devices, exchange(): lax.all_to_all(parcel, ('wide', 'lev'), split_axis=0, concat_axis=0, tile...  17.1 us
    pallas_call x1, Pallas kernels, fourier(): pl.pallas_call(fourier_kernel, grid=(fields, halves), in_specs=[pl.BlockS...  9.22 us
  transfers between devices with their start and end apart: 6, of which 3 were waited for; matrix products, arithmetic and copies ran while one was open for 2% of the time, Pallas kernels for 36%

profile of v2, /device:TPU:0, one launch (start us, length us, event | category | flops | bytes accessed | tf_op | source)
XLA Modules:
  0.0 256.8 jit_solution(107826249305533292)
XLA Ops:
  0.6 2.6 %sine_multiply_fusion = (f32[512,128]{1,0:T(8,128)}, f32[512,128]{1,0:T(8,128)}) fusion(s32[512]{0:T(512)} %param.12), kind=kLoop, calls=%fused_computation.20 | loop fusion | flops 1048576 | bytes 526336 | tf_op jit(solution)/shard_map/mul | solution.py:185
  3.3 2.6 %fusion.16 = (f32[512,8]{1,0:T(8,128)}, f32[512,8]{1,0:T(8,128)}) fusion(s32[8]{0:T(128)S(1)} %iota_multiply_fusion, s32[512]{0:T(512)} %param.12), kind=kLoop, calls=%fused_computation.30 | loop fusion | flops 57344 | bytes 34848 | tf_op jit(solution)/shard_map/sin | solution.py:185
  5.9 1.1 fusion.18
  7.0 4.9 %collective-permute-start = (bf16[1,3,4,1,1024]{4,3,2,1,0:T(2,128)(2,1)S(1)}, bf16[1,3,4,1,1024]{4,3,2,1,0:T(2,128)(2,1)S(1)}, u32[]{:S(2)}, u32[]{:S(2)}) collective-permute-start(bf16[1,3,4,1,1024]{4,3,2,1,0:T(2,128)(2,1)S(1)} %get-tuple-element.24), channel_id=1, source_target_pairs={{0,4},{4,8},{8,12},{1,5},{5,9},{9,13},{2,6},{6,10},{10,14},{3,7},{... | collective-permute-start | bytes 73736 | tf_op jit(solution)/shard_map/ppermute | solution.py:572
  11.9 1.3 collective-permute-start.1
  13.2 3.9 %shard_map.122 = bf16[2,8,2,32,1024]{4,3,2,1,0:T(8,128)(2,1)} custom-call(f32[512,8]{1,0:T(8,128)} %get-tuple-element.26.ca_ref, f32[512,8]{1,0:T(8,128)} %get-tuple-element.27.sa_ref, f32[512,128]{1,0:T(8,128)} %get-tuple-element.28.cb_ref, f32[512,128]{1,0:T(8,128)} %get-tuple-element.29.sb_ref), custom_call_target="tpu_custom_call" | custom-call | tf_op jit(solution)/shard_map/pallas_call | solution.py:574
  17.1 0.0 collective-permute-done
  17.1 0.8 collective-permute-done.1
  17.9 0.0 copy-done.10
  17.9 0.6 copy-done.11
  18.5 9.2 %shard_map.123 = (bf16[512,1536]{1,0:T(8,128)(2,1)}, bf16[512,1536]{1,0:T(8,128)(2,1)}) custom-call(bf16[3,4,128,1024]{3,2,1,0:T(8,128)(2,1)} %bitcast.24, bf16[3,4,128,1024]{3,2,1,0:T(8,128)(2,1)} %bitcast.25, bf16[3,4,1,1024]{3,2,1,0:T(2,128)(2,1)} %bitcast.28, bf16[3,4,1,1024]{3,2,1,0:T(2,128)(2,1)} %bitcast.29, bf16[1024,1024]{1,0:T(8,128)(2,1)} %bitcast.18), custom_call_target="tpu_custom_call" | custom-call | flops 3221225472 | bytes 6291456 | tf_op jit(solution)/shard_map/pallas_call | solution.py:229
  27.7 42.7 %all_to_all.25 = bf16[8,64,1536]{2,1,0:T(8,128)(2,1)} all-to-all(bf16[8,64,1536]{2,1,0:T(8,128)(2,1)} %bitcast.23), channel_id=1, replica_groups=mesh['groups'=2,'wide'=4,'lev'=2,'fld'=2] {'wide','lev'}, dimensions={0} | all-to-all | bytes 3145728 | tf_op jit(solution)/shard_map/all_to_all | solution.py:583
  70.4 0.0 copy-start.4
  70.4 3.7 %all-to-all-start = ((bf16[8,64,1536]{2,1,0:T(8,128)(2,1)}), bf16[8,64,1536]{2,1,0:T(8,128)(2,1)S(1)}, u32[]{:S(2)}, u32[]{:S(2)}) async-start(bf16[8,64,1536]{2,1,0:T(8,128)(2,1)} %bitcast.5), calls=%async_computation | async-start | bytes 3145728 | tf_op jit(solution)/shard_map/all_to_all | solution.py:583
  74.2 0.0 copy-done.5
  74.2 0.1 copy.53
  74.3 0.1 copy.52
  74.5 0.0 copy-done.6
  74.5 0.1 copy.51
  74.6 0.0 copy-done.8
  74.6 0.1 copy.55
  74.7 0.1 reduce
  74.8 0.8 dynamic-slice_bitcast_fusion
  75.6 0.7 copy.57.wave_ref
  76.3 0.0 copy-done.7
  76.3 0.6 pad.9.w_out_ref
  76.9 0.1 convert_reduce_fusion
  77.0 0.1 reduce-precision_convert_fusion
  77.1 0.8 fusion.15.w_in_ref
  77.9 0.0 copy-done.4
  77.9 0.9 broadcast_multiply_fusion.w_mid_ref
  78.8 22.3 %shard_map.124 = (f32[12288,128]{1,0:T(8,128)}, bf16[8,1,2,3,2,32,128]{6,5,4,3,2,1,0:T(8,128)(2,1)}, bf16[8,2,2,3,2,32,128]{6,5,4,3,2,1,0:T(8,128)(2,1)}) custom-call(f32[3,8]{1,0:T(4,128)} %rates_ref.3, f32[8,8]{1,0:T(8,128)} %modes_ref.3, s32[64,1]{1,0:T(8,128)} %copy.57.wave_ref, bf16[8,2,32,1536]{3,2,1,0:T(8,128)(2,1)} %bitcast.22, ...), custom_call_target="tpu_custom_call" | custom-call | flops 16106127360 | bytes 16777216 | tf_op jit(solution)/shard_map/pallas_call | solution.py:417
  101.1 9.5 %all-to-all-done = bf16[8,64,1536]{2,1,0:T(8,128)(2,1)S(1)} async-done(((bf16[8,64,1536]{2,1,0:T(8,128)(2,1)}), bf16[8,64,1536]{2,1,0:T(8,128)(2,1)S(1)}, u32[]{:S(2)}, u32[]{:S(2)}) %all-to-all-start) | async-done | bytes 1572896 | tf_op jit(solution)/shard_map/all_to_all | solution.py:583
  110.6 3.6 %all-to-all-start.3 = ((bf16[8,1,2,3,2,32,128]{6,5,4,3,2,1,0:T(8,128)(2,1)}), bf16[8,1,2,3,2,32,128]{6,5,4,3,2,1,0:T(8,128)(2,1)S(1)}, u32[]{:S(2)}, u32[]{:S(2)}) async-start(bf16[8,1,2,3,2,32,128]{6,5,4,3,2,1,0:T(8,128)(2,1)} %get-tuple-element.42), calls=%async_computation.3 | async-start | bytes 1572864 | tf_op jit(solution)/shard_map/all_to_all | solution.py:583
  114.3 0.0 copy-done
  114.3 0.0 copy-start.9
  114.3 22.4 %shard_map.125 = (f32[12288,128]{1,0:T(8,128)}, bf16[8,1,2,3,2,32,128]{6,5,4,3,2,1,0:T(8,128)(2,1)}, bf16[8,2,2,3,2,32,128]{6,5,4,3,2,1,0:T(8,128)(2,1)}) custom-call(f32[3,8]{1,0:T(4,128)} %rates_ref.3, f32[8,8]{1,0:T(8,128)} %modes_ref.3, s32[64,1]{1,0:T(8,128)} %copy.57.wave_ref, ...), custom_call_target="tpu_custom_call", output_to_operand_aliasing={{0}: (5, {}), {2}: (6, {})} | custom-call | flops 16106127360 | bytes 16777216 | tf_op jit(solution)/shard_map/pallas_call | solution.py:417
  136.7 0.0 all-to-all-done.3.rest_0_
  136.7 6.0 %all-to-all-start.4 = ((bf16[8,1,2,3,2,32,128]{6,5,4,3,2,1,0:T(8,128)(2,1)}), bf16[8,1,2,3,2,32,128]{6,5,4,3,2,1,0:T(8,128)(2,1)S(1)}, u32[]{:S(2)}, u32[]{:S(2)}) async-start(bf16[8,1,2,3,2,32,128]{6,5,4,3,2,1,0:T(8,128)(2,1)} %get-tuple-element.45), calls=%async_computation.4 | async-start | bytes 1572864 | tf_op jit(solution)/shard_map/all_to_all | solution.py:583
  142.7 0.0 copy-done.9
  142.7 0.7 copy.60.gain_ref
  143.4 0.6 fusion.19
  144.0 18.5 %all-to-all-done.4.rest_1_ = bf16[8,1,2,3,2,32,128]{6,5,4,3,2,1,0:T(8,128)(2,1)S(1)} async-done(((bf16[8,1,2,3,2,32,128]{6,5,4,3,2,1,0:T(8,128)(2,1)}), bf16[8,1,2,3,2,32,128]{6,5,4,3,2,1,0:T(8,128)(2,1)S(1)}, u32[]{:S(2)}, u32[]{:S(2)}) %all-to-all-start.4) | async-done | bytes 786464 | tf_op jit(solution)/shard_map/all_to_all | solution.py:583
  162.6 3.8 %all-to-all-start.2 = ((bf16[8,2,2,3,2,32,128]{6,5,4,3,2,1,0:T(8,128)(2,1)}), bf16[8,2,2,3,2,32,128]{6,5,4,3,2,1,0:T(8,128)(2,1)S(1)}, u32[]{:S(2)}, u32[]{:S(2)}) async-start(bf16[8,2,2,3,2,32,128]{6,5,4,3,2,1,0:T(8,128)(2,1)} %get-tuple-element.41), calls=%async_computation.2 | async-start | bytes 3145728 | tf_op jit(solution)/shard_map/all_to_all | solution.py:583
  166.4 44.6 %shard_map.126.rest_1_ = bf16[24,64,1024]{2,1,0:T(8,128)(2,1)} custom-call(s32[32]{0:T(128)} %get-tuple-element.55.band_ref, bf16[1024,1024]{1,0:T(8,128)(2,1)} %bitcast.19, bf16[512,80]{1,0:T(8,128)(2,1)} %fusion.15.w_in_ref, bf16[512,512]{1,0:T(8,128)(2,1)} %broadcast_multiply_fusion.w_mid_ref, bf16[32,512]{1,0:T(8,128)(2,1)} %pad.9.w_out_ref, ...), custom_call_target="tpu_custom_call" | custom-call | flops 35970351104 | bytes 3145728 | tf_op jit(solution)/shard_map/pallas_call | solution.py:532
  211.0 0.0 all-to-all-done.2.rest_0_
  211.0 1.1 copy-done.1
  212.1 44.6 %shard_map.127 = bf16[24,64,1024]{2,1,0:T(8,128)(2,1)} custom-call(s32[32]{0:T(128)} %get-tuple-element.56.band_ref, bf16[1024,1024]{1,0:T(8,128)(2,1)} %bitcast.20, bf16[512,80]{1,0:T(8,128)(2,1)} %fusion.15.w_in_ref, bf16[512,512]{1,0:T(8,128)(2,1)} %broadcast_multiply_fusion.w_mid_ref, ...), custom_call_target="tpu_custom_call", output_to_operand_aliasing={{}: (7, {})} | custom-call | flops 35970351104 | bytes 3145728 | tf_op jit(solution)/shard_map/pallas_call | solution.py:532
  (16 shorter events, 0.1 us)
Async XLA Ops:
  7.0 10.1 %collective-permute-start = (bf16[1,3,4,1,1024]{4,3,2,1,0:T(2,128)(2,1)S(1)}, bf16[1,3,4,1,1024]{4,3,2,1,0:T(2,128)(2,1)S(1)}, u32[]{:S(2)}, u32[]{:S(2)}) collective-permute-start(bf16[1,3,4,1,1024]{4,3,2,1,0:T(2,128)(2,1)S(1)} %get-tuple-element.24), channel_id=1, source_target_pairs={{0,4},{4,8},{8,12},{1,5},{5,9},{9,13},{2,6},{6,10},{10,14},{3,7},{... | collective-permute-start | bytes 73736 | tf_op jit(solution)/shard_map/ppermute | solution.py:572
  11.9 6.0 %collective-permute-start.1 = (bf16[1,3,4,1,1024]{4,3,2,1,0:T(2,128)(2,1)S(1)}, bf16[1,3,4,1,1024]{4,3,2,1,0:T(2,128)(2,1)S(1)}, u32[]{:S(2)}, u32[]{:S(2)}) collective-permute-start(bf16[1,3,4,1,1024]{4,3,2,1,0:T(2,128)(2,1)S(1)} %get-tuple-element.25), channel_id=1, source_target_pairs={{4,0},{8,4},{12,8},{5,1},{9,5},{13,9},{6,2},{10,6},{14,10},{7,3},{... | collective-permute-start | bytes 73736 | tf_op jit(solution)/shard_map/ppermute | solution.py:573
  17.1 0.8 copy-start.10
  17.9 0.6 copy-start.11
  70.4 3.8 %copy-start.5 = (f32[512,16]{0,1:T(8,128)S(1)}, f32[512,16]{0,1:T(8,128)}, u32[]{:S(2)}) copy-start(f32[512,16]{0,1:T(8,128)} %param.19) | copy-start | bytes 98308
  70.4 4.0 %copy-start.6 = (bf16[512,24]{0,1:T(8,128)(2,1)S(1)}, bf16[512,24]{0,1:T(8,128)(2,1)}, u32[]{:S(2)}) copy-start(bf16[512,24]{0,1:T(8,128)(2,1)} %param.18) | copy-start | bytes 73732
  70.4 4.2 %copy-start.8 = (s32[16]{0:T(128)S(1)}, s32[16]{0:T(128)}, u32[]{:S(2)}) copy-start(s32[16]{0:T(128)} %param.16) | copy-start | bytes 196
  70.4 5.9 %copy-start.7 = (bf16[24,512]{1,0:T(8,128)(2,1)S(1)}, bf16[24,512]{1,0:T(8,128)(2,1)}, u32[]{:S(2)}) copy-start(bf16[24,512]{1,0:T(8,128)(2,1)} %param.21) | copy-start | bytes 73732
  70.4 7.5 %copy-start.4 = (bf16[512,512]{1,0:T(8,128)(2,1)S(1)}, bf16[512,512]{1,0:T(8,128)(2,1)}, u32[]{:S(2)}) copy-start(bf16[512,512]{1,0:T(8,128)(2,1)} %param.20) | copy-start | bytes 1572868
  70.4 40.2 %all-to-all-start = ((bf16[8,64,1536]{2,1,0:T(8,128)(2,1)}), bf16[8,64,1536]{2,1,0:T(8,128)(2,1)S(1)}, u32[]{:S(2)}, u32[]{:S(2)}) async-start(bf16[8,64,1536]{2,1,0:T(8,128)(2,1)} %bitcast.5), calls=%async_computation | async-start | bytes 3145728 | tf_op jit(solution)/shard_map/all_to_all | solution.py:583
  110.6 3.6 %copy-start = (bf16[8,64,1536]{2,1,0:T(8,128)(2,1)}, bf16[8,64,1536]{2,1,0:T(8,128)(2,1)S(1)}, u32[]{:S(2)}) copy-start(bf16[8,64,1536]{2,1,0:T(8,128)(2,1)S(1)} %all-to-all-done) | copy-start | bytes 4718596
  110.6 26.1 %all-to-all-start.3 = ((bf16[8,1,2,3,2,32,128]{6,5,4,3,2,1,0:T(8,128)(2,1)}), bf16[8,1,2,3,2,32,128]{6,5,4,3,2,1,0:T(8,128)(2,1)S(1)}, u32[]{:S(2)}, u32[]{:S(2)}) async-start(bf16[8,1,2,3,2,32,128]{6,5,4,3,2,1,0:T(8,128)(2,1)} %get-tuple-element.42), calls=%async_computation.3 | async-start | bytes 1572864 | tf_op jit(solution)/shard_map/all_to_all | solution.py:583
  114.3 28.4 %copy-start.9 = (f32[24]{0:T(128)S(1)}, f32[24]{0:T(128)}, u32[]{:S(2)}) copy-start(f32[24]{0:T(128)} %param.17) | copy-start | bytes 292
  136.7 25.9 %copy-start.2 = (bf16[8,1,2,3,2,32,128]{6,5,4,3,2,1,0:T(8,128)(2,1)}, bf16[8,1,2,3,2,32,128]{6,5,4,3,2,1,0:T(8,128)(2,1)S(1)}, u32[]{:S(2)}) copy-start(bf16[8,1,2,3,2,32,128]{6,5,4,3,2,1,0:T(8,128)(2,1)S(1)} %all-to-all-done.3.rest_0_) | copy-start | bytes 2359300
  136.7 25.9 %all-to-all-start.4 = ((bf16[8,1,2,3,2,32,128]{6,5,4,3,2,1,0:T(8,128)(2,1)}), bf16[8,1,2,3,2,32,128]{6,5,4,3,2,1,0:T(8,128)(2,1)S(1)}, u32[]{:S(2)}, u32[]{:S(2)}) async-start(bf16[8,1,2,3,2,32,128]{6,5,4,3,2,1,0:T(8,128)(2,1)} %get-tuple-element.45), calls=%async_computation.4 | async-start | bytes 1572864 | tf_op jit(solution)/shard_map/all_to_all | solution.py:583
  162.6 3.8 %copy-start.3 = (bf16[8,1,2,3,2,32,128]{6,5,4,3,2,1,0:T(8,128)(2,1)}, bf16[8,1,2,3,2,32,128]{6,5,4,3,2,1,0:T(8,128)(2,1)S(1)}, u32[]{:S(2)}) copy-start(bf16[8,1,2,3,2,32,128]{6,5,4,3,2,1,0:T(8,128)(2,1)S(1)} %all-to-all-done.4.rest_1_) | copy-start | bytes 2359300
  162.6 48.4 %all-to-all-start.2 = ((bf16[8,2,2,3,2,32,128]{6,5,4,3,2,1,0:T(8,128)(2,1)}), bf16[8,2,2,3,2,32,128]{6,5,4,3,2,1,0:T(8,128)(2,1)S(1)}, u32[]{:S(2)}, u32[]{:S(2)}) async-start(bf16[8,2,2,3,2,32,128]{6,5,4,3,2,1,0:T(8,128)(2,1)} %get-tuple-element.41), calls=%async_computation.2 | async-start | bytes 3145728 | tf_op jit(solution)/shard_map/all_to_all | solution.py:583
  211.0 1.1 copy-start.1

commit v3 on v2

--- a/solution.py
+++ b/solution.py
@@ -172,58 +172,83 @@
 VMEM_BYTES = 58 * 2**20
 
 
-def angle_parts(slot_waves, lon_count):
+FINE = 16
+
+
+def angle_parts(wave_slots, lon_count):
     coarse = jnp.arange(lon_count // LANES, dtype=jnp.int32) * LANES
-    fine = jnp.arange(LANES, dtype=jnp.int32)
-
-    def angles(longitude):
-        phase = slot_waves[:, None] * longitude[None, :] % lon_count
-        return phase.astype(jnp.float32) * (2.0 * math.pi / lon_count)
-
-    a, b = angles(coarse), angles(fine)
+    middle = jnp.arange(LANES // FINE, dtype=jnp.int32) * FINE
+    fine = jnp.arange(FINE, dtype=jnp.int32)
+    longitude = jnp.concatenate([coarse, middle, fine])
+    phase = longitude[:, None] * wave_slots[None, :]
+    phase = jnp.concatenate([phase, phase + (lon_count - lon_count // 4)], axis=0) % lon_count
+    return jnp.cos(phase.astype(jnp.float32) * (2.0 * math.pi / lon_count))
+
+
+def table_kernel(chunk, parts_ref, out_ref):
+    devices, _, per, lon_count = out_ref.shape
+    tiles, pieces = lon_count // LANES, LANES // FINE
+    count = parts_ref.shape[0] // 2
+    apart = parts_ref.shape[1] // devices
+    both = parts_ref[...].T
+    both = jnp.concatenate(
+        [both[d * apart + chunk * per : d * apart + (chunk + 1) * per] for d in range(devices)], axis=0
+    )
+    cos_parts, sin_parts = both[:, :count], both[:, count:]
+    part = lax.broadcasted_iota(jnp.int32, (count, 2 * LANES), 0)
+    lane = lax.broadcasted_iota(jnp.int32, (count, 2 * LANES), 1)
+    wanted = jnp.where(
+        lane < LANES, tiles + lax.div(lane, FINE), tiles + pieces + lax.rem(lane, FINE)
+    )
+    spread = jnp.where(part == wanted, 1.0, 0.0)
+    cos_spread = jnp.dot(cos_parts, spread, precision=lax.Precision.HIGHEST)
+    sin_spread = jnp.dot(sin_parts, spread, precision=lax.Precision.HIGHEST)
+    cm, cf = cos_spread[:, :LANES], cos_spread[:, LANES:]
+    sm, sf = sin_spread[:, :LANES], sin_spread[:, LANES:]
     scale = 1.0 / math.sqrt(lon_count)
-    return jnp.cos(a), jnp.sin(a), jnp.cos(b) * scale, jnp.sin(b) * scale
-
-
-def table_kernel(ca_ref, sa_ref, cb_ref, sb_ref, out_ref):
-    tiles = ca_ref.shape[1]
-    chunks, devices, _, per, _ = out_ref.shape
-    cb, sb = cb_ref[...], sb_ref[...]
+    cb, sb = (cm * cf - sm * sf) * scale, (sm * cf + cm * sf) * scale
     for t in range(tiles):
-        ca, sa = ca_ref[:, t : t + 1], sa_ref[:, t : t + 1]
+        ca, sa = cos_parts[:, t : t + 1], sin_parts[:, t : t + 1]
         cosine = (ca * cb - sa * sb).astype(jnp.bfloat16)
         minus_sine = (-(sa * cb + ca * sb)).astype(jnp.bfloat16)
         cols = slice(t * LANES, (t + 1) * LANES)
         for d in range(devices):
-            for c in range(chunks):
-                first = (d * chunks + c) * per
-                out_ref[c, d, 0, :, cols] = cosine[first : first + per]
-                out_ref[c, d, 1, :, cols] = minus_sine[first : first + per]
-
-
-def fourier_kernel(x_ref, next_ref, before_ref, after_ref, table_ref, *out_refs):
+            out_ref[d, 0, :, cols] = cosine[d * per : (d + 1) * per]
+            out_ref[d, 1, :, cols] = minus_sine[d * per : (d + 1) * per]
+
+
+def table_of(angles, devices, lon_count, chunk, chunks):
+    slots = angles.shape[1] // chunks
+    return pl.pallas_call(
+        functools.partial(table_kernel, chunk),
+        out_shape=jax.ShapeDtypeStruct((devices, 2, slots // devices, lon_count), jnp.bfloat16),
+        compiler_params=pltpu.CompilerParams(vmem_limit_bytes=VMEM_BYTES),
+    )(angles).reshape(2 * slots, lon_count)
+
+
+def fourier_kernel(x_ref, next_ref, before_ref, after_ref, table_ref, out_ref):
     _, levels, rows, _ = x_ref.shape
-    parts = []
     row = lax.broadcasted_iota(jnp.int32, (rows, 1), 0)
-    for l in range(levels):
+
+    def advected(l):
         x = x_ref[0, l].astype(jnp.float32)
         up = jnp.where(row == rows - 1, after_ref[0, l].astype(jnp.float32), pltpu.roll(x, rows - 1, 0))
         down = jnp.where(row == 0, before_ref[0, l].astype(jnp.float32), pltpu.roll(x, 1, 0))
         mixed = x + transport_speed * next_ref[0, l].astype(jnp.float32) * (up - down)
-        parts.append(mixed.astype(jnp.bfloat16))
-    advected = jnp.concatenate(parts, axis=0)
-    coeffs = lax.dot_general(
-        table_ref[...], advected, (((1,), (1,)), ((), ())), preferred_element_type=jnp.float32
-    ).astype(jnp.bfloat16)
-    rows = coeffs.shape[0] // len(out_refs)
-    for c, out_ref in enumerate(out_refs):
-        out_ref[...] = coeffs[c * rows : (c + 1) * rows]
-
-
-def fourier(grid_state, before, after, table, chunks):
+        return mixed.astype(jnp.bfloat16)
+
+    pair = 2 if levels % 2 == 0 else 1
+    for first in range(0, levels, pair):
+        both = jnp.concatenate([advected(first + l) for l in range(pair)], axis=0)
+        out_ref[:, first * rows : (first + pair) * rows] = lax.dot_general(
+            table_ref[...], both, (((1,), (1,)), ((), ())), preferred_element_type=jnp.float32
+        ).astype(jnp.bfloat16)
+
+
+def fourier(grid_state, before, after, table):
     _, fields, lev_dev, lat_dev, lon_count = grid_state.shape
     x, before, after = grid_state[0], before[0], after[0]
-    pair = 2 if lev_dev % 2 == 0 else 1
+    pair = lev_dev if lev_dev <= 4 else 1
     rows = table.shape[0]
     halves = lev_dev // pair
     return pl.pallas_call(
@@ -236,8 +261,8 @@
             pl.BlockSpec((1, pair, 1, lon_count), lambda f, h: (f, h, 0, 0)),
             pl.BlockSpec((rows, lon_count), lambda f, h: (0, 0)),
         ],
-        out_specs=[pl.BlockSpec((rows // chunks, pair * lat_dev), lambda f, h: (0, f * halves + h))] * chunks,
-        out_shape=[jax.ShapeDtypeStruct((rows // chunks, fields * lev_dev * lat_dev), jnp.bfloat16)] * chunks,
+        out_specs=pl.BlockSpec((rows, pair * lat_dev), lambda f, h: (0, f * halves + h)),
+        out_shape=jax.ShapeDtypeStruct((rows, fields * lev_dev * lat_dev), jnp.bfloat16),
         compiler_params=pltpu.CompilerParams(vmem_limit_bytes=VMEM_BYTES),
         cost_estimate=pl.CostEstimate(
             flops=2 * rows * lon_count * fields * lev_dev * lat_dev,
@@ -449,34 +474,25 @@
 
 
 def column_kernel(
-    shape, band_ref, table_ref, w_in_ref, w_mid_ref, w_out_ref, gain_ref, *rest
+    shape, band_ref, w_in_ref, w_mid_ref, w_out_ref, gain_ref, *rest
 ):
-    fields, levels, jw, padded, count = shape
-    y_refs, (out_ref, grid_ref, done_ref) = rest[:count], rest[-3:]
+    fields, levels, jw, padded, chunks, count = shape
+    table_refs, y_refs = rest[:chunks], rest[chunks : chunks + count]
+    out_ref, grid_ref, done_ref = rest[-3:]
     features = fields * levels
     subs = y_refs[0].shape[2]
-    lon_count = table_ref.shape[1]
+    lon_count = table_refs[0].shape[1]
     lon_tiles = lon_count // LANES
     bands = (w_in_ref.shape[1] - padded) // 3
     row = lax.broadcasted_iota(jnp.int32, (3 * bands, lon_count), 0)
     for sub in range(subs):
-        lhs = jnp.concatenate(
-            [
-                jnp.concatenate(
-                    [
-                        y_ref[:, c, sub, f].reshape(-1, LANES)
-                        for y_ref in y_refs
-                        for c in range(y_ref.shape[1])
-                    ],
-                    axis=0,
-                )
-                for f in range(fields)
-            ],
-            axis=1,
-        )
-        grid_mid = lax.dot_general(
-            lhs, table_ref[...], (((0,), (0,)), ((), ())), preferred_element_type=jnp.float32
-        )
+        pieces = [(y_ref, c) for y_ref in y_refs for c in range(y_ref.shape[1])]
+        grid_mid = 0.0
+        for (y_ref, c), table_ref in zip(pieces, table_refs):
+            lhs = jnp.concatenate([y_ref[:, c, sub, f].reshape(-1, LANES) for f in range(fields)], axis=1)
+            grid_mid = grid_mid + lax.dot_general(
+                lhs, table_ref[...], (((0,), (0,)), ((), ())), preferred_element_type=jnp.float32
+            )
         grid_mid = grid_mid.astype(jnp.bfloat16).astype(jnp.float32)
         for t in range(lon_tiles):
             grid_ref[t] = grid_mid[:, t * LANES : (t + 1) * LANES]
@@ -504,24 +520,24 @@
                 done_ref[t, where, :] = result[:, t * LANES : (t + 1) * LANES]
             return carry
 
-        lax.fori_loop(0, jw, one_row, 0)
+        lax.fori_loop(0, jw, one_row, 0, unroll=4)
         for t in range(lon_tiles):
             out_ref[:, sub * jw : (sub + 1) * jw, t * LANES : (t + 1) * LANES] = (
                 done_ref[t].reshape(features, jw, LANES).astype(jnp.bfloat16)
             )
 
 
-def column_part(arrived, table, bands_here, weights, so_far, first, lat_quarter, dims):
+def column_part(arrived, tables, bands_here, weights, so_far, first, lat_quarter, dims):
     fields, levels, jw = dims
     w_in, w_mid, w_out, gain = weights
     padded = w_out.shape[0]
     subs = arrived[0].shape[2]
     features = fields * levels
-    depth, lon_count = table.shape
+    depth, lon_count = sum(t.shape[0] for t in tables), tables[0].shape[1]
     rows = subs * jw
     whole = pl.BlockSpec(memory_space=pltpu.VMEM)
-    args = [bands_here, table, w_in, w_mid, w_out, gain] + list(arrived)
-    specs = [pl.BlockSpec(memory_space=pltpu.SMEM)] + [whole] * (5 + len(arrived))
+    args = [bands_here, w_in, w_mid, w_out, gain] + list(tables) + list(arrived)
+    specs = [pl.BlockSpec(memory_space=pltpu.SMEM)] + [whole] * (len(args) - 1)
     aliases = {}
     if so_far is not None:
         args.append(so_far)
@@ -530,7 +546,7 @@
     block = first // rows
     units = w_mid.shape[0]
     return pl.pallas_call(
-        functools.partial(column_kernel, (fields, levels, jw, padded, len(arrived))),
+        functools.partial(column_kernel, (fields, levels, jw, padded, len(tables), len(arrived))),
         grid=(1,),
         in_specs=specs,
         out_specs=pl.BlockSpec((features, rows, lon_count), lambda g: (0, block, 0)),
@@ -564,25 +580,19 @@
     block_index = lax.axis_index("wide") * lev_count + lax.axis_index("lev")
 
     chunks = 2 if slot_dev % (2 * PACK) == 0 else 1
-    angle_arrays = angle_parts(wave_slots, lon_count)
+    angles = angle_parts(wave_slots, lon_count)
     edges = (grid_state[:, :, :, lat_dev - 1 :], grid_state[:, :, :, :1])
-    edges, angle_arrays = lax.optimization_barrier((edges, angle_arrays))
+    edges, angles = lax.optimization_barrier((edges, angles))
     up = [(i, i + 1) for i in range(wide_count - 1)]
     down = [(j, i) for i, j in up]
     before = lax.ppermute(edges[0], "wide", up)
     after = lax.ppermute(edges[1], "wide", down)
-    table = pl.pallas_call(
-        table_kernel,
-        out_shape=jax.ShapeDtypeStruct(
-            (chunks, devices, 2, slot_dev // chunks, lon_count), jnp.bfloat16
-        ),
-        compiler_params=pltpu.CompilerParams(vmem_limit_bytes=VMEM_BYTES),
-    )(*angle_arrays).reshape(devices * 2 * slot_dev, lon_count)
+    tables = [table_of(angles, devices, lon_count, c, chunks) for c in range(chunks)]
 
     def exchange(parcel):
         return lax.all_to_all(parcel, ("wide", "lev"), split_axis=0, concat_axis=0, tiled=True)
 
-    coeffs = fourier(grid_state, before, after, table, chunks)
+    coeffs = [fourier(grid_state, before, after, table) for table in tables]
     received = [exchange(c.reshape(devices, -1, c.shape[1])) for c in coeffs]
     wave_part = lax.dynamic_slice_in_dim(wave_slots, block_index * slot_dev, slot_dev)
     count = 2 if subs % 2 == 0 else 1
@@ -628,7 +638,7 @@
         arrived = [exchange(so_far[1 + index])] if index else arrived_first
         rows = slice(part[0] * jw, (part[-1] + 1) * jw)
         new_state = column_part(
-            arrived, table, bands_here[rows], weights, new_state, part[0] * jw, lat_quarter, (fields, levels, jw)
+            arrived, tables, bands_here[rows], weights, new_state, part[0] * jw, lat_quarter, (fields, levels, jw)
         )
     return spectral, new_state.reshape(1, fields, levels, lat_quarter, lon_count)
 

time: 257 us -> 244 us (0.949)
  blocking collectives: 42.7 us -> 0 us
  waiting for transfers between devices: 28.8 us -> 52.7 us
  starting transfers between devices: 23.3 us -> 28.2 us
    all_to_all x1 -> x0, blocking collectives: 42.7 us -> none  [exchange(): lax.all_to_all(parcel, ('wide', 'lev'), split_axis=0, concat_axis=0, tile...]
    all_to_all x4 -> x5, waiting for transfers between devices: 28 us -> 50.9 us  [exchange(): lax.all_to_all(parcel, ('wide', 'lev'), split_axis=0, concat_axis=0, tile...]
    pallas_call x2, Pallas kernels: 89.3 us -> 81.7 us  [column_part(): pl.pallas_call(functools.partial(column_kernel, (fields, levels, jw, padd...]
    pallas_call x1 -> x2, Pallas kernels: 9.22 us -> 14.4 us  [fourier(): pl.pallas_call(fourier_kernel, grid=(fields, halves), in_specs=[pl.BlockS...]
    all_to_all x4 -> x5, starting transfers between devices: 17.1 us -> 21.9 us  [exchange(): lax.all_to_all(parcel, ('wide', 'lev'), split_axis=0, concat_axis=0, tile...]
    sin x1 -> x0, other arithmetic: 2.59 us -> none  [angle_parts(): return (jnp.cos(a), jnp.sin(a), jnp.cos(b) * scale, jnp.sin(b) * scale)]
    pallas_call x1 -> x2, Pallas kernels: 3.88 us -> 5.76 us  [table_of(): pl.pallas_call(functools.partial(table_kernel, chunk), out_shape=jax.Shap...]
  transfers between devices with their start and end apart: 6 -> 7, of which waited for: 3 -> 4; matrix products, arithmetic and copies ran while one was open for 2% -> 4% of each run, Pallas kernels for 36% -> 40%
where the time goes in v3:
time: 244 us; the launch traced here: 243 us
  Pallas kernels  146 us (60%)
  waiting for transfers between devices  52.7 us (22%)
  starting transfers between devices  28.2 us (12%)
  local copies, waits for them, and re-layouts  8.96 us (4%)
  other arithmetic  6.08 us (2%)
    pallas_call x2, Pallas kernels, column_part(): pl.pallas_call(functools.partial(column_kernel, (fields, levels, jw, padd...  81.7 us
    all_to_all x5, waiting for transfers between devices, exchange(): lax.all_to_all(parcel, ('wide', 'lev'), split_axis=0, concat_axis=0, tile...  50.9 us
    pallas_call x2, Pallas kernels, legendre(): pl.pallas_call(functools.partial(legendre_kernel, (fields, levels, lev_de...  44.7 us
    all_to_all x5, starting transfers between devices, exchange(): lax.all_to_all(parcel, ('wide', 'lev'), split_axis=0, concat_axis=0, tile...  21.9 us
    pallas_call x2, Pallas kernels, fourier(): pl.pallas_call(fourier_kernel, grid=(fields, halves), in_specs=[pl.BlockS...  14.4 us
    pallas_call x2, Pallas kernels, table_of(): pl.pallas_call(functools.partial(table_kernel, chunk), out_shape=jax.Shap...  5.76 us
    ppermute x1, starting transfers between devices, local_tiled(): before = lax.ppermute(edges[0], 'wide', up)  4.92 us
  transfers between devices with their start and end apart: 7, of which 4 were waited for; matrix products, arithmetic and copies ran while one was open for 4% of the time, Pallas kernels for 40%

profile of v3, /device:TPU:0, one launch (start us, length us, event | category | flops | bytes accessed | tf_op | source)
XLA Modules:
  0.0 243.2 jit_solution(11411800764825744125)
XLA Ops:
  0.6 1.1 fusion.11
  1.8 0.1 pad_add_fusion
  1.8 0.8 broadcast_multiply_fusion.1
  2.6 1.1 fusion.6.parts_ref
  3.7 4.9 %collective-permute-start = (bf16[1,3,4,1,1024]{4,3,2,1,0:T(2,128)(2,1)S(1)}, bf16[1,3,4,1,1024]{4,3,2,1,0:T(2,128)(2,1)S(1)}, u32[]{:S(2)}, u32[]{:S(2)}) collective-permute-start(bf16[1,3,4,1,1024]{4,3,2,1,0:T(2,128)(2,1)S(1)} %get-tuple-element.19), channel_id=1, source_target_pairs={{0,4},{4,8},{8,12},{1,5},{5,9},{9,13},{2,6},{6,10},{10,14},{3,7},{... | collective-permute-start | bytes 73736 | tf_op jit(solution)/shard_map/ppermute | solution.py:588
  8.7 1.3 collective-permute-start.1
  10.0 2.9 %shard_map.124 = bf16[8,2,32,1024]{3,2,1,0:T(8,128)(2,1)} custom-call(f32[64,512]{1,0:T(8,128)} %fusion.6.parts_ref), custom_call_target="tpu_custom_call" | custom-call | tf_op jit(solution)/shard_map/pallas_call | solution.py:222
  12.8 0.0 collective-permute-done
  12.8 1.8 collective-permute-done.1
  14.7 0.0 copy-done.5
  14.7 0.6 copy-done.6
  15.3 7.2 %shard_map.125 = bf16[512,1536]{1,0:T(8,128)(2,1)} custom-call(bf16[3,4,128,1024]{3,2,1,0:T(8,128)(2,1)} %bitcast.19, bf16[3,4,128,1024]{3,2,1,0:T(8,128)(2,1)} %bitcast.20, bf16[3,4,1,1024]{3,2,1,0:T(2,128)(2,1)} %bitcast.33, bf16[3,4,1,1024]{3,2,1,0:T(2,128)(2,1)} %bitcast.35, bf16[512,1024]{1,0:T(8,128)(2,1)} %bitcast.25), custom_call_target="tpu_custom_call" | custom-call | flops 1610612736 | bytes 3145728 | tf_op jit(solution)/shard_map/pallas_call | solution.py:254
  22.4 5.1 %all-to-all-start.1 = ((bf16[8,64,1536]{2,1,0:T(8,128)(2,1)}), bf16[8,64,1536]{2,1,0:T(8,128)(2,1)S(1)}, u32[]{:S(2)}, u32[]{:S(2)}) async-start(bf16[8,64,1536]{2,1,0:T(8,128)(2,1)} %bitcast.24), calls=%async_computation.1 | async-start | bytes 3145728 | tf_op jit(solution)/shard_map/all_to_all | solution.py:593
  27.5 2.9 %shard_map.122 = bf16[8,2,32,1024]{3,2,1,0:T(8,128)(2,1)} custom-call(f32[64,512]{1,0:T(8,128)} %fusion.6.parts_ref), custom_call_target="tpu_custom_call" | custom-call | tf_op jit(solution)/shard_map/pallas_call | solution.py:222
  30.4 7.2 %shard_map.123 = bf16[512,1536]{1,0:T(8,128)(2,1)} custom-call(bf16[3,4,128,1024]{3,2,1,0:T(8,128)(2,1)} %bitcast.21, bf16[3,4,128,1024]{3,2,1,0:T(8,128)(2,1)} %bitcast.22, bf16[3,4,1,1024]{3,2,1,0:T(2,128)(2,1)} %bitcast.34, bf16[3,4,1,1024]{3,2,1,0:T(2,128)(2,1)} %bitcast.36, bf16[512,1024]{1,0:T(8,128)(2,1)} %bitcast.28), custom_call_target="tpu_custom_call" | custom-call | flops 1610612736 | bytes 3145728 | tf_op jit(solution)/shard_map/pallas_call | solution.py:254
  37.6 26.4 %all-to-all-done.1 = bf16[8,64,1536]{2,1,0:T(8,128)(2,1)S(1)} async-done(((bf16[8,64,1536]{2,1,0:T(8,128)(2,1)}), bf16[8,64,1536]{2,1,0:T(8,128)(2,1)S(1)}, u32[]{:S(2)}, u32[]{:S(2)}) %all-to-all-start.1) | async-done | bytes 1572896 | tf_op jit(solution)/shard_map/all_to_all | solution.py:593
  64.0 3.6 %all-to-all-start = ((bf16[8,64,1536]{2,1,0:T(8,128)(2,1)}), bf16[8,64,1536]{2,1,0:T(8,128)(2,1)S(1)}, u32[]{:S(2)}, u32[]{:S(2)}) async-start(bf16[8,64,1536]{2,1,0:T(8,128)(2,1)} %bitcast.23), calls=%async_computation | async-start | bytes 3145728 | tf_op jit(solution)/shard_map/all_to_all | solution.py:593
  67.6 0.0 copy-done.7
  67.7 0.1 copy.59
  67.8 0.8 copy.58
  68.6 0.9 copy.57
  69.5 0.0 copy-done.8
  69.5 0.1 copy.61
  69.6 0.1 reduce
  69.7 0.8 dynamic-slice_bitcast_fusion
  70.5 0.7 copy.63.wave_ref
  71.2 1.3 pad.9.w_out_ref
  72.6 0.1 convert_reduce_fusion
  72.7 1.1 reduce-precision_convert_fusion
  73.7 0.8 fusion.10.w_in_ref
  74.6 1.9 broadcast_multiply_fusion.w_mid_ref
  76.5 0.0 copy-done.1
  76.5 22.3 %shard_map.126 = (f32[12288,128]{1,0:T(8,128)}, bf16[8,1,2,3,2,32,128]{6,5,4,3,2,1,0:T(8,128)(2,1)}, bf16[8,2,2,3,2,32,128]{6,5,4,3,2,1,0:T(8,128)(2,1)}) custom-call(f32[3,8]{1,0:T(4,128)} %rates_ref.3, f32[8,8]{1,0:T(8,128)} %modes_ref.3, s32[64,1]{1,0:T(8,128)} %copy.63.wave_ref, bf16[8,2,32,1536]{3,2,1,0:T(8,128)(2,1)} %bitcast.32, ...), custom_call_target="tpu_custom_call" | custom-call | flops 16106127360 | bytes 16777216 | tf_op jit(solution)/shard_map/pallas_call | solution.py:442
  98.8 6.0 %all-to-all-done = bf16[8,64,1536]{2,1,0:T(8,128)(2,1)S(1)} async-done(((bf16[8,64,1536]{2,1,0:T(8,128)(2,1)}), bf16[8,64,1536]{2,1,0:T(8,128)(2,1)S(1)}, u32[]{:S(2)}, u32[]{:S(2)}) %all-to-all-start) | async-done | bytes 1572896 | tf_op jit(solution)/shard_map/all_to_all | solution.py:593
  104.8 3.7 %all-to-all-start.3 = ((bf16[8,1,2,3,2,32,128]{6,5,4,3,2,1,0:T(8,128)(2,1)}), bf16[8,1,2,3,2,32,128]{6,5,4,3,2,1,0:T(8,128)(2,1)S(1)}, u32[]{:S(2)}, u32[]{:S(2)}) async-start(bf16[8,1,2,3,2,32,128]{6,5,4,3,2,1,0:T(8,128)(2,1)} %get-tuple-element.32), calls=%async_computation.3 | async-start | bytes 1572864 | tf_op jit(solution)/shard_map/all_to_all | solution.py:593
  108.6 0.0 copy-start.9
  108.6 22.4 %shard_map.127 = (f32[12288,128]{1,0:T(8,128)}, bf16[8,1,2,3,2,32,128]{6,5,4,3,2,1,0:T(8,128)(2,1)}, bf16[8,2,2,3,2,32,128]{6,5,4,3,2,1,0:T(8,128)(2,1)}) custom-call(f32[3,8]{1,0:T(4,128)} %rates_ref.3, f32[8,8]{1,0:T(8,128)} %modes_ref.3, s32[64,1]{1,0:T(8,128)} %copy.63.wave_ref, ...), custom_call_target="tpu_custom_call", output_to_operand_aliasing={{0}: (5, {}), {2}: (6, {})} | custom-call | flops 16106127360 | bytes 16777216 | tf_op jit(solution)/shard_map/pallas_call | solution.py:442
  131.0 0.0 all-to-all-done.3.rest_2_
  131.0 5.9 %all-to-all-start.4 = ((bf16[8,1,2,3,2,32,128]{6,5,4,3,2,1,0:T(8,128)(2,1)}), bf16[8,1,2,3,2,32,128]{6,5,4,3,2,1,0:T(8,128)(2,1)S(1)}, u32[]{:S(2)}, u32[]{:S(2)}) async-start(bf16[8,1,2,3,2,32,128]{6,5,4,3,2,1,0:T(8,128)(2,1)} %get-tuple-element.35), calls=%async_computation.4 | async-start | bytes 1572864 | tf_op jit(solution)/shard_map/all_to_all | solution.py:593
  136.9 0.0 copy-done.9
  136.9 0.7 copy.66.gain_ref
  137.6 0.6 fusion.12
  138.2 18.5 %all-to-all-done.4.rest_3_ = bf16[8,1,2,3,2,32,128]{6,5,4,3,2,1,0:T(8,128)(2,1)S(1)} async-done(((bf16[8,1,2,3,2,32,128]{6,5,4,3,2,1,0:T(8,128)(2,1)}), bf16[8,1,2,3,2,32,128]{6,5,4,3,2,1,0:T(8,128)(2,1)S(1)}, u32[]{:S(2)}, u32[]{:S(2)}) %all-to-all-start.4) | async-done | bytes 786464 | tf_op jit(solution)/shard_map/all_to_all | solution.py:593
  156.8 3.6 %all-to-all-start.2 = ((bf16[8,2,2,3,2,32,128]{6,5,4,3,2,1,0:T(8,128)(2,1)}), bf16[8,2,2,3,2,32,128]{6,5,4,3,2,1,0:T(8,128)(2,1)S(1)}, u32[]{:S(2)}, u32[]{:S(2)}) async-start(bf16[8,2,2,3,2,32,128]{6,5,4,3,2,1,0:T(8,128)(2,1)} %get-tuple-element.31), calls=%async_computation.2 | async-start | bytes 3145728 | tf_op jit(solution)/shard_map/all_to_all | solution.py:593
  160.4 40.7 %shard_map.128.rest_3_ = bf16[24,64,1024]{2,1,0:T(8,128)(2,1)} custom-call(s32[32]{0:T(128)} %get-tuple-element.43.band_ref, bf16[512,80]{1,0:T(8,128)(2,1)} %fusion.10.w_in_ref, bf16[512,512]{1,0:T(8,128)(2,1)} %broadcast_multiply_fusion.w_mid_ref, bf16[32,512]{1,0:T(8,128)(2,1)} %pad.9.w_out_ref, f32[24,1]{1,0:T(8,128)} %copy.66.gain_ref, ...), custom_call_target="tpu_custom_call" | custom-call | flops 35970351104 | bytes 3145728 | tf_op jit(solution)/shard_map/pallas_call | solution.py:548
  201.1 0.0 all-to-all-done.2.rest_2_
  201.1 1.2 copy-done.2
  202.2 41.0 %shard_map.129 = bf16[24,64,1024]{2,1,0:T(8,128)(2,1)} custom-call(s32[32]{0:T(128)} %get-tuple-element.44.band_ref, bf16[512,80]{1,0:T(8,128)(2,1)} %fusion.10.w_in_ref, bf16[512,512]{1,0:T(8,128)(2,1)} %broadcast_multiply_fusion.w_mid_ref, bf16[32,512]{1,0:T(8,128)(2,1)} %pad.9.w_out_ref, f32[24,1]{1,0:T(8,128)} %copy.66.gain_ref, ...), custom_call_target="tpu_custom_call", output_to_operand_aliasing={{}: (8, {})} | custom-call | flops 35970351104 | bytes 3145728 | tf_op jit(solution)/shard_map/pallas_call | solution.py:548
  (17 shorter events, 0.1 us)
Async XLA Ops:
  3.7 9.1 %collective-permute-start = (bf16[1,3,4,1,1024]{4,3,2,1,0:T(2,128)(2,1)S(1)}, bf16[1,3,4,1,1024]{4,3,2,1,0:T(2,128)(2,1)S(1)}, u32[]{:S(2)}, u32[]{:S(2)}) collective-permute-start(bf16[1,3,4,1,1024]{4,3,2,1,0:T(2,128)(2,1)S(1)} %get-tuple-element.19), channel_id=1, source_target_pairs={{0,4},{4,8},{8,12},{1,5},{5,9},{9,13},{2,6},{6,10},{10,14},{3,7},{... | collective-permute-start | bytes 73736 | tf_op jit(solution)/shard_map/ppermute | solution.py:588
  8.7 6.0 %collective-permute-start.1 = (bf16[1,3,4,1,1024]{4,3,2,1,0:T(2,128)(2,1)S(1)}, bf16[1,3,4,1,1024]{4,3,2,1,0:T(2,128)(2,1)S(1)}, u32[]{:S(2)}, u32[]{:S(2)}) collective-permute-start(bf16[1,3,4,1,1024]{4,3,2,1,0:T(2,128)(2,1)S(1)} %get-tuple-element.20), channel_id=1, source_target_pairs={{4,0},{8,4},{12,8},{5,1},{9,5},{13,9},{6,2},{10,6},{14,10},{7,3},{... | collective-permute-start | bytes 73736 | tf_op jit(solution)/shard_map/ppermute | solution.py:589
  12.8 1.8 copy-start.5
  14.7 0.6 copy-start.6
  22.4 41.5 %all-to-all-start.1 = ((bf16[8,64,1536]{2,1,0:T(8,128)(2,1)}), bf16[8,64,1536]{2,1,0:T(8,128)(2,1)S(1)}, u32[]{:S(2)}, u32[]{:S(2)}) async-start(bf16[8,64,1536]{2,1,0:T(8,128)(2,1)} %bitcast.24), calls=%async_computation.1 | async-start | bytes 3145728 | tf_op jit(solution)/shard_map/all_to_all | solution.py:593
  37.6 30.0 %copy-start.7 = (f32[512,16]{0,1:T(8,128)S(1)}, f32[512,16]{0,1:T(8,128)}, u32[]{:S(2)}) copy-start(f32[512,16]{0,1:T(8,128)} %param.19) | copy-start | bytes 98308
  37.6 31.9 %copy-start.8 = (s32[16]{0:T(128)S(1)}, s32[16]{0:T(128)}, u32[]{:S(2)}) copy-start(s32[16]{0:T(128)} %param.16) | copy-start | bytes 196
  64.0 12.5 %copy-start.1 = (bf16[8,64,1536]{2,1,0:T(8,128)(2,1)}, bf16[8,64,1536]{2,1,0:T(8,128)(2,1)S(1)}, u32[]{:S(2)}) copy-start(bf16[8,64,1536]{2,1,0:T(8,128)(2,1)S(1)} %all-to-all-done.1) | copy-start | bytes 4718596
  64.0 40.8 %all-to-all-start = ((bf16[8,64,1536]{2,1,0:T(8,128)(2,1)}), bf16[8,64,1536]{2,1,0:T(8,128)(2,1)S(1)}, u32[]{:S(2)}, u32[]{:S(2)}) async-start(bf16[8,64,1536]{2,1,0:T(8,128)(2,1)} %bitcast.23), calls=%async_computation | async-start | bytes 3145728 | tf_op jit(solution)/shard_map/all_to_all | solution.py:593
  104.8 3.7 %copy-start = (bf16[8,64,1536]{2,1,0:T(8,128)(2,1)}, bf16[8,64,1536]{2,1,0:T(8,128)(2,1)S(1)}, u32[]{:S(2)}) copy-start(bf16[8,64,1536]{2,1,0:T(8,128)(2,1)S(1)} %all-to-all-done) | copy-start | bytes 4718596
  104.8 26.2 %all-to-all-start.3 = ((bf16[8,1,2,3,2,32,128]{6,5,4,3,2,1,0:T(8,128)(2,1)}), bf16[8,1,2,3,2,32,128]{6,5,4,3,2,1,0:T(8,128)(2,1)S(1)}, u32[]{:S(2)}, u32[]{:S(2)}) async-start(bf16[8,1,2,3,2,32,128]{6,5,4,3,2,1,0:T(8,128)(2,1)} %get-tuple-element.32), calls=%async_computation.3 | async-start | bytes 1572864 | tf_op jit(solution)/shard_map/all_to_all | solution.py:593
  108.6 28.3 %copy-start.9 = (f32[24]{0:T(128)S(1)}, f32[24]{0:T(128)}, u32[]{:S(2)}) copy-start(f32[24]{0:T(128)} %param.17) | copy-start | bytes 292
  131.0 29.4 %copy-start.3 = (bf16[8,1,2,3,2,32,128]{6,5,4,3,2,1,0:T(8,128)(2,1)}, bf16[8,1,2,3,2,32,128]{6,5,4,3,2,1,0:T(8,128)(2,1)S(1)}, u32[]{:S(2)}) copy-start(bf16[8,1,2,3,2,32,128]{6,5,4,3,2,1,0:T(8,128)(2,1)S(1)} %all-to-all-done.3.rest_2_) | copy-start | bytes 2359300
  131.0 25.8 %all-to-all-start.4 = ((bf16[8,1,2,3,2,32,128]{6,5,4,3,2,1,0:T(8,128)(2,1)}), bf16[8,1,2,3,2,32,128]{6,5,4,3,2,1,0:T(8,128)(2,1)S(1)}, u32[]{:S(2)}, u32[]{:S(2)}) async-start(bf16[8,1,2,3,2,32,128]{6,5,4,3,2,1,0:T(8,128)(2,1)} %get-tuple-element.35), calls=%async_computation.4 | async-start | bytes 1572864 | tf_op jit(solution)/shard_map/all_to_all | solution.py:593
  156.7 3.6 %copy-start.4 = (bf16[8,1,2,3,2,32,128]{6,5,4,3,2,1,0:T(8,128)(2,1)}, bf16[8,1,2,3,2,32,128]{6,5,4,3,2,1,0:T(8,128)(2,1)S(1)}, u32[]{:S(2)}) copy-start(bf16[8,1,2,3,2,32,128]{6,5,4,3,2,1,0:T(8,128)(2,1)S(1)} %all-to-all-done.4.rest_3_) | copy-start | bytes 2359300
  156.8 44.3 %all-to-all-start.2 = ((bf16[8,2,2,3,2,32,128]{6,5,4,3,2,1,0:T(8,128)(2,1)}), bf16[8,2,2,3,2,32,128]{6,5,4,3,2,1,0:T(8,128)(2,1)S(1)}, u32[]{:S(2)}, u32[]{:S(2)}) async-start(bf16[8,2,2,3,2,32,128]{6,5,4,3,2,1,0:T(8,128)(2,1)} %get-tuple-element.31), calls=%async_computation.2 | async-start | bytes 3145728 | tf_op jit(solution)/shard_map/all_to_all | solution.py:593
  201.1 1.2 copy-start.2

commit v4 on v3

--- a/solution.py
+++ b/solution.py
@@ -169,7 +169,7 @@
 
 LANES = 128
 PACK = 16
-VMEM_BYTES = 58 * 2**20
+VMEM_BYTES = 32 * 2**20
 
 
 FINE = 16
@@ -262,7 +262,7 @@
             pl.BlockSpec((rows, lon_count), lambda f, h: (0, 0)),
         ],
         out_specs=pl.BlockSpec((rows, pair * lat_dev), lambda f, h: (0, f * halves + h)),
-        out_shape=jax.ShapeDtypeStruct((rows, fields * lev_dev * lat_dev), jnp.bfloat16),
+        out_shape=pltpu.HBM((rows, fields * lev_dev * lat_dev), jnp.bfloat16),
         compiler_params=pltpu.CompilerParams(vmem_limit_bytes=VMEM_BYTES),
         cost_estimate=pl.CostEstimate(
             flops=2 * rows * lon_count * fields * lev_dev * lat_dev,
@@ -452,9 +452,9 @@
         + [pl.BlockSpec(memory_space=pl.ANY)] * len(aliases),
         out_specs=[pl.BlockSpec((group * per_slot, LANES), lambda g: (first + g, 0))]
         + [part_spec(i, p) for i, p in enumerate(parts)],
-        out_shape=[jax.ShapeDtypeStruct((slots * per_slot, LANES), jnp.float32)]
+        out_shape=[pltpu.HBM((slots * per_slot, LANES), jnp.float32)]
         + [
-            jax.ShapeDtypeStruct(
+            pltpu.HBM(
                 (devices, chunks if i else 1, len(p), fields, 2, here, LANES), jnp.bfloat16
             )
             for i, p in enumerate(parts)
@@ -474,17 +474,21 @@
 
 
 def column_kernel(
-    shape, band_ref, w_in_ref, w_mid_ref, w_out_ref, gain_ref, *rest
+    shape, scalars_ref, w_in_ref, w_deep_ref, *rest
 ):
     fields, levels, jw, padded, chunks, count = shape
     table_refs, y_refs = rest[:chunks], rest[chunks : chunks + count]
-    out_ref, grid_ref, done_ref = rest[-3:]
+    out_ref, grid_ref, done_ref, gain_ref = rest[-4:]
     features = fields * levels
+    for i in range(features):
+        gain_ref[i : i + 1, :] = jnp.full((1, LANES), scalars_ref[i])
     subs = y_refs[0].shape[2]
     lon_count = table_refs[0].shape[1]
     lon_tiles = lon_count // LANES
     bands = (w_in_ref.shape[1] - padded) // 3
-    row = lax.broadcasted_iota(jnp.int32, (3 * bands, lon_count), 0)
+    row = lax.rem(lax.broadcasted_iota(jnp.int32, (3 * bands, lon_count), 0), bands).astype(jnp.float32)
+    units = w_in_ref.shape[0]
+    gain = jnp.concatenate([gain_ref[...]] * lon_tiles, axis=1)
     for sub in range(subs):
         pieces = [(y_ref, c) for y_ref in y_refs for c in range(y_ref.shape[1])]
         grid_mid = 0.0
@@ -501,20 +505,20 @@
             where = pl.ds(j, features, stride=jw)
             x = jnp.concatenate([grid_ref[t, where, :] for t in range(lon_tiles)], axis=1)
             mean = jnp.sum(x * x, axis=0, keepdims=True) * (1.0 / features)
-            normed = x * lax.rsqrt(mean + norm_eps) * gain_ref[...]
+            normed = x * lax.rsqrt(mean + norm_eps) * gain
             if padded > features:
                 normed = jnp.concatenate(
                     [normed, jnp.zeros((padded - features, lon_count), jnp.float32)], axis=0
                 )
-            chosen = lax.rem(row, bands) == band_ref[sub * jw + j]
+            chosen = row == scalars_ref[features + sub * jw + j]
             entries = jnp.concatenate(
                 [normed.astype(jnp.bfloat16), jnp.where(chosen, 1.0, 0.0).astype(jnp.bfloat16)], axis=0
             )
             half = jnp.dot(w_in_ref[...], entries, preferred_element_type=jnp.float32)
             hidden = (half * jnp.tanh(half) + half).astype(jnp.bfloat16)
-            half = jnp.dot(w_mid_ref[...], hidden, preferred_element_type=jnp.float32)
+            half = jnp.dot(w_deep_ref[:units], hidden, preferred_element_type=jnp.float32)
             hidden = (half * jnp.tanh(half) + half).astype(jnp.bfloat16)
-            grown = jnp.dot(w_out_ref[...], hidden, preferred_element_type=jnp.float32)
+            grown = jnp.dot(w_deep_ref[units:], hidden, preferred_element_type=jnp.float32)
             result = x + grown[:features]
             for t in range(lon_tiles):
                 done_ref[t, where, :] = result[:, t * LANES : (t + 1) * LANES]
@@ -529,14 +533,16 @@
 
 def column_part(arrived, tables, bands_here, weights, so_far, first, lat_quarter, dims):
     fields, levels, jw = dims
-    w_in, w_mid, w_out, gain = weights
-    padded = w_out.shape[0]
+    w_in, w_deep, gain = weights
+    units = w_in.shape[0]
+    padded = w_deep.shape[0] - units
+    scalars = jnp.concatenate([gain, bands_here.astype(jnp.float32)])
     subs = arrived[0].shape[2]
     features = fields * levels
     depth, lon_count = sum(t.shape[0] for t in tables), tables[0].shape[1]
     rows = subs * jw
     whole = pl.BlockSpec(memory_space=pltpu.VMEM)
-    args = [bands_here, w_in, w_mid, w_out, gain] + list(tables) + list(arrived)
+    args = [scalars, w_in, w_deep] + list(tables) + list(arrived)
     specs = [pl.BlockSpec(memory_space=pltpu.SMEM)] + [whole] * (len(args) - 1)
     aliases = {}
     if so_far is not None:
@@ -544,7 +550,6 @@
         specs.append(pl.BlockSpec(memory_space=pl.ANY))
         aliases = {len(args) - 1: 0}
     block = first // rows
-    units = w_mid.shape[0]
     return pl.pallas_call(
         functools.partial(column_kernel, (fields, levels, jw, padded, len(tables), len(arrived))),
         grid=(1,),
@@ -555,6 +560,7 @@
         scratch_shapes=[
             pltpu.VMEM((lon_count // LANES, features * jw, LANES), jnp.float32),
             pltpu.VMEM((lon_count // LANES, features * jw, LANES), jnp.float32),
+            pltpu.VMEM((features, LANES), jnp.float32),
         ],
         compiler_params=pltpu.CompilerParams(vmem_limit_bytes=VMEM_BYTES),
         cost_estimate=pl.CostEstimate(
@@ -582,7 +588,6 @@
     chunks = 2 if slot_dev % (2 * PACK) == 0 else 1
     angles = angle_parts(wave_slots, lon_count)
     edges = (grid_state[:, :, :, lat_dev - 1 :], grid_state[:, :, :, :1])
-    edges, angles = lax.optimization_barrier((edges, angles))
     up = [(i, i + 1) for i in range(wide_count - 1)]
     down = [(j, i) for i, j in up]
     before = lax.ppermute(edges[0], "wide", up)
@@ -618,9 +623,8 @@
     ) * half
     weights = (
         w_first,
-        w_mid * half,
-        jnp.pad(w_out, ((0, padded - features), (0, 0))),
-        norm_gain[:, None],
+        jnp.concatenate([w_mid * half, jnp.pad(w_out, ((0, padded - features), (0, 0)))], axis=0),
+        norm_gain,
     )
     received[0], weights, bands_here = lax.optimization_barrier((received[0], weights, bands_here))
     so_far, arrived_first = None, []

time: 244 us -> 239 us (0.980)
  Pallas kernels: 146 us -> 132 us
  waiting for transfers between devices: 52.7 us -> 64.7 us
  other arithmetic: 6.08 us -> 2.71 us
    all_to_all x5, waiting for transfers between devices: 50.9 us -> 62.4 us  [exchange(): lax.all_to_all(parcel, ('wide', 'lev'), split_axis=0, concat_axis=0, tile...]
    pallas_call x2, Pallas kernels: 14.4 us -> 8.02 us  [fourier(): pl.pallas_call(fourier_kernel, grid=(fields, halves), in_specs=[pl.BlockS...]
    pallas_call x2, Pallas kernels: 81.7 us -> 77.1 us  [column_part(): pl.pallas_call(functools.partial(column_kernel, (fields, levels, jw, padd...]
    unnamed x22 -> x38, local copies, waits for them, and re-layouts: 2.79 us -> 7.01 us
    pallas_call x2, Pallas kernels: 5.76 us -> 1.97 us  [table_of(): pl.pallas_call(functools.partial(table_kernel, chunk), out_shape=jax.Shap...]
  transfers between devices with their start and end apart: 7 -> 7, of which waited for: 4 -> 4; matrix products, arithmetic and copies ran while one was open for 4% -> 2% of each run, Pallas kernels for 40% -> 37%
where the time goes in v4:
time: 239 us; the launch traced here: 238 us
  Pallas kernels  132 us (55%)
  waiting for transfers between devices  64.7 us (27%)
  starting transfers between devices  29.2 us (12%)
  local copies, waits for them, and re-layouts  9.18 us (4%)
  other arithmetic  2.71 us (1%)
    pallas_call x2, Pallas kernels, column_part(): pl.pallas_call(functools.partial(column_kernel, (fields, levels, jw, padd...  77.1 us
    all_to_all x5, waiting for transfers between devices, exchange(): lax.all_to_all(parcel, ('wide', 'lev'), split_axis=0, concat_axis=0, tile...  62.4 us
    pallas_call x2, Pallas kernels, legendre(): pl.pallas_call(functools.partial(legendre_kernel, (fields, levels, lev_de...  44.5 us
    all_to_all x5, starting transfers between devices, exchange(): lax.all_to_all(parcel, ('wide', 'lev'), split_axis=0, concat_axis=0, tile...  23 us
    pallas_call x2, Pallas kernels, fourier(): pl.pallas_call(fourier_kernel, grid=(fields, halves), in_specs=[pl.BlockS...  8.02 us
    unnamed x38, local copies, waits for them, and re-layouts  7.01 us
    ppermute x1, starting transfers between devices, local_tiled(): before = lax.ppermute(edges[0], 'wide', up)  4.93 us
  transfers between devices with their start and end apart: 7, of which 4 were waited for; matrix products, arithmetic and copies ran while one was open for 2% of the time, Pallas kernels for 37%

profile of v4, /device:TPU:0, one launch (start us, length us, event | category | flops | bytes accessed | tf_op | source)
XLA Modules:
  0.0 238.3 jit_solution(2754304171516957678)
XLA Ops:
  0.6 1.1 fusion.13
  1.7 4.9 %collective-permute-start = (bf16[1,3,4,1,1024]{4,3,2,1,0:T(2,128)(2,1)S(1)}, bf16[1,3,4,1,1024]{4,3,2,1,0:T(2,128)(2,1)S(1)}, u32[]{:S(2)}, u32[]{:S(2)}) collective-permute-start(bf16[1,3,4,1,1024]{4,3,2,1,0:T(2,128)(2,1)S(1)} %get-tuple-element.29), channel_id=1, source_target_pairs={{0,4},{4,8},{8,12},{1,5},{5,9},{9,13},{2,6},{6,10},{10,14},{3,7},{... | collective-permute-start | bytes 73736 | tf_op jit(solution)/shard_map/ppermute | solution.py:593
  6.7 1.3 collective-permute-start.1
  8.0 0.1 pad_add_fusion
  8.1 0.8 broadcast_multiply_fusion.1
  8.8 0.5 fusion.8.parts_ref
  9.3 1.0 shard_map.124
  10.3 0.0 collective-permute-done
  10.3 2.3 collective-permute-done.1
  12.7 1.9 copy-done
  14.5 4.0 %shard_map.125 = bf16[512,1536]{1,0:T(8,128)(2,1)} custom-call(bf16[3,4,128,1024]{3,2,1,0:T(8,128)(2,1)S(1)} %bitcast.18, bf16[3,4,128,1024]{3,2,1,0:T(8,128)(2,1)S(1)} %bitcast.19, bf16[3,4,1,1024]{3,2,1,0:T(2,128)(2,1)S(1)} %bitcast.29, bf16[3,4,1,1024]{3,2,1,0:T(2,128)(2,1)S(1)} %bitcast.31, bf16[512,1024]{1,0:T(8,128)(2,1)S(1)} %bitcast.22), custom_call_target="tpu_custom_call" | custom-call | flops 1610612736 | bytes 3145728 | tf_op jit(solution)/shard_map/pallas_call | solution.py:254
  18.6 5.2 %all-to-all-start.1 = ((bf16[8,64,1536]{2,1,0:T(8,128)(2,1)}), bf16[8,64,1536]{2,1,0:T(8,128)(2,1)}, u32[]{:S(2)}, u32[]{:S(2)}) async-start(bf16[8,64,1536]{2,1,0:T(8,128)(2,1)} %bitcast.34), calls=%async_computation.1 | async-start | bytes 3145728 | tf_op jit(solution)/shard_map/all_to_all | solution.py:598
  23.7 1.0 shard_map.122
  24.7 4.0 %shard_map.123 = bf16[512,1536]{1,0:T(8,128)(2,1)} custom-call(bf16[3,4,128,1024]{3,2,1,0:T(8,128)(2,1)S(1)} %bitcast.20, bf16[3,4,128,1024]{3,2,1,0:T(8,128)(2,1)S(1)} %bitcast.21, bf16[3,4,1,1024]{3,2,1,0:T(2,128)(2,1)S(1)} %bitcast.30, bf16[3,4,1,1024]{3,2,1,0:T(2,128)(2,1)S(1)} %bitcast.32, bf16[512,1024]{1,0:T(8,128)(2,1)S(1)} %bitcast.25), custom_call_target="tpu_custom_call" | custom-call | flops 1610612736 | bytes 3145728 | tf_op jit(solution)/shard_map/pallas_call | solution.py:254
  28.8 1.0 copy-done.4
  29.8 30.5 %all-to-all-done.1 = bf16[8,64,1536]{2,1,0:T(8,128)(2,1)} async-done(((bf16[8,64,1536]{2,1,0:T(8,128)(2,1)}), bf16[8,64,1536]{2,1,0:T(8,128)(2,1)}, u32[]{:S(2)}, u32[]{:S(2)}) %all-to-all-start.1) | async-done | bytes 1572896 | tf_op jit(solution)/shard_map/all_to_all | solution.py:598
  60.3 3.8 %all-to-all-start = ((bf16[8,64,1536]{2,1,0:T(8,128)(2,1)}), bf16[8,64,1536]{2,1,0:T(8,128)(2,1)S(1)}, u32[]{:S(2)}, u32[]{:S(2)}) async-start(bf16[8,64,1536]{2,1,0:T(8,128)(2,1)} %bitcast.33), calls=%async_computation | async-start | bytes 3145728 | tf_op jit(solution)/shard_map/all_to_all | solution.py:598
  64.1 0.0 copy-start.12
  64.1 0.1 copy.53
  64.2 0.0 copy-start.15
  64.2 0.1 copy.52
  64.4 0.1 copy.51
  64.5 0.1 copy.55
  64.6 0.1 reduce
  64.8 0.8 dynamic-slice_bitcast_fusion
  65.5 0.1 copy.57.wave_ref
  65.6 0.1 convert_reduce_fusion
  65.7 0.1 reduce-precision_convert_fusion
  65.8 0.0 copy-start.10
  65.8 0.0 copy-start.11
  65.8 0.8 fusion.12.w_in_ref
  66.8 22.3 %shard_map.126 = (f32[12288,128]{1,0:T(8,128)}, bf16[8,1,2,3,2,32,128]{6,5,4,3,2,1,0:T(8,128)(2,1)}, bf16[8,2,2,3,2,32,128]{6,5,4,3,2,1,0:T(8,128)(2,1)}) custom-call(f32[3,8]{1,0:T(4,128)S(1)} %copy-done.11, f32[8,8]{1,0:T(8,128)S(1)} %copy-done.10, s32[64,1]{1,0:T(8,128)S(1)} %copy.57.wave_ref, bf16[8,2,32,1536]{3,2,1,0:T(8,128)(2,1)} %bitcast.10.x_ref, ...), custom_call_target="tpu_custom_call" | custom-call | flops 16106127360 | bytes 16777216 | tf_op jit(solution)/shard_map/pallas_call | solution.py:442
  89.1 12.1 %all-to-all-done = bf16[8,64,1536]{2,1,0:T(8,128)(2,1)S(1)} async-done(((bf16[8,64,1536]{2,1,0:T(8,128)(2,1)}), bf16[8,64,1536]{2,1,0:T(8,128)(2,1)S(1)}, u32[]{:S(2)}, u32[]{:S(2)}) %all-to-all-start) | async-done | bytes 1572896 | tf_op jit(solution)/shard_map/all_to_all | solution.py:598
  101.2 3.7 %all-to-all-start.3 = ((bf16[8,1,2,3,2,32,128]{6,5,4,3,2,1,0:T(8,128)(2,1)}), bf16[8,1,2,3,2,32,128]{6,5,4,3,2,1,0:T(8,128)(2,1)S(1)}, u32[]{:S(2)}, u32[]{:S(2)}) async-start(bf16[8,1,2,3,2,32,128]{6,5,4,3,2,1,0:T(8,128)(2,1)} %get-tuple-element.24), calls=%async_computation.3 | async-start | bytes 1572864 | tf_op jit(solution)/shard_map/all_to_all | solution.py:598
  105.0 22.2 %shard_map.127 = (f32[12288,128]{1,0:T(8,128)}, bf16[8,1,2,3,2,32,128]{6,5,4,3,2,1,0:T(8,128)(2,1)}, bf16[8,2,2,3,2,32,128]{6,5,4,3,2,1,0:T(8,128)(2,1)}) custom-call(f32[3,8]{1,0:T(4,128)S(1)} %copy-done.11, f32[8,8]{1,0:T(8,128)S(1)} %copy-done.10, s32[64,1]{1,0:T(8,128)S(1)} %copy.57.wave_ref, ...), custom_call_target="tpu_custom_call", output_to_operand_aliasing={{0}: (5, {}), {2}: (6, {})} | custom-call | flops 16106127360 | bytes 16777216 | tf_op jit(solution)/shard_map/pallas_call | solution.py:442
  127.1 0.0 all-to-all-done.3.rest_2_
  127.1 5.9 %all-to-all-start.4 = ((bf16[8,1,2,3,2,32,128]{6,5,4,3,2,1,0:T(8,128)(2,1)}), bf16[8,1,2,3,2,32,128]{6,5,4,3,2,1,0:T(8,128)(2,1)S(1)}, u32[]{:S(2)}, u32[]{:S(2)}) async-start(bf16[8,1,2,3,2,32,128]{6,5,4,3,2,1,0:T(8,128)(2,1)} %get-tuple-element.27), calls=%async_computation.4 | async-start | bytes 1572864 | tf_op jit(solution)/shard_map/all_to_all | solution.py:598
  133.0 0.1 slice_convert_fusion
  133.1 0.1 pad_maximum_fusion.1
  133.2 19.7 %all-to-all-done.4.rest_3_ = bf16[8,1,2,3,2,32,128]{6,5,4,3,2,1,0:T(8,128)(2,1)S(1)} async-done(((bf16[8,1,2,3,2,32,128]{6,5,4,3,2,1,0:T(8,128)(2,1)}), bf16[8,1,2,3,2,32,128]{6,5,4,3,2,1,0:T(8,128)(2,1)S(1)}, u32[]{:S(2)}, u32[]{:S(2)}) %all-to-all-start.4) | async-done | bytes 786464 | tf_op jit(solution)/shard_map/all_to_all | solution.py:598
  152.9 0.9 copy-done.6
  153.8 4.4 %all-to-all-start.2 = ((bf16[8,2,2,3,2,32,128]{6,5,4,3,2,1,0:T(8,128)(2,1)}), bf16[8,2,2,3,2,32,128]{6,5,4,3,2,1,0:T(8,128)(2,1)}, u32[]{:S(2)}, u32[]{:S(2)}) async-start(bf16[8,2,2,3,2,32,128]{6,5,4,3,2,1,0:T(8,128)(2,1)} %get-tuple-element.23), calls=%async_computation.2 | async-start | bytes 3145728 | tf_op jit(solution)/shard_map/all_to_all | solution.py:598
  158.3 0.0 copy-start.7
  158.3 1.1 copy-done.7
  159.4 0.9 copy-done.8
  160.3 38.0 %shard_map.128.rest_3_ = bf16[24,64,1024]{2,1,0:T(8,128)(2,1)} custom-call(f32[56]{0:T(128)S(1)} %get-tuple-element.35.scalars_ref, bf16[512,80]{1,0:T(8,128)(2,1)S(1)} %copy-done.8, bf16[544,512]{1,0:T(8,128)(2,1)S(1)} %fusion.1.w_deep_ref, bf16[512,1024]{1,0:T(8,128)(2,1)S(1)} %bitcast.23, bf16[512,1024]{1,0:T(8,128)(2,1)S(1)} %bitcast.26, ...), custom_call_target="tpu_custom_call" | custom-call | flops 35970351104 | bytes 3145728 | tf_op jit(solution)/shard_map/pallas_call | solution.py:553
  198.3 0.9 copy-done.9
  199.2 39.1 %shard_map.129 = bf16[24,64,1024]{2,1,0:T(8,128)(2,1)} custom-call(f32[56]{0:T(128)S(1)} %get-tuple-element.36.scalars_ref, bf16[512,80]{1,0:T(8,128)(2,1)S(1)} %copy-done.9, bf16[544,512]{1,0:T(8,128)(2,1)S(1)} %fusion.1.w_deep_ref, bf16[512,1024]{1,0:T(8,128)(2,1)S(1)} %bitcast.24, bf16[512,1024]{1,0:T(8,128)(2,1)S(1)} %bitcast.27, ...), custom_call_target="tpu_custom_call", output_to_operand_aliasing={{}: (6, {})} | custom-call | flops 35970351104 | bytes 3145728 | tf_op jit(solution)/shard_map/pallas_call | solution.py:553
  (33 shorter events, 0.2 us)
Async XLA Ops:
  1.7 8.6 %collective-permute-start = (bf16[1,3,4,1,1024]{4,3,2,1,0:T(2,128)(2,1)S(1)}, bf16[1,3,4,1,1024]{4,3,2,1,0:T(2,128)(2,1)S(1)}, u32[]{:S(2)}, u32[]{:S(2)}) collective-permute-start(bf16[1,3,4,1,1024]{4,3,2,1,0:T(2,128)(2,1)S(1)} %get-tuple-element.29), channel_id=1, source_target_pairs={{0,4},{4,8},{8,12},{1,5},{5,9},{9,13},{2,6},{6,10},{10,14},{3,7},{... | collective-permute-start | bytes 73736 | tf_op jit(solution)/shard_map/ppermute | solution.py:593
  6.7 6.0 %collective-permute-start.1 = (bf16[1,3,4,1,1024]{4,3,2,1,0:T(2,128)(2,1)S(1)}, bf16[1,3,4,1,1024]{4,3,2,1,0:T(2,128)(2,1)S(1)}, u32[]{:S(2)}, u32[]{:S(2)}) collective-permute-start(bf16[1,3,4,1,1024]{4,3,2,1,0:T(2,128)(2,1)S(1)} %get-tuple-element.28), channel_id=1, source_target_pairs={{4,0},{8,4},{12,8},{5,1},{9,5},{13,9},{6,2},{10,6},{14,10},{7,3},{... | collective-permute-start | bytes 73736 | tf_op jit(solution)/shard_map/ppermute | solution.py:594
  10.3 8.2 %copy-start.2 = (bf16[8,2,32,1024]{3,2,1,0:T(8,128)(2,1)}, bf16[8,2,32,1024]{3,2,1,0:T(8,128)(2,1)S(1)}, u32[]{:S(2)}) copy-start(bf16[8,2,32,1024]{3,2,1,0:T(8,128)(2,1)S(1)} %shard_map.124) | copy-start | bytes 3145732
  12.7 1.9 copy-start
  18.5 6.2 %copy-start.1 = (bf16[1,3,4,128,1024]{4,3,2,1,0:T(8,128)(2,1)S(1)}, bf16[1,3,4,128,1024]{4,3,2,1,0:T(8,128)(2,1)}, u32[]{:S(2)}) copy-start(bf16[1,3,4,128,1024]{4,3,2,1,0:T(8,128)(2,1)} %param.11) | copy-start | bytes 9437188
  18.6 41.7 %all-to-all-start.1 = ((bf16[8,64,1536]{2,1,0:T(8,128)(2,1)}), bf16[8,64,1536]{2,1,0:T(8,128)(2,1)}, u32[]{:S(2)}, u32[]{:S(2)}) async-start(bf16[8,64,1536]{2,1,0:T(8,128)(2,1)} %bitcast.34), calls=%async_computation.1 | async-start | bytes 3145728 | tf_op jit(solution)/shard_map/all_to_all | solution.py:598
  28.8 1.0 copy-start.4
  60.3 3.8 %copy-start.13 = (f32[512,16]{0,1:T(8,128)S(1)}, f32[512,16]{0,1:T(8,128)}, u32[]{:S(2)}) copy-start(f32[512,16]{0,1:T(8,128)} %param.19) | copy-start | bytes 98308
  60.3 4.1 %copy-start.14 = (bf16[512,24]{0,1:T(8,128)(2,1)S(1)}, bf16[512,24]{0,1:T(8,128)(2,1)}, u32[]{:S(2)}) copy-start(bf16[512,24]{0,1:T(8,128)(2,1)} %param.18) | copy-start | bytes 73732
  60.3 4.2 %copy-start.16 = (s32[16]{0:T(128)S(1)}, s32[16]{0:T(128)}, u32[]{:S(2)}) copy-start(s32[16]{0:T(128)} %param.16) | copy-start | bytes 196
  60.3 41.0 %all-to-all-start = ((bf16[8,64,1536]{2,1,0:T(8,128)(2,1)}), bf16[8,64,1536]{2,1,0:T(8,128)(2,1)S(1)}, u32[]{:S(2)}, u32[]{:S(2)}) async-start(bf16[8,64,1536]{2,1,0:T(8,128)(2,1)} %bitcast.33), calls=%async_computation | async-start | bytes 3145728 | tf_op jit(solution)/shard_map/all_to_all | solution.py:598
  64.1 2.6 %copy-start.12 = (bf16[512,512]{1,0:T(8,128)(2,1)S(1)}, bf16[512,512]{1,0:T(8,128)(2,1)}, u32[]{:S(2)}) copy-start(bf16[512,512]{1,0:T(8,128)(2,1)} %param.20) | copy-start | bytes 1572868
  64.2 2.5 %copy-start.15 = (bf16[24,512]{1,0:T(8,128)(2,1)S(1)}, bf16[24,512]{1,0:T(8,128)(2,1)}, u32[]{:S(2)}) copy-start(bf16[24,512]{1,0:T(8,128)(2,1)} %param.21) | copy-start | bytes 73732
  65.8 1.0 copy-start.10
  65.8 1.0 copy-start.11
  101.2 25.9 %all-to-all-start.3 = ((bf16[8,1,2,3,2,32,128]{6,5,4,3,2,1,0:T(8,128)(2,1)}), bf16[8,1,2,3,2,32,128]{6,5,4,3,2,1,0:T(8,128)(2,1)S(1)}, u32[]{:S(2)}, u32[]{:S(2)}) async-start(bf16[8,1,2,3,2,32,128]{6,5,4,3,2,1,0:T(8,128)(2,1)} %get-tuple-element.24), calls=%async_computation.3 | async-start | bytes 1572864 | tf_op jit(solution)/shard_map/all_to_all | solution.py:598
  127.1 6.0 %copy-start.17 = (f32[24]{0:T(128)S(1)}, f32[24]{0:T(128)}, u32[]{:S(2)}) copy-start(f32[24]{0:T(128)} %param.17) | copy-start | bytes 292
  127.1 25.8 %all-to-all-start.4 = ((bf16[8,1,2,3,2,32,128]{6,5,4,3,2,1,0:T(8,128)(2,1)}), bf16[8,1,2,3,2,32,128]{6,5,4,3,2,1,0:T(8,128)(2,1)S(1)}, u32[]{:S(2)}, u32[]{:S(2)}) async-start(bf16[8,1,2,3,2,32,128]{6,5,4,3,2,1,0:T(8,128)(2,1)} %get-tuple-element.27), calls=%async_computation.4 | async-start | bytes 1572864 | tf_op jit(solution)/shard_map/all_to_all | solution.py:598
  152.9 0.9 copy-start.6
  153.8 4.4 %copy-start.3 = (bf16[8,2,32,1024]{3,2,1,0:T(8,128)(2,1)S(1)}, bf16[8,2,32,1024]{3,2,1,0:T(8,128)(2,1)}, u32[]{:S(2)}) copy-start(bf16[8,2,32,1024]{3,2,1,0:T(8,128)(2,1)} %copy-done.2) | copy-start | bytes 3145732
  153.8 4.5 %copy-start.5 = (bf16[8,2,32,1024]{3,2,1,0:T(8,128)(2,1)S(1)}, bf16[8,2,32,1024]{3,2,1,0:T(8,128)(2,1)}, u32[]{:S(2)}) copy-start(bf16[8,2,32,1024]{3,2,1,0:T(8,128)(2,1)} %copy-done.4) | copy-start | bytes 3145732
  153.8 44.5 %all-to-all-start.2 = ((bf16[8,2,2,3,2,32,128]{6,5,4,3,2,1,0:T(8,128)(2,1)}), bf16[8,2,2,3,2,32,128]{6,5,4,3,2,1,0:T(8,128)(2,1)}, u32[]{:S(2)}, u32[]{:S(2)}) async-start(bf16[8,2,2,3,2,32,128]{6,5,4,3,2,1,0:T(8,128)(2,1)} %get-tuple-element.23), calls=%async_computation.2 | async-start | bytes 3145728 | tf_op jit(solution)/shard_map/all_to_all | solution.py:598
  158.3 1.1 copy-start.7
  159.4 0.9 copy-start.8
  198.3 0.9 copy-start.9

commit v5 on v4

--- a/solution.py
+++ b/solution.py
@@ -474,9 +474,9 @@
 
 
 def column_kernel(
-    shape, scalars_ref, w_in_ref, w_deep_ref, *rest
+    shape, scalars_ref, weights_ref, *rest
 ):
-    fields, levels, jw, padded, chunks, count = shape
+    fields, levels, jw, padded, bands, chunks, count = shape
     table_refs, y_refs = rest[:chunks], rest[chunks : chunks + count]
     out_ref, grid_ref, done_ref, gain_ref = rest[-4:]
     features = fields * levels
@@ -485,9 +485,9 @@
     subs = y_refs[0].shape[2]
     lon_count = table_refs[0].shape[1]
     lon_tiles = lon_count // LANES
-    bands = (w_in_ref.shape[1] - padded) // 3
     row = lax.rem(lax.broadcasted_iota(jnp.int32, (3 * bands, lon_count), 0), bands).astype(jnp.float32)
-    units = w_in_ref.shape[0]
+    units = weights_ref.shape[0] - padded
+    entry_cols = slice(units, units + padded + 3 * bands)
     gain = jnp.concatenate([gain_ref[...]] * lon_tiles, axis=1)
     for sub in range(subs):
         pieces = [(y_ref, c) for y_ref in y_refs for c in range(y_ref.shape[1])]
@@ -514,11 +514,11 @@
             entries = jnp.concatenate(
                 [normed.astype(jnp.bfloat16), jnp.where(chosen, 1.0, 0.0).astype(jnp.bfloat16)], axis=0
             )
-            half = jnp.dot(w_in_ref[...], entries, preferred_element_type=jnp.float32)
+            half = jnp.dot(weights_ref[:units, entry_cols], entries, preferred_element_type=jnp.float32)
             hidden = (half * jnp.tanh(half) + half).astype(jnp.bfloat16)
-            half = jnp.dot(w_deep_ref[:units], hidden, preferred_element_type=jnp.float32)
+            half = jnp.dot(weights_ref[:units, :units], hidden, preferred_element_type=jnp.float32)
             hidden = (half * jnp.tanh(half) + half).astype(jnp.bfloat16)
-            grown = jnp.dot(w_deep_ref[units:], hidden, preferred_element_type=jnp.float32)
+            grown = jnp.dot(weights_ref[units:, :units], hidden, preferred_element_type=jnp.float32)
             result = x + grown[:features]
             for t in range(lon_tiles):
                 done_ref[t, where, :] = result[:, t * LANES : (t + 1) * LANES]
@@ -533,16 +533,15 @@
 
 def column_part(arrived, tables, bands_here, weights, so_far, first, lat_quarter, dims):
     fields, levels, jw = dims
-    w_in, w_deep, gain = weights
-    units = w_in.shape[0]
-    padded = w_deep.shape[0] - units
+    w_all, gain, padded, bands = weights
+    units = w_all.shape[0] - padded
     scalars = jnp.concatenate([gain, bands_here.astype(jnp.float32)])
     subs = arrived[0].shape[2]
     features = fields * levels
     depth, lon_count = sum(t.shape[0] for t in tables), tables[0].shape[1]
     rows = subs * jw
     whole = pl.BlockSpec(memory_space=pltpu.VMEM)
-    args = [scalars, w_in, w_deep] + list(tables) + list(arrived)
+    args = [scalars, w_all] + list(tables) + list(arrived)
     specs = [pl.BlockSpec(memory_space=pltpu.SMEM)] + [whole] * (len(args) - 1)
     aliases = {}
     if so_far is not None:
@@ -551,7 +550,7 @@
         aliases = {len(args) - 1: 0}
     block = first // rows
     return pl.pallas_call(
-        functools.partial(column_kernel, (fields, levels, jw, padded, len(tables), len(arrived))),
+        functools.partial(column_kernel, (fields, levels, jw, padded, bands, len(tables), len(arrived))),
         grid=(1,),
         in_specs=specs,
         out_specs=pl.BlockSpec((features, rows, lon_count), lambda g: (0, block, 0)),
@@ -621,12 +620,13 @@
     w_first = jnp.concatenate(
         [jnp.pad(w_in, ((0, 0), (0, padded - features)))] + pieces, axis=1
     ) * half
-    weights = (
-        w_first,
-        jnp.concatenate([w_mid * half, jnp.pad(w_out, ((0, padded - features), (0, 0)))], axis=0),
-        norm_gain,
-    )
-    received[0], weights, bands_here = lax.optimization_barrier((received[0], weights, bands_here))
+    units = w_mid.shape[0]
+    w_all = jnp.zeros((units + padded, units + -(-w_first.shape[1] // LANES) * LANES), jnp.bfloat16)
+    w_all = w_all.at[:units, :units].set(w_mid * half)
+    w_all = w_all.at[units : units + features, :units].set(w_out)
+    w_all = w_all.at[:units, units : units + w_first.shape[1]].set(w_first)
+    received[0], w_all, bands_here = lax.optimization_barrier((received[0], w_all, bands_here))
+    weights = (w_all, norm_gain, padded, bands)
     so_far, arrived_first = None, []
     for c in range(chunks):
         so_far = legendre(received[c], lat_basis, wave_part, vert_modes, vert_rates, c, so_far, dims)

time: 239 us -> 236 us (0.987)
  waiting for transfers between devices: 64.7 us -> 57.6 us
  other arithmetic: 2.71 us -> 5.74 us
    all_to_all x5, waiting for transfers between devices: 62.4 us -> 55.3 us  [exchange(): lax.all_to_all(parcel, ('wide', 'lev'), split_axis=0, concat_axis=0, tile...]
    unnamed x38 -> x32, local copies, waits for them, and re-layouts: 7.01 us -> 3.2 us
    another operation x2 -> x5, other arithmetic: 0.16 us -> 3.02 us
  transfers between devices with their start and end apart: 7 -> 7, of which waited for: 4 -> 4; matrix products, arithmetic and copies ran while one was open for 2% -> 5% of each run, Pallas kernels for 37% -> 38%
where the time goes in v5:
time: 236 us; the launch traced here: 235 us
  Pallas kernels  132 us (56%)
  waiting for transfers between devices  57.6 us (24%)
  starting transfers between devices  29.6 us (13%)
  local copies, waits for them, and re-layouts  9.04 us (4%)
  other arithmetic  5.74 us (2%)
    pallas_call x2, Pallas kernels, column_part(): pl.pallas_call(functools.partial(column_kernel, (fields, levels, jw, padd...  77.7 us
    all_to_all x5, waiting for transfers between devices, exchange(): lax.all_to_all(parcel, ('wide', 'lev'), split_axis=0, concat_axis=0, tile...  55.3 us
    pallas_call x2, Pallas kernels, legendre(): pl.pallas_call(functools.partial(legendre_kernel, (fields, levels, lev_de...  44.5 us
    all_to_all x5, starting transfers between devices, exchange(): lax.all_to_all(parcel, ('wide', 'lev'), split_axis=0, concat_axis=0, tile...  23.4 us
    pallas_call x2, Pallas kernels, fourier(): pl.pallas_call(fourier_kernel, grid=(fields, halves), in_specs=[pl.BlockS...  8.02 us
    ppermute x1, starting transfers between devices, local_tiled(): before = lax.ppermute(edges[0], 'wide', up)  4.93 us
  transfers between devices with their start and end apart: 7, of which 4 were waited for; matrix products, arithmetic and copies ran while one was open for 5% of the time, Pallas kernels for 38%

profile of v5, /device:TPU:0, one launch (start us, length us, event | category | flops | bytes accessed | tf_op | source)
XLA Modules:
  0.0 235.0 jit_solution(15136657629169132821)
XLA Ops:
  0.6 1.1 fusion.12
  1.7 4.9 %collective-permute-start = (bf16[1,3,4,1,1024]{4,3,2,1,0:T(2,128)(2,1)S(1)}, bf16[1,3,4,1,1024]{4,3,2,1,0:T(2,128)(2,1)S(1)}, u32[]{:S(2)}, u32[]{:S(2)}) collective-permute-start(bf16[1,3,4,1,1024]{4,3,2,1,0:T(2,128)(2,1)S(1)} %get-tuple-element.61), channel_id=1, source_target_pairs={{0,4},{4,8},{8,12},{1,5},{5,9},{9,13},{2,6},{6,10},{10,14},{3,7},{... | collective-permute-start | bytes 73736 | tf_op jit(solution)/shard_map/ppermute | solution.py:592
  6.7 1.3 collective-permute-start.1
  8.0 0.1 pad_add_fusion
  8.1 0.8 broadcast_multiply_fusion.1
  8.8 0.5 fusion.6.parts_ref
  9.3 1.0 shard_map.124
  10.3 0.0 collective-permute-done
  10.3 2.3 collective-permute-done.1
  12.7 1.9 copy-done
  14.5 4.0 %shard_map.125 = bf16[512,1536]{1,0:T(8,128)(2,1)} custom-call(bf16[3,4,128,1024]{3,2,1,0:T(8,128)(2,1)S(1)} %bitcast.20, bf16[3,4,128,1024]{3,2,1,0:T(8,128)(2,1)S(1)} %bitcast.21, bf16[3,4,1,1024]{3,2,1,0:T(2,128)(2,1)S(1)} %bitcast.31, bf16[3,4,1,1024]{3,2,1,0:T(2,128)(2,1)S(1)} %bitcast.33, bf16[512,1024]{1,0:T(8,128)(2,1)S(1)} %bitcast.24), custom_call_target="tpu_custom_call" | custom-call | flops 1610612736 | bytes 3145728 | tf_op jit(solution)/shard_map/pallas_call | solution.py:254
  18.6 5.2 %all-to-all-start.1 = ((bf16[8,64,1536]{2,1,0:T(8,128)(2,1)}), bf16[8,64,1536]{2,1,0:T(8,128)(2,1)}, u32[]{:S(2)}, u32[]{:S(2)}) async-start(bf16[8,64,1536]{2,1,0:T(8,128)(2,1)} %bitcast.36), calls=%async_computation.1 | async-start | bytes 3145728 | tf_op jit(solution)/shard_map/all_to_all | solution.py:597
  23.7 1.0 shard_map.122
  24.7 4.0 %shard_map.123 = bf16[512,1536]{1,0:T(8,128)(2,1)} custom-call(bf16[3,4,128,1024]{3,2,1,0:T(8,128)(2,1)S(1)} %bitcast.22, bf16[3,4,128,1024]{3,2,1,0:T(8,128)(2,1)S(1)} %bitcast.23, bf16[3,4,1,1024]{3,2,1,0:T(2,128)(2,1)S(1)} %bitcast.32, bf16[3,4,1,1024]{3,2,1,0:T(2,128)(2,1)S(1)} %bitcast.34, bf16[512,1024]{1,0:T(8,128)(2,1)S(1)} %bitcast.27), custom_call_target="tpu_custom_call" | custom-call | flops 1610612736 | bytes 3145728 | tf_op jit(solution)/shard_map/pallas_call | solution.py:254
  28.8 1.0 copy-done.4
  29.8 0.0 copy-start.11
  29.8 30.5 %all-to-all-done.1 = bf16[8,64,1536]{2,1,0:T(8,128)(2,1)} async-done(((bf16[8,64,1536]{2,1,0:T(8,128)(2,1)}), bf16[8,64,1536]{2,1,0:T(8,128)(2,1)}, u32[]{:S(2)}, u32[]{:S(2)}) %all-to-all-start.1) | async-done | bytes 1572896 | tf_op jit(solution)/shard_map/all_to_all | solution.py:597
  60.3 3.6 %all-to-all-start = ((bf16[8,64,1536]{2,1,0:T(8,128)(2,1)}), bf16[8,64,1536]{2,1,0:T(8,128)(2,1)S(1)}, u32[]{:S(2)}, u32[]{:S(2)}) async-start(bf16[8,64,1536]{2,1,0:T(8,128)(2,1)} %bitcast.35), calls=%async_computation | async-start | bytes 3145728 | tf_op jit(solution)/shard_map/all_to_all | solution.py:597
  63.9 0.0 copy-start.12
  63.9 0.0 copy-start.6
  63.9 0.0 copy-start.7
  64.0 0.1 copy.53
  64.2 0.8 copy.52
  65.0 0.1 copy.51
  65.1 0.1 scatter.10
  65.2 0.6 fusion.13
  65.9 0.7 and_reduce_fusion
  66.6 1.1 reduce-precision_convert_fusion
  67.7 2.2 fusion.11
  69.8 2.2 scatter.14.weights_ref
  72.1 0.1 copy.55
  72.2 0.1 reduce.11
  72.3 0.8 dynamic-slice_bitcast_fusion
  73.1 0.1 copy.57.wave_ref
  73.2 0.1 convert_reduce_fusion
  73.3 22.3 %shard_map.126 = (f32[12288,128]{1,0:T(8,128)}, bf16[8,1,2,3,2,32,128]{6,5,4,3,2,1,0:T(8,128)(2,1)}, bf16[8,2,2,3,2,32,128]{6,5,4,3,2,1,0:T(8,128)(2,1)}) custom-call(f32[3,8]{1,0:T(4,128)S(1)} %copy-done.7, f32[8,8]{1,0:T(8,128)S(1)} %copy-done.6, s32[64,1]{1,0:T(8,128)S(1)} %copy.57.wave_ref, bf16[8,2,32,1536]{3,2,1,0:T(8,128)(2,1)} %bitcast.12.x_ref, ...), custom_call_target="tpu_custom_call" | custom-call | flops 16106127360 | bytes 16777216 | tf_op jit(solution)/shard_map/pallas_call | solution.py:442
  95.6 5.5 %all-to-all-done = bf16[8,64,1536]{2,1,0:T(8,128)(2,1)S(1)} async-done(((bf16[8,64,1536]{2,1,0:T(8,128)(2,1)}), bf16[8,64,1536]{2,1,0:T(8,128)(2,1)S(1)}, u32[]{:S(2)}, u32[]{:S(2)}) %all-to-all-start) | async-done | bytes 1572896 | tf_op jit(solution)/shard_map/all_to_all | solution.py:597
  101.1 4.4 %all-to-all-start.3 = ((bf16[8,1,2,3,2,32,128]{6,5,4,3,2,1,0:T(8,128)(2,1)}), bf16[8,1,2,3,2,32,128]{6,5,4,3,2,1,0:T(8,128)(2,1)}, u32[]{:S(2)}, u32[]{:S(2)}) async-start(bf16[8,1,2,3,2,32,128]{6,5,4,3,2,1,0:T(8,128)(2,1)} %get-tuple-element.56), calls=%async_computation.3 | async-start | bytes 1572864 | tf_op jit(solution)/shard_map/all_to_all | solution.py:597
  105.5 0.0 copy-start.13
  105.5 22.1 %shard_map.127 = (f32[12288,128]{1,0:T(8,128)}, bf16[8,1,2,3,2,32,128]{6,5,4,3,2,1,0:T(8,128)(2,1)}, bf16[8,2,2,3,2,32,128]{6,5,4,3,2,1,0:T(8,128)(2,1)}) custom-call(f32[3,8]{1,0:T(4,128)S(1)} %copy-done.7, f32[8,8]{1,0:T(8,128)S(1)} %copy-done.6, s32[64,1]{1,0:T(8,128)S(1)} %copy.57.wave_ref, ...), custom_call_target="tpu_custom_call", output_to_operand_aliasing={{0}: (5, {}), {2}: (6, {})} | custom-call | flops 16106127360 | bytes 16777216 | tf_op jit(solution)/shard_map/pallas_call | solution.py:442
  127.7 0.0 all-to-all-done.3.rest_2_
  127.7 5.8 %all-to-all-start.4 = ((bf16[8,1,2,3,2,32,128]{6,5,4,3,2,1,0:T(8,128)(2,1)}), bf16[8,1,2,3,2,32,128]{6,5,4,3,2,1,0:T(8,128)(2,1)}, u32[]{:S(2)}, u32[]{:S(2)}) async-start(bf16[8,1,2,3,2,32,128]{6,5,4,3,2,1,0:T(8,128)(2,1)} %get-tuple-element.59), calls=%async_computation.4 | async-start | bytes 1572864 | tf_op jit(solution)/shard_map/all_to_all | solution.py:597
  133.5 0.1 slice_convert_fusion
  133.6 0.1 pad_maximum_fusion.1
  133.7 19.3 %all-to-all-done.4.rest_3_ = bf16[8,1,2,3,2,32,128]{6,5,4,3,2,1,0:T(8,128)(2,1)} async-done(((bf16[8,1,2,3,2,32,128]{6,5,4,3,2,1,0:T(8,128)(2,1)}), bf16[8,1,2,3,2,32,128]{6,5,4,3,2,1,0:T(8,128)(2,1)}, u32[]{:S(2)}, u32[]{:S(2)}) %all-to-all-start.4) | async-done | bytes 786464 | tf_op jit(solution)/shard_map/all_to_all | solution.py:597
  153.0 4.3 %all-to-all-start.2 = ((bf16[8,2,2,3,2,32,128]{6,5,4,3,2,1,0:T(8,128)(2,1)}), bf16[8,2,2,3,2,32,128]{6,5,4,3,2,1,0:T(8,128)(2,1)}, u32[]{:S(2)}, u32[]{:S(2)}) async-start(bf16[8,2,2,3,2,32,128]{6,5,4,3,2,1,0:T(8,128)(2,1)} %get-tuple-element.55), calls=%async_computation.2 | async-start | bytes 3145728 | tf_op jit(solution)/shard_map/all_to_all | solution.py:597
  157.3 38.7 %shard_map.128.rest_3_ = bf16[24,64,1024]{2,1,0:T(8,128)(2,1)} custom-call(f32[56]{0:T(128)S(1)} %get-tuple-element.67.scalars_ref, bf16[544,640]{1,0:T(8,128)(2,1)S(1)} %scatter.14.weights_ref, bf16[512,1024]{1,0:T(8,128)(2,1)S(1)} %bitcast.25, bf16[512,1024]{1,0:T(8,128)(2,1)S(1)} %bitcast.28, bf16[8,1,2,3,2,32,128]{6,5,4,3,2,1,0:T(8,128)(2,1)} %all-to-all-done.3.rest_2_, ...), custom_call_target="tpu_custom_call" | custom-call | flops 35970351104 | bytes 3145728 | tf_op jit(solution)/shard_map/pallas_call | solution.py:552
  196.0 39.0 %shard_map.129 = bf16[24,64,1024]{2,1,0:T(8,128)(2,1)} custom-call(f32[56]{0:T(128)S(1)} %get-tuple-element.68.scalars_ref, bf16[544,640]{1,0:T(8,128)(2,1)S(1)} %scatter.14.weights_ref, bf16[512,1024]{1,0:T(8,128)(2,1)S(1)} %bitcast.26, bf16[512,1024]{1,0:T(8,128)(2,1)S(1)} %bitcast.29, ...), custom_call_target="tpu_custom_call", output_to_operand_aliasing={{}: (5, {})} | custom-call | flops 35970351104 | bytes 3145728 | tf_op jit(solution)/shard_map/pallas_call | solution.py:552
  (32 shorter events, 0.2 us)
Async XLA Ops:
  1.7 8.6 %collective-permute-start = (bf16[1,3,4,1,1024]{4,3,2,1,0:T(2,128)(2,1)S(1)}, bf16[1,3,4,1,1024]{4,3,2,1,0:T(2,128)(2,1)S(1)}, u32[]{:S(2)}, u32[]{:S(2)}) collective-permute-start(bf16[1,3,4,1,1024]{4,3,2,1,0:T(2,128)(2,1)S(1)} %get-tuple-element.61), channel_id=1, source_target_pairs={{0,4},{4,8},{8,12},{1,5},{5,9},{9,13},{2,6},{6,10},{10,14},{3,7},{... | collective-permute-start | bytes 73736 | tf_op jit(solution)/shard_map/ppermute | solution.py:592
  6.7 6.0 %collective-permute-start.1 = (bf16[1,3,4,1,1024]{4,3,2,1,0:T(2,128)(2,1)S(1)}, bf16[1,3,4,1,1024]{4,3,2,1,0:T(2,128)(2,1)S(1)}, u32[]{:S(2)}, u32[]{:S(2)}) collective-permute-start(bf16[1,3,4,1,1024]{4,3,2,1,0:T(2,128)(2,1)S(1)} %get-tuple-element.60), channel_id=1, source_target_pairs={{4,0},{8,4},{12,8},{5,1},{9,5},{13,9},{6,2},{10,6},{14,10},{7,3},{... | collective-permute-start | bytes 73736 | tf_op jit(solution)/shard_map/ppermute | solution.py:593
  10.3 8.2 %copy-start.2 = (bf16[8,2,32,1024]{3,2,1,0:T(8,128)(2,1)}, bf16[8,2,32,1024]{3,2,1,0:T(8,128)(2,1)S(1)}, u32[]{:S(2)}) copy-start(bf16[8,2,32,1024]{3,2,1,0:T(8,128)(2,1)S(1)} %shard_map.124) | copy-start | bytes 3145732
  12.7 1.9 copy-start
  18.5 6.2 %copy-start.1 = (bf16[1,3,4,128,1024]{4,3,2,1,0:T(8,128)(2,1)S(1)}, bf16[1,3,4,128,1024]{4,3,2,1,0:T(8,128)(2,1)}, u32[]{:S(2)}) copy-start(bf16[1,3,4,128,1024]{4,3,2,1,0:T(8,128)(2,1)} %param.17) | copy-start | bytes 9437188
  18.6 41.7 %all-to-all-start.1 = ((bf16[8,64,1536]{2,1,0:T(8,128)(2,1)}), bf16[8,64,1536]{2,1,0:T(8,128)(2,1)}, u32[]{:S(2)}, u32[]{:S(2)}) async-start(bf16[8,64,1536]{2,1,0:T(8,128)(2,1)} %bitcast.36), calls=%async_computation.1 | async-start | bytes 3145728 | tf_op jit(solution)/shard_map/all_to_all | solution.py:597
  28.8 1.0 copy-start.4
  29.8 34.1 %copy-start.8 = (bf16[512,512]{1,0:T(8,128)(2,1)S(1)}, bf16[512,512]{1,0:T(8,128)(2,1)}, u32[]{:S(2)}) copy-start(bf16[512,512]{1,0:T(8,128)(2,1)} %param.26) | copy-start | bytes 1572868
  29.8 34.2 %copy-start.9 = (f32[512,16]{0,1:T(8,128)S(1)}, f32[512,16]{0,1:T(8,128)}, u32[]{:S(2)}) copy-start(f32[512,16]{0,1:T(8,128)} %param.25) | copy-start | bytes 98308
  29.8 35.2 %copy-start.10 = (bf16[512,24]{0,1:T(8,128)(2,1)S(1)}, bf16[512,24]{0,1:T(8,128)(2,1)}, u32[]{:S(2)}) copy-start(bf16[512,24]{0,1:T(8,128)(2,1)} %param.24) | copy-start | bytes 73732
  29.8 36.1 %copy-start.14 = (s32[2]{0:T(128)S(1)}, s32[2]{0:T(128)}, u32[]{:S(2)}) copy-start(s32[2]{0:T(128)} %constant.120.clone.1) | copy-start | bytes 28
  29.8 36.8 %copy-start.11 = (bf16[24,512]{1,0:T(8,128)(2,1)S(1)}, bf16[24,512]{1,0:T(8,128)(2,1)}, u32[]{:S(2)}) copy-start(bf16[24,512]{1,0:T(8,128)(2,1)} %param.27) | copy-start | bytes 73732
  60.3 40.8 %all-to-all-start = ((bf16[8,64,1536]{2,1,0:T(8,128)(2,1)}), bf16[8,64,1536]{2,1,0:T(8,128)(2,1)S(1)}, u32[]{:S(2)}, u32[]{:S(2)}) async-start(bf16[8,64,1536]{2,1,0:T(8,128)(2,1)} %bitcast.35), calls=%async_computation | async-start | bytes 3145728 | tf_op jit(solution)/shard_map/all_to_all | solution.py:597
  63.9 8.2 %copy-start.12 = (s32[16]{0:T(128)S(1)}, s32[16]{0:T(128)}, u32[]{:S(2)}) copy-start(s32[16]{0:T(128)} %param.22) | copy-start | bytes 196
  63.9 9.4 %copy-start.6 = (f32[8,8]{1,0:T(8,128)S(1)}, f32[8,8]{1,0:T(8,128)}, u32[]{:S(2)}) copy-start(f32[8,8]{1,0:T(8,128)} %modes_ref.3) | copy-start | bytes 772
  63.9 9.3 %copy-start.7 = (f32[3,8]{1,0:T(4,128)S(1)}, f32[3,8]{1,0:T(4,128)}, u32[]{:S(2)}) copy-start(f32[3,8]{1,0:T(4,128)} %rates_ref.3) | copy-start | bytes 292
  101.1 26.6 %all-to-all-start.3 = ((bf16[8,1,2,3,2,32,128]{6,5,4,3,2,1,0:T(8,128)(2,1)}), bf16[8,1,2,3,2,32,128]{6,5,4,3,2,1,0:T(8,128)(2,1)}, u32[]{:S(2)}, u32[]{:S(2)}) async-start(bf16[8,1,2,3,2,32,128]{6,5,4,3,2,1,0:T(8,128)(2,1)} %get-tuple-element.56), calls=%async_computation.3 | async-start | bytes 1572864 | tf_op jit(solution)/shard_map/all_to_all | solution.py:597
  105.5 28.1 %copy-start.13 = (f32[24]{0:T(128)S(1)}, f32[24]{0:T(128)}, u32[]{:S(2)}) copy-start(f32[24]{0:T(128)} %param.23) | copy-start | bytes 292
  127.7 29.6 %copy-start.3 = (bf16[8,2,32,1024]{3,2,1,0:T(8,128)(2,1)S(1)}, bf16[8,2,32,1024]{3,2,1,0:T(8,128)(2,1)}, u32[]{:S(2)}) copy-start(bf16[8,2,32,1024]{3,2,1,0:T(8,128)(2,1)} %copy-done.2) | copy-start | bytes 3145732
  127.7 29.6 %copy-start.5 = (bf16[8,2,32,1024]{3,2,1,0:T(8,128)(2,1)S(1)}, bf16[8,2,32,1024]{3,2,1,0:T(8,128)(2,1)}, u32[]{:S(2)}) copy-start(bf16[8,2,32,1024]{3,2,1,0:T(8,128)(2,1)} %copy-done.4) | copy-start | bytes 3145732
  127.7 25.3 %all-to-all-start.4 = ((bf16[8,1,2,3,2,32,128]{6,5,4,3,2,1,0:T(8,128)(2,1)}), bf16[8,1,2,3,2,32,128]{6,5,4,3,2,1,0:T(8,128)(2,1)}, u32[]{:S(2)}, u32[]{:S(2)}) async-start(bf16[8,1,2,3,2,32,128]{6,5,4,3,2,1,0:T(8,128)(2,1)} %get-tuple-element.59), calls=%async_computation.4 | async-start | bytes 1572864 | tf_op jit(solution)/shard_map/all_to_all | solution.py:597
  153.0 43.0 %all-to-all-start.2 = ((bf16[8,2,2,3,2,32,128]{6,5,4,3,2,1,0:T(8,128)(2,1)}), bf16[8,2,2,3,2,32,128]{6,5,4,3,2,1,0:T(8,128)(2,1)}, u32[]{:S(2)}, u32[]{:S(2)}) async-start(bf16[8,2,2,3,2,32,128]{6,5,4,3,2,1,0:T(8,128)(2,1)} %get-tuple-element.55), calls=%async_computation.2 | async-start | bytes 3145728 | tf_op jit(solution)/shard_map/all_to_all | solution.py:597
